TPU v7x, 512 devices: a whole 4x4x16 slice. The times are simulated.
512 devices in a mesh: gx: 4 (over y_hi, core), gy: 4 (over x), gz: 32 (over y_lo, z).
Axes of the slice: x: 4, y: 4 (y_hi: 2, y_lo: 2; y = y_hi * 2 + y_lo), z: 16, core: 2. Of those that a mesh axis runs over, the one named last changes fastest.
Arguments:
- features: bfloat16 [4, 4, 32, 64, 3200], P('gx', 'gy', 'gz'), may hold values from -6 to 6
- positions: float32 [4, 4, 32, 3, 64], P('gx', 'gy', 'gz'), as said below
- neighbours: int32 [4, 4, 32, 64, 32], P('gx', 'gy', 'gz'), may hold values from 0 to 575, as said below
- counts: int32 [4, 4, 32, 64], P('gx', 'gy', 'gz'), may hold values from 8 to 32, as said below
- cell_atoms: int32 [4, 4, 32, 64], P('gx', 'gy', 'gz'), may hold values from 0 to 63, as said below
- rbf_weight: bfloat16 [512, 128], replicated, may hold values from -3 to 3
- radial_weight: bfloat16 [128, 640], replicated, may hold values from -0.5 to 0.5
- mix_weight: bfloat16 [5, 128, 128], replicated, may hold values from -0.5 to 0.5
- out_weight: bfloat16 [5, 128, 128], replicated, may hold values from -1 to 1
- energy_weight: float32 [128], replicated, may hold values from -0.5 to 0.5
- norm_weight: float32 [4, 128], replicated, may hold values from -0.5 to 0.5
Outputs:
- new_features: bfloat16 [4, 4, 32, 64, 3200], P('gx', 'gy', 'gz')
- energies: float32 [4, 4, 32, 64], P('gx', 'gy', 'gz')
- forces: float32 [4, 4, 32, 3, 64], P('gx', 'gy', 'gz')
Inputs may be any that keep to these rules, and one draw needn't show every extreme that they name: `positions`: the atom cell_atoms[q] of cell slot q = 8 c + r lies within 0.2 of the lattice site (2 cx + rx + 0.5, 2 cy + ry + 0.5, 2 cz + rz + 0.5) of its box. `neighbours`: the first 16 slots of atom i name other atoms of its domain (rows 0 to 63, never i); the rest name rows 64 + 8 e + r of extended cells e = ((ex 4 + ey) (4) + ez) that touch atom i's cell and lie outside the domain. `counts`: atom 0 of every domain has all 32 slots live. `cell_atoms`: A permutation of the domain's atoms.
All inputs are finite; a program needn't handle non-finite values.
Results may differ from a plain program's by a relative error of at most 0.012.
Values may be sent and summed in bfloat16 or wider, within the bound.
A program may use at most 64 MiB of HBM per device.

v0:
```python
from functools import partial
import math

import jax
import jax.numpy as jnp
import numpy as np
from jax import lax
from jax.sharding import PartitionSpec as P


def padded(shard, sides, width):
    for axis, dim in sides:
        peers, length = (lax.axis_size(axis), shard.shape[dim])
        up = [(i, (i + 1) % peers) for i in range(peers)]
        down = [(j, i) for i, j in up]
        last = lax.slice_in_dim(shard, length - width, length, axis=dim)
        first = lax.slice_in_dim(shard, 0, width, axis=dim)
        before = lax.ppermute(last, axis, up)
        after = lax.ppermute(first, axis, down)
        shard = jnp.concatenate([before, shard, after], axis=dim)
    return shard


def degree_of(coeff_total):
    top_degree = int(math.isqrt(coeff_total)) - 1
    return np.array(
        [degree for degree in range(top_degree + 1) for _ in range(2 * degree + 1)], dtype=np.int32
    )


def product(pattern, first_op, second_op):
    return jnp.einsum(pattern, first_op, second_op, preferred_element_type=jnp.float32)


def degree_matmul(values, weights, flipped):
    edge_rows, coefficients, channels = values.shape
    degrees = weights.shape[0]
    pieces = []
    for degree in range(degrees):
        width = 2 * degree + 1
        block = values[:, degree * degree : degree * degree + width, :].reshape(
            edge_rows * width, channels
        )
        if flipped:
            result = lax.dot_general(
                block, weights[degree], (((1,), (1,)), ((), ())), preferred_element_type=jnp.float32
            )
        else:
            result = jnp.dot(block, weights[degree], preferred_element_type=jnp.float32)
        pieces.append(result.reshape(edge_rows, width, channels))
    return jnp.concatenate(pieces, axis=1)


def image_shifts(zcells):
    depth = 2 * zcells
    side_x = [-4.0, 0.0, 0.0, 4.0]
    side_z = [-float(depth)] + [0.0] * zcells + [float(depth)]
    table = [
        [
            [
                [[side_x[ex], side_x[ey], side_z[ez]][comp] for ez in range(zcells + 2)]
                for ey in range(4)
            ]
            for ex in range(4)
        ]
        for comp in range(3)
    ]
    return jnp.asarray(table, jnp.float32)


def block_step(
    table_feat,
    table_places,
    rbf_weight,
    radial_weight,
    mix_weight,
    out_weight,
    energy_weight,
    norm_expanded,
    reach_max,
    grad_table,
    block,
):
    own_feat, own_places, neigh_rows, live_counts = block
    atom_rows, slot_count = neigh_rows.shape
    channels = energy_weight.shape[0]
    coefficients = own_feat.shape[1] // channels
    degrees = radial_weight.shape[1] // channels
    edge_rows = atom_rows * slot_count
    flat_rows = neigh_rows.reshape(edge_rows)
    near_feat = jnp.take(table_feat, flat_rows, axis=0).reshape(edge_rows, coefficients, channels)
    near_places = jnp.take(table_places, flat_rows, axis=1)
    relative = near_places - jnp.repeat(own_places, slot_count, axis=1)
    distance = jnp.sqrt(jnp.sum(relative * relative, axis=0))
    nbasis = rbf_weight.shape[0]
    spacing = reach_max / (nbasis - 1)
    centred = (
        distance[:, None] - spacing * jnp.arange(nbasis, dtype=jnp.float32)[None, :]
    ) / spacing
    basis_vals = jnp.exp(-0.5 * centred * centred)
    preact = product("eb,bh->eh", basis_vals.astype(jnp.bfloat16), rbf_weight)
    hidden = jax.nn.silu(preact).astype(jnp.bfloat16)
    radial = product("eh,hf->ef", hidden, radial_weight).reshape(edge_rows, degrees, channels)
    scaled = jnp.concatenate(
        [
            near_feat[:, degree * degree : (degree + 1) * (degree + 1), :]
            * radial[:, degree : degree + 1, :]
            for degree in range(degrees)
        ],
        axis=1,
    ).astype(jnp.bfloat16)
    mixed = degree_matmul(scaled, mix_weight, False)
    gating = jax.nn.sigmoid(mixed[:, :1, :])
    message = mixed * gating
    live_mask = (jnp.arange(slot_count, dtype=jnp.int32)[None, :] < live_counts[:, None]).astype(
        jnp.float32
    )
    norm_scale = 1.0 / math.sqrt(slot_count)
    summed = (
        jnp.sum(
            message.reshape(atom_rows, slot_count, coefficients, channels)
            * live_mask[:, :, None, None],
            axis=1,
        )
        * norm_scale
    )
    updated = own_feat.reshape(atom_rows, coefficients, channels).astype(
        jnp.float32
    ) + degree_matmul(summed.astype(jnp.bfloat16), out_weight, False)
    scalar_part = updated[:, 0, :]
    energy = jnp.sum(energy_weight[None, :] * jax.nn.silu(scalar_part), axis=1) + jnp.sum(
        norm_expanded[None] * updated * updated, axis=(1, 2)
    )
    logistic = jax.nn.sigmoid(scalar_part)
    grad_updated = jnp.concatenate(
        [
            (energy_weight[None, :] * logistic * (1.0 + scalar_part * (1.0 - logistic)))[
                :, None, :
            ],
            2.0 * norm_expanded[None, 1:, :] * updated[:, 1:, :],
        ],
        axis=1,
    )
    grad_summed = degree_matmul(grad_updated.astype(jnp.bfloat16), out_weight, True) * norm_scale
    grad_message = (grad_summed[:, None, :, :] * live_mask[:, :, None, None]).reshape(
        edge_rows, coefficients, channels
    )
    grad_first = grad_message[:, :1, :] * gating * (
        1.0 + mixed[:, :1, :] * (1.0 - gating)
    ) + jnp.sum(grad_message[:, 1:, :] * mixed[:, 1:, :], axis=1, keepdims=True) * gating * (
        1.0 - gating
    )
    grad_mixed = jnp.concatenate([grad_first, grad_message[:, 1:, :] * gating], axis=1).astype(
        jnp.bfloat16
    )
    grad_scaled = degree_matmul(grad_mixed, mix_weight, True)
    weighted = grad_scaled * near_feat
    grad_radial = jnp.stack(
        [
            jnp.sum(weighted[:, degree * degree : (degree + 1) * (degree + 1), :], axis=1)
            for degree in range(degrees)
        ],
        axis=1,
    )
    grad_hidden = product(
        "ef,hf->eh",
        grad_radial.reshape(edge_rows, degrees * channels).astype(jnp.bfloat16),
        radial_weight,
    )
    logistic_pre = jax.nn.sigmoid(preact)
    grad_preact = grad_hidden * logistic_pre * (1.0 + preact * (1.0 - logistic_pre))
    grad_basis = product("eh,bh->eb", grad_preact.astype(jnp.bfloat16), rbf_weight)
    grad_dist = jnp.sum(grad_basis * basis_vals * centred, axis=1) * (-1.0 / spacing)
    pull_vec = relative * (grad_dist / distance)[None, :]
    grad_own = -jnp.sum(pull_vec.reshape(3, atom_rows, slot_count), axis=2)
    grad_table = grad_table.at[:, flat_rows].add(pull_vec)
    return (
        grad_table,
        (
            updated.reshape(atom_rows, coefficients * channels).astype(jnp.bfloat16),
            energy,
            grad_own,
        ),
    )


def domain_layer(
    own_feat,
    own_places,
    ghost_feat,
    ghost_places,
    neigh_rows,
    live_counts,
    rbf_weight,
    radial_weight,
    mix_weight,
    out_weight,
    energy_weight,
    norm_weight,
):
    atom_rows = own_feat.shape[0]
    channels = energy_weight.shape[0]
    coefficients = own_feat.shape[1] // channels
    table_deg = degree_of(coefficients)
    upper_deg = table_deg[1:]
    divisor = jnp.asarray(2 * upper_deg + 1, jnp.float32)
    norm_expanded = jnp.concatenate(
        [jnp.zeros((1, channels), jnp.float32), norm_weight[upper_deg - 1] / divisor[:, None]],
        axis=0,
    )
    table_feat = jnp.concatenate([own_feat, ghost_feat], axis=0)
    table_places = jnp.concatenate([own_places, ghost_places], axis=1)
    blocks = atom_rows // 8
    layer_depth = atom_rows // 16
    reach_max = 2.0 * math.sqrt(32.0 + layer_depth * layer_depth)
    scanned = (
        own_feat.reshape(blocks, 8, -1),
        jnp.transpose(own_places.reshape(3, blocks, 8), (1, 0, 2)),
        neigh_rows.reshape(blocks, 8, -1),
        live_counts.reshape(blocks, 8),
    )
    advance = partial(
        block_step,
        table_feat,
        table_places,
        rbf_weight,
        radial_weight,
        mix_weight,
        out_weight,
        energy_weight,
        norm_expanded,
        reach_max,
    )
    grad_table, (updated, energy, grad_own) = lax.scan(
        advance, jnp.zeros(table_places.shape, jnp.float32), scanned
    )
    grad_own = jnp.transpose(grad_own, (1, 0, 2)).reshape(3, atom_rows) + grad_table[:, :atom_rows]
    return (
        updated.reshape(atom_rows, -1),
        energy.reshape(atom_rows),
        grad_own,
        grad_table[:, atom_rows:],
    )


def fold_axis(received, axis, count):
    middle = lax.slice_in_dim(received, 2, count + 2, axis=axis)
    lower = lax.slice_in_dim(received, 0, 1, axis=axis)
    upper = lax.slice_in_dim(received, count + 3, count + 4, axis=axis)
    widths_low = [(0, 0)] * received.ndim
    widths_high = [(0, 0)] * received.ndim
    widths_low[axis] = (0, count - 1)
    widths_high[axis] = (count - 1, 0)
    return middle + jnp.pad(lower, widths_low) + jnp.pad(upper, widths_high)


def local(
    features,
    positions,
    neighbours,
    counts,
    cell_atoms,
    rbf_weight,
    radial_weight,
    mix_weight,
    out_weight,
    energy_weight,
    norm_weight,
):
    atom_rows = features.shape[3]
    zcells = atom_rows // 32
    order = cell_atoms[0, 0, 0]
    own_feat = features[0, 0, 0]
    own_places = positions[0, 0, 0]
    cell_feat = jnp.take(own_feat, order, axis=0).reshape(2, 2, zcells, 8, -1)
    cell_places = jnp.take(own_places, order, axis=1).reshape(3, 2, 2, zcells, 8)
    ghost_feat = padded(cell_feat, (("gx", 0), ("gy", 1), ("gz", 2)), 1)
    ghost_places = padded(cell_places, (("gx", 1), ("gy", 2), ("gz", 3)), 1)
    ghost_places = (ghost_places + image_shifts(zcells)[..., None]).reshape(3, -1)
    updated, energy, grad_own, grad_ghost = domain_layer(
        own_feat,
        own_places,
        ghost_feat.reshape(-1, own_feat.shape[1]),
        ghost_places,
        neighbours[0, 0, 0],
        counts[0, 0, 0],
        rbf_weight,
        radial_weight,
        mix_weight,
        out_weight,
        energy_weight,
        norm_weight,
    )
    grad_blocks = grad_ghost.reshape(3, 4, 4, zcells + 2, 8)
    returned = padded(grad_blocks, (("gx", 1), ("gy", 2), ("gz", 3)), 1)
    cell_grad = fold_axis(fold_axis(fold_axis(returned, 1, 2), 2, 2), 3, zcells).reshape(
        3, atom_rows
    )
    onehot = (order[:, None] == jnp.arange(atom_rows, dtype=jnp.int32)[None, :]).astype(jnp.float32)
    back_own = jnp.sum(cell_grad[:, :, None] * onehot[None], axis=1)
    forces = -(grad_own + back_own)
    return (updated[None, None, None], energy[None, None, None], forces[None, None, None])


def solution(mesh):
    return jax.shard_map(
        local,
        mesh=mesh,
        in_specs=(
            P("gx", "gy", "gz", None, None),
            P("gx", "gy", "gz", None, None),
            P("gx", "gy", "gz", None, None),
            P("gx", "gy", "gz", None),
            P("gx", "gy", "gz", None),
            P(),
            P(),
            P(),
            P(),
            P(),
            P(),
        ),
        out_specs=(
            P("gx", "gy", "gz", None, None),
            P("gx", "gy", "gz", None),
            P("gx", "gy", "gz", None, None),
        ),
        check_vma=False,
    )
```

profile of v0, /device:TPU:1, one launch (start us, length us, event | category | flops | bytes accessed | tf_op | source)
XLA Modules:
  0.0 446.8 jit_solution(16261976376984354333)
XLA Ops:
  4.8 6.2 %collective-permute-start = (f32[3,1,2,2,8]{4,1,3,2,0:T(1,128)S(1)}, f32[3,1,2,2,8]{4,1,3,2,0:T(1,128)S(1)}, u32[]{:S(2)}, u32[]{:S(2)}) collective-permute-start(f32[3,1,2,2,8]{4,1,3,2,0:T(1,128)S(1)} %get-tuple-element.371), channel_id=1, source_target_pairs={{0,128},{128,256},{256,384},{384,0},{1,129},{129,257},{257,385},{3... | collective-permute-start | bytes 1160 | tf_op jit(solution)/shard_map/ppermute | solution.py:18
  11.0 4.5 %collective-permute-start.1 = (f32[3,1,2,2,8]{4,1,3,2,0:T(1,128)S(1)}, f32[3,1,2,2,8]{4,1,3,2,0:T(1,128)S(1)}, u32[]{:S(2)}, u32[]{:S(2)}) collective-permute-start(f32[3,1,2,2,8]{4,1,3,2,0:T(1,128)S(1)} %get-tuple-element.372), channel_id=1, source_target_pairs={{128,0},{256,128},{384,256},{0,384},{129,1},{257,129},{385,257},{1... | collective-permute-start | bytes 1160 | tf_op jit(solution)/shard_map/ppermute | solution.py:19
  16.2 2.3 gather_fusion.3
  18.6 5.1 %collective-permute-start.7 = (bf16[1,2,2,8,3200]{4,3,2,1,0:T(8,128)(2,1)S(1)}, bf16[1,2,2,8,3200]{4,3,2,1,0:T(8,128)(2,1)S(1)}, u32[]{:S(2)}, u32[]{:S(2)}) collective-permute-start(bf16[1,2,2,8,3200]{4,3,2,1,0:T(8,128)(2,1)S(1)} %bitcast.410), channel_id=1, source_target_pairs={{128,0},{256,128},{384,256},{0,384},{129,1},{257,129},{385,257},{1... | collective-permute-start | bytes 614408 | tf_op jit(solution)/shard_map/ppermute | solution.py:19
  23.8 1.9 collective-permute-start.6
  27.2 1.6 collective-permute-done.6
  29.0 1.9 collective-permute-start.8
  31.0 4.6 %collective-permute-start.9 = (bf16[4,1,2,8,3200]{4,3,2,1,0:T(8,128)(2,1)S(1)}, bf16[4,1,2,8,3200]{4,3,2,1,0:T(8,128)(2,1)S(1)}, u32[]{:S(2)}, u32[]{:S(2)}) collective-permute-start(bf16[4,1,2,8,3200]{4,3,2,1,0:T(8,128)(2,1)S(1)} %get-tuple-element.358), channel_id=1, source_target_pairs={{32,0},{64,32},{96,64},{0,96},{33,1},{65,33},{97,65},{1,97},{34,2}... | collective-permute-start | bytes 1228808 | tf_op jit(solution)/shard_map/ppermute | solution.py:19
  36.2 1.9 collective-permute-start.2
  38.2 4.7 %collective-permute-start.3 = (f32[3,4,1,2,8]{4,1,3,2,0:T(4,128)S(1)}, f32[3,4,1,2,8]{4,1,3,2,0:T(4,128)S(1)}, u32[]{:S(2)}, u32[]{:S(2)}) collective-permute-start(f32[3,4,1,2,8]{4,1,3,2,0:T(4,128)S(1)} %get-tuple-element.370), channel_id=1, source_target_pairs={{32,0},{64,32},{96,64},{0,96},{33,1},{65,33},{97,65},{1,97},{34,2}... | collective-permute-start | bytes 2312 | tf_op jit(solution)/shard_map/ppermute | solution.py:19
  44.5 1.9 collective-permute-start.10
  46.5 8.2 %collective-permute-start.11 = (bf16[4,4,1,8,3200]{4,3,2,1,0:T(8,128)(2,1)}, bf16[4,4,1,8,3200]{4,3,2,1,0:T(8,128)(2,1)S(1)}, u32[]{:S(2)}, u32[]{:S(2)}) collective-permute-start(bf16[4,4,1,8,3200]{4,3,2,1,0:T(8,128)(2,1)} %get-tuple-element.356), channel_id=1, source_target_pairs={{1,0},{2,1},{3,2},{4,3},{5,4},{6,5},{7,6},{8,7},{9,8},{10,9},{11,1... | collective-permute-start | bytes 2457608 | tf_op jit(solution)/shard_map/ppermute | solution.py:19
  55.4 1.9 collective-permute-start.4
  57.3 5.5 %collective-permute-start.5 = (f32[3,4,4,1,8]{4,1,3,2,0:T(4,128)}, f32[3,4,4,1,8]{4,1,3,2,0:T(4,128)S(1)}, u32[]{:S(2)}, u32[]{:S(2)}) collective-permute-start(f32[3,4,4,1,8]{4,1,3,2,0:T(4,128)} %get-tuple-element.368), channel_id=1, source_target_pairs={{1,0},{2,1},{3,2},{4,3},{5,4},{6,5},{7,6},{8,7},{9,8},{10,9},{11,1... | collective-permute-start | bytes 4616 | tf_op jit(solution)/shard_map/ppermute | solution.py:19
  63.9 4.9 %collective-permute-done.4 = f32[3,4,4,1,8]{4,1,3,2,0:T(4,128)S(1)} collective-permute-done((f32[3,4,4,1,8]{4,1,3,2,0:T(4,128)}, f32[3,4,4,1,8]{4,1,3,2,0:T(4,128)S(1)}, u32[]{:S(2)}, u32[]{:S(2)}) %collective-permute-start.4) | collective-permute-done | bytes 1568 | tf_op jit(solution)/shard_map/ppermute | solution.py:18
  72.0 2.0 pad_maximum_fusion
  74.8 335.1 %while.18 = (s32[]{:T(128)}, f32[3,576]{0,1:T(8,128)}, bf16[8,8,3200]{2,1,0:T(8,128)(2,1)}, f32[8,8]{1,0:T(8,128)}, f32[8,3,8]{2,1,0:T(4,128)}, /*index=5*/s32[8...) while((s32[]{:T(128)}, f32[3,576]{0,1:T(8,128)}, ...), condition=%wide.region_13.14_spmd, body=%wide.region_0.13_spmd.sunk | while | flops 601584384 | bytes 85508784 | solution.py:234
  77.1 1.7 gather_fusion
  82.5 5.9 %gather_fusion.1 = bf16[256,3200]{1,0:T(8,128)(2,1)S(1)} fusion(bf16[576,3200]{1,0:T(8,128)(2,1)} %get-tuple-element.552, s32[1024]{0:T(1024)S(1)} %pad_clamp_fusion.4), kind=kCustom, calls=%fused_computation.1.clone.1 | custom fusion | bytes 3277824 | tf_op jit(solution)/shard_map/while/body/eval_jaxpr/jit(_take)/gather | solution.py:91
  113.7 2.2 scatter_custom_fusion.5
  119.0 1.7 gather_fusion
  124.4 5.9 %gather_fusion.1 = bf16[256,3200]{1,0:T(8,128)(2,1)S(1)} fusion(bf16[576,3200]{1,0:T(8,128)(2,1)} %get-tuple-element.552, s32[1024]{0:T(1024)S(1)} %pad_clamp_fusion.4), kind=kCustom, calls=%fused_computation.1.clone.1 | custom fusion | bytes 3277824 | tf_op jit(solution)/shard_map/while/body/eval_jaxpr/jit(_take)/gather | solution.py:91
  155.6 2.2 scatter_custom_fusion.5
  160.9 1.7 gather_fusion
  166.3 5.9 %gather_fusion.1 = bf16[256,3200]{1,0:T(8,128)(2,1)S(1)} fusion(bf16[576,3200]{1,0:T(8,128)(2,1)} %get-tuple-element.552, s32[1024]{0:T(1024)S(1)} %pad_clamp_fusion.4), kind=kCustom, calls=%fused_computation.1.clone.1 | custom fusion | bytes 3277824 | tf_op jit(solution)/shard_map/while/body/eval_jaxpr/jit(_take)/gather | solution.py:91
  197.4 2.2 scatter_custom_fusion.5
  202.8 1.7 gather_fusion
  208.2 5.9 %gather_fusion.1 = bf16[256,3200]{1,0:T(8,128)(2,1)S(1)} fusion(bf16[576,3200]{1,0:T(8,128)(2,1)} %get-tuple-element.552, s32[1024]{0:T(1024)S(1)} %pad_clamp_fusion.4), kind=kCustom, calls=%fused_computation.1.clone.1 | custom fusion | bytes 3277824 | tf_op jit(solution)/shard_map/while/body/eval_jaxpr/jit(_take)/gather | solution.py:91
  239.3 2.2 scatter_custom_fusion.5
  244.7 1.7 gather_fusion
  250.1 5.9 %gather_fusion.1 = bf16[256,3200]{1,0:T(8,128)(2,1)S(1)} fusion(bf16[576,3200]{1,0:T(8,128)(2,1)} %get-tuple-element.552, s32[1024]{0:T(1024)S(1)} %pad_clamp_fusion.4), kind=kCustom, calls=%fused_computation.1.clone.1 | custom fusion | bytes 3277824 | tf_op jit(solution)/shard_map/while/body/eval_jaxpr/jit(_take)/gather | solution.py:91
  281.2 2.2 scatter_custom_fusion.5
  286.6 1.7 gather_fusion
  292.0 5.9 %gather_fusion.1 = bf16[256,3200]{1,0:T(8,128)(2,1)S(1)} fusion(bf16[576,3200]{1,0:T(8,128)(2,1)} %get-tuple-element.552, s32[1024]{0:T(1024)S(1)} %pad_clamp_fusion.4), kind=kCustom, calls=%fused_computation.1.clone.1 | custom fusion | bytes 3277824 | tf_op jit(solution)/shard_map/while/body/eval_jaxpr/jit(_take)/gather | solution.py:91
  323.1 2.2 scatter_custom_fusion.5
  328.5 1.7 gather_fusion
  333.9 5.9 %gather_fusion.1 = bf16[256,3200]{1,0:T(8,128)(2,1)S(1)} fusion(bf16[576,3200]{1,0:T(8,128)(2,1)} %get-tuple-element.552, s32[1024]{0:T(1024)S(1)} %pad_clamp_fusion.4), kind=kCustom, calls=%fused_computation.1.clone.1 | custom fusion | bytes 3277824 | tf_op jit(solution)/shard_map/while/body/eval_jaxpr/jit(_take)/gather | solution.py:91
  365.0 2.2 scatter_custom_fusion.5
  370.4 1.7 gather_fusion
  375.8 5.9 %gather_fusion.1 = bf16[256,3200]{1,0:T(8,128)(2,1)S(1)} fusion(bf16[576,3200]{1,0:T(8,128)(2,1)} %get-tuple-element.552, s32[1024]{0:T(1024)S(1)} %pad_clamp_fusion.4), kind=kCustom, calls=%fused_computation.1.clone.1 | custom fusion | bytes 3277824 | tf_op jit(solution)/shard_map/while/body/eval_jaxpr/jit(_take)/gather | solution.py:91
  406.9 2.2 scatter_custom_fusion.5
  411.3 7.5 %collective-permute-start.12 = (f32[3,1,4,4,8]{4,3,2,1,0:T(4,128)S(1)}, f32[3,1,4,4,8]{4,3,2,1,0:T(4,128)S(1)}, u32[]{:S(2)}, u32[]{:S(2)}) collective-permute-start(f32[3,1,4,4,8]{4,3,2,1,0:T(4,128)S(1)} %get-tuple-element.365), channel_id=1, source_target_pairs={{0,128},{128,256},{256,384},{384,0},{1,129},{129,257},{257,385},{3... | collective-permute-start | bytes 4616 | tf_op jit(solution)/shard_map/ppermute | solution.py:18
  418.9 1.9 collective-permute-start.13
  420.8 4.7 %collective-permute-done.13 = f32[3,1,4,4,8]{4,3,2,1,0:T(4,128)S(1)} collective-permute-done((f32[3,1,4,4,8]{4,3,2,1,0:T(4,128)S(1)}, f32[3,1,4,4,8]{4,3,2,1,0:T(4,128)S(1)}, u32[]{:S(2)}, u32[]{:S(2)}) %collective-permute-start.13) | collective-permute-done | bytes 1568 | tf_op jit(solution)/shard_map/ppermute | solution.py:19
  425.5 1.9 collective-permute-start.14
  427.5 4.6 %collective-permute-start.15 = (f32[3,6,1,4,8]{4,3,2,1,0:T(4,128)S(1)}, f32[3,6,1,4,8]{4,3,2,1,0:T(4,128)S(1)}, u32[]{:S(2)}, u32[]{:S(2)}) collective-permute-start(f32[3,6,1,4,8]{4,3,2,1,0:T(4,128)S(1)} %get-tuple-element.364), channel_id=1, source_target_pairs={{32,0},{64,32},{96,64},{0,96},{33,1},{65,33},{97,65},{1,97},{34,2}... | collective-permute-start | bytes 6920 | tf_op jit(solution)/shard_map/ppermute | solution.py:19
  433.2 1.9 collective-permute-start.16
  435.1 5.8 %collective-permute-start.17 = (f32[3,6,6,1,8]{4,3,2,1,0:T(1,128)S(1)}, f32[3,6,6,1,8]{4,3,2,1,0:T(1,128)S(1)}, u32[]{:S(2)}, u32[]{:S(2)}) collective-permute-start(f32[3,6,6,1,8]{4,3,2,1,0:T(1,128)S(1)} %get-tuple-element.362), channel_id=1, source_target_pairs={{1,0},{2,1},{3,2},{4,3},{5,4},{6,5},{7,6},{8,7},{9,8},{10,9},{11,1... | collective-permute-start | bytes 10376 | tf_op jit(solution)/shard_map/ppermute | solution.py:19
  (1403 shorter events, 273.6 us)
Async XLA Ops:
  0.6 34.9 %copy-start = (f32[4,128]{1,0:T(4,128)S(1)}, f32[4,128]{1,0:T(4,128)}, u32[]{:S(2)}) copy-start(f32[4,128]{1,0:T(4,128)} %param.27) | copy-start | bytes 6148
  4.8 31.4 %collective-permute-start = (f32[3,1,2,2,8]{4,1,3,2,0:T(1,128)S(1)}, f32[3,1,2,2,8]{4,1,3,2,0:T(1,128)S(1)}, u32[]{:S(2)}, u32[]{:S(2)}) collective-permute-start(f32[3,1,2,2,8]{4,1,3,2,0:T(1,128)S(1)} %get-tuple-element.371), channel_id=1, source_target_pairs={{0,128},{128,256},{256,384},{384,0},{1,129},{129,257},{257,385},{3... | collective-permute-start | bytes 1160 | tf_op jit(solution)/shard_map/ppermute | solution.py:18
  11.0 25.1 %collective-permute-start.1 = (f32[3,1,2,2,8]{4,1,3,2,0:T(1,128)S(1)}, f32[3,1,2,2,8]{4,1,3,2,0:T(1,128)S(1)}, u32[]{:S(2)}, u32[]{:S(2)}) collective-permute-start(f32[3,1,2,2,8]{4,1,3,2,0:T(1,128)S(1)} %get-tuple-element.372), channel_id=1, source_target_pairs={{128,0},{256,128},{384,256},{0,384},{129,1},{257,129},{385,257},{1... | collective-permute-start | bytes 1160 | tf_op jit(solution)/shard_map/ppermute | solution.py:19
  18.5 17.1 %copy-start.50 = (s32[24]{0:T(128)S(1)}, s32[24]{0:T(128)}, u32[]{:S(2)}) copy-start(s32[24]{0:T(128)} %constant.190) | copy-start | bytes 292
  18.6 8.6 %collective-permute-start.7 = (bf16[1,2,2,8,3200]{4,3,2,1,0:T(8,128)(2,1)S(1)}, bf16[1,2,2,8,3200]{4,3,2,1,0:T(8,128)(2,1)S(1)}, u32[]{:S(2)}, u32[]{:S(2)}) collective-permute-start(bf16[1,2,2,8,3200]{4,3,2,1,0:T(8,128)(2,1)S(1)} %bitcast.410), channel_id=1, source_target_pairs={{128,0},{256,128},{384,256},{0,384},{129,1},{257,129},{385,257},{1... | collective-permute-start | bytes 614408 | tf_op jit(solution)/shard_map/ppermute | solution.py:19
  23.8 5.1 %collective-permute-start.6 = (bf16[1,2,2,8,3200]{4,3,2,1,0:T(8,128)(2,1)S(1)}, bf16[1,2,2,8,3200]{4,3,2,1,0:T(8,128)(2,1)S(1)}, u32[]{:S(2)}, u32[]{:S(2)}) collective-permute-start(bf16[1,2,2,8,3200]{4,3,2,1,0:T(8,128)(2,1)S(1)} %bitcast.409), channel_id=1, source_target_pairs={{0,128},{128,256},{256,384},{384,0},{1,129},{129,257},{257,385},{3... | collective-permute-start | bytes 614408 | tf_op jit(solution)/shard_map/ppermute | solution.py:18
  29.0 13.9 %collective-permute-start.8 = (bf16[4,1,2,8,3200]{4,3,2,1,0:T(8,128)(2,1)S(1)}, bf16[4,1,2,8,3200]{4,3,2,1,0:T(8,128)(2,1)S(1)}, u32[]{:S(2)}, u32[]{:S(2)}) collective-permute-start(bf16[4,1,2,8,3200]{4,3,2,1,0:T(8,128)(2,1)S(1)} %get-tuple-element.357), channel_id=1, source_target_pairs={{0,32},{32,64},{64,96},{96,0},{1,33},{33,65},{65,97},{97,1},{2,34}... | collective-permute-start | bytes 1228808 | tf_op jit(solution)/shard_map/ppermute | solution.py:18
  31.0 12.0 %collective-permute-start.9 = (bf16[4,1,2,8,3200]{4,3,2,1,0:T(8,128)(2,1)S(1)}, bf16[4,1,2,8,3200]{4,3,2,1,0:T(8,128)(2,1)S(1)}, u32[]{:S(2)}, u32[]{:S(2)}) collective-permute-start(bf16[4,1,2,8,3200]{4,3,2,1,0:T(8,128)(2,1)S(1)} %get-tuple-element.358), channel_id=1, source_target_pairs={{32,0},{64,32},{96,64},{0,96},{33,1},{65,33},{97,65},{1,97},{34,2}... | collective-permute-start | bytes 1228808 | tf_op jit(solution)/shard_map/ppermute | solution.py:19
  36.2 18.5 %collective-permute-start.2 = (f32[3,4,1,2,8]{4,1,3,2,0:T(4,128)S(1)}, f32[3,4,1,2,8]{4,1,3,2,0:T(4,128)S(1)}, u32[]{:S(2)}, u32[]{:S(2)}) collective-permute-start(f32[3,4,1,2,8]{4,1,3,2,0:T(4,128)S(1)} %get-tuple-element.369), channel_id=1, source_target_pairs={{0,32},{32,64},{64,96},{96,0},{1,33},{33,65},{65,97},{97,1},{2,34}... | collective-permute-start | bytes 2312 | tf_op jit(solution)/shard_map/ppermute | solution.py:18
  38.1 24.6 %copy-start.49 = (f32[24]{0:T(128)S(1)}, f32[24]{0:T(128)}, u32[]{:S(2)}) copy-start(f32[24]{0:T(128)} %constant.188) | copy-start | bytes 292
  38.1 24.8 %copy-start.51 = (s32[1,1,1,64]{3,2,1,0:T(1,128)S(1)}, s32[1,1,1,64]{3,2,1,0:T(1,128)}, u32[]{:S(2)}) copy-start(s32[1,1,1,64]{3,2,1,0:T(1,128)} %param.20) | copy-start | bytes 772
  38.2 25.4 %copy-start.45 = (f32[1,1,1,3,64]{4,2,3,1,0:T(1,128)S(1)}, f32[1,1,1,3,64]{4,2,3,1,0:T(1,128)}, u32[]{:S(2)}) copy-start(f32[1,1,1,3,64]{4,2,3,1,0:T(1,128)} %param.18) | copy-start | bytes 2308
  38.2 25.6 %copy-start.43 = (s32[1,1,1,64,32]{3,4,2,1,0:T(8,128)S(1)}, s32[1,1,1,64,32]{3,4,2,1,0:T(8,128)}, u32[]{:S(2)}) copy-start(s32[1,1,1,64,32]{3,4,2,1,0:T(8,128)} %param.19) | copy-start | bytes 24580
  38.2 31.6 %copy-start.42 = (f32[3,4,4,4]{3,2,1,0:T(4,128)S(1)}, f32[3,4,4,4]{3,2,1,0:T(4,128)}, u32[]{:S(2)}) copy-start(f32[3,4,4,4]{3,2,1,0:T(4,128)} %constant.171.clone) | copy-start | bytes 2308
  38.2 16.5 %collective-permute-start.3 = (f32[3,4,1,2,8]{4,1,3,2,0:T(4,128)S(1)}, f32[3,4,1,2,8]{4,1,3,2,0:T(4,128)S(1)}, u32[]{:S(2)}, u32[]{:S(2)}) collective-permute-start(f32[3,4,1,2,8]{4,1,3,2,0:T(4,128)S(1)} %get-tuple-element.370), channel_id=1, source_target_pairs={{32,0},{64,32},{96,64},{0,96},{33,1},{65,33},{97,65},{1,97},{34,2}... | collective-permute-start | bytes 2312 | tf_op jit(solution)/shard_map/ppermute | solution.py:19
  44.5 26.4 %collective-permute-start.10 = (bf16[4,4,1,8,3200]{4,3,2,1,0:T(8,128)(2,1)}, bf16[4,4,1,8,3200]{4,3,2,1,0:T(8,128)(2,1)S(1)}, u32[]{:S(2)}, u32[]{:S(2)}) collective-permute-start(bf16[4,4,1,8,3200]{4,3,2,1,0:T(8,128)(2,1)} %get-tuple-element.355), channel_id=1, source_target_pairs={{0,1},{1,2},{2,3},{3,4},{4,5},{5,6},{6,7},{7,8},{8,9},{9,10},{10,1... | collective-permute-start | bytes 2457608 | tf_op jit(solution)/shard_map/ppermute | solution.py:18
  46.5 24.5 %collective-permute-start.11 = (bf16[4,4,1,8,3200]{4,3,2,1,0:T(8,128)(2,1)}, bf16[4,4,1,8,3200]{4,3,2,1,0:T(8,128)(2,1)S(1)}, u32[]{:S(2)}, u32[]{:S(2)}) collective-permute-start(bf16[4,4,1,8,3200]{4,3,2,1,0:T(8,128)(2,1)} %get-tuple-element.356), channel_id=1, source_target_pairs={{1,0},{2,1},{3,2},{4,3},{5,4},{6,5},{7,6},{8,7},{9,8},{10,9},{11,1... | collective-permute-start | bytes 2457608 | tf_op jit(solution)/shard_map/ppermute | solution.py:19
  55.4 13.5 %collective-permute-start.4 = (f32[3,4,4,1,8]{4,1,3,2,0:T(4,128)}, f32[3,4,4,1,8]{4,1,3,2,0:T(4,128)S(1)}, u32[]{:S(2)}, u32[]{:S(2)}) collective-permute-start(f32[3,4,4,1,8]{4,1,3,2,0:T(4,128)} %get-tuple-element.367), channel_id=1, source_target_pairs={{0,1},{1,2},{2,3},{3,4},{4,5},{5,6},{6,7},{7,8},{8,9},{9,10},{10,1... | collective-permute-start | bytes 4616 | tf_op jit(solution)/shard_map/ppermute | solution.py:18
  57.3 12.4 %collective-permute-start.5 = (f32[3,4,4,1,8]{4,1,3,2,0:T(4,128)}, f32[3,4,4,1,8]{4,1,3,2,0:T(4,128)S(1)}, u32[]{:S(2)}, u32[]{:S(2)}) collective-permute-start(f32[3,4,4,1,8]{4,1,3,2,0:T(4,128)} %get-tuple-element.368), channel_id=1, source_target_pairs={{1,0},{2,1},{3,2},{4,3},{5,4},{6,5},{7,6},{8,7},{9,8},{10,9},{11,1... | collective-permute-start | bytes 4616 | tf_op jit(solution)/shard_map/ppermute | solution.py:19
  93.9 12.9 %copy-start.32 = (f32[256]{0:T(256)S(1)}, f32[256]{0:T(256)}, u32[]{:S(2)}) copy-start(f32[256]{0:T(256)} %reshape.653) | copy-start | bytes 3076 | tf_op jit(solution)/shard_map/while
  99.7 7.6 %copy-start.4 = (f32[256,3,128]{2,0,1:T(8,128)S(1)}, f32[256,3,128]{2,0,1:T(8,128)}, u32[]{:S(2)}) copy-start(f32[256,3,128]{2,0,1:T(8,128)} %copy-done.3) | copy-start | bytes 1179652 | tf_op jit(solution)/shard_map/while
  99.7 7.6 %copy-start.12 = (f32[256,128]{1,0:T(8,128)S(1)}, f32[256,128]{1,0:T(8,128)}, u32[]{:S(2)}) copy-start(f32[256,128]{1,0:T(8,128)} %copy-done.11) | copy-start | bytes 393220 | tf_op jit(solution)/shard_map/while
  135.8 12.9 %copy-start.32 = (f32[256]{0:T(256)S(1)}, f32[256]{0:T(256)}, u32[]{:S(2)}) copy-start(f32[256]{0:T(256)} %reshape.653) | copy-start | bytes 3076 | tf_op jit(solution)/shard_map/while
  141.6 7.6 %copy-start.4 = (f32[256,3,128]{2,0,1:T(8,128)S(1)}, f32[256,3,128]{2,0,1:T(8,128)}, u32[]{:S(2)}) copy-start(f32[256,3,128]{2,0,1:T(8,128)} %copy-done.3) | copy-start | bytes 1179652 | tf_op jit(solution)/shard_map/while
  141.6 7.6 %copy-start.12 = (f32[256,128]{1,0:T(8,128)S(1)}, f32[256,128]{1,0:T(8,128)}, u32[]{:S(2)}) copy-start(f32[256,128]{1,0:T(8,128)} %copy-done.11) | copy-start | bytes 393220 | tf_op jit(solution)/shard_map/while
  177.7 12.9 %copy-start.32 = (f32[256]{0:T(256)S(1)}, f32[256]{0:T(256)}, u32[]{:S(2)}) copy-start(f32[256]{0:T(256)} %reshape.653) | copy-start | bytes 3076 | tf_op jit(solution)/shard_map/while
  183.5 7.6 %copy-start.4 = (f32[256,3,128]{2,0,1:T(8,128)S(1)}, f32[256,3,128]{2,0,1:T(8,128)}, u32[]{:S(2)}) copy-start(f32[256,3,128]{2,0,1:T(8,128)} %copy-done.3) | copy-start | bytes 1179652 | tf_op jit(solution)/shard_map/while
  183.5 7.6 %copy-start.12 = (f32[256,128]{1,0:T(8,128)S(1)}, f32[256,128]{1,0:T(8,128)}, u32[]{:S(2)}) copy-start(f32[256,128]{1,0:T(8,128)} %copy-done.11) | copy-start | bytes 393220 | tf_op jit(solution)/shard_map/while
  219.6 12.9 %copy-start.32 = (f32[256]{0:T(256)S(1)}, f32[256]{0:T(256)}, u32[]{:S(2)}) copy-start(f32[256]{0:T(256)} %reshape.653) | copy-start | bytes 3076 | tf_op jit(solution)/shard_map/while
  225.3 7.6 %copy-start.4 = (f32[256,3,128]{2,0,1:T(8,128)S(1)}, f32[256,3,128]{2,0,1:T(8,128)}, u32[]{:S(2)}) copy-start(f32[256,3,128]{2,0,1:T(8,128)} %copy-done.3) | copy-start | bytes 1179652 | tf_op jit(solution)/shard_map/while
  225.4 7.6 %copy-start.12 = (f32[256,128]{1,0:T(8,128)S(1)}, f32[256,128]{1,0:T(8,128)}, u32[]{:S(2)}) copy-start(f32[256,128]{1,0:T(8,128)} %copy-done.11) | copy-start | bytes 393220 | tf_op jit(solution)/shard_map/while
  261.5 12.9 %copy-start.32 = (f32[256]{0:T(256)S(1)}, f32[256]{0:T(256)}, u32[]{:S(2)}) copy-start(f32[256]{0:T(256)} %reshape.653) | copy-start | bytes 3076 | tf_op jit(solution)/shard_map/while
  267.3 7.6 %copy-start.4 = (f32[256,3,128]{2,0,1:T(8,128)S(1)}, f32[256,3,128]{2,0,1:T(8,128)}, u32[]{:S(2)}) copy-start(f32[256,3,128]{2,0,1:T(8,128)} %copy-done.3) | copy-start | bytes 1179652 | tf_op jit(solution)/shard_map/while
  267.3 7.6 %copy-start.12 = (f32[256,128]{1,0:T(8,128)S(1)}, f32[256,128]{1,0:T(8,128)}, u32[]{:S(2)}) copy-start(f32[256,128]{1,0:T(8,128)} %copy-done.11) | copy-start | bytes 393220 | tf_op jit(solution)/shard_map/while
  303.4 12.9 %copy-start.32 = (f32[256]{0:T(256)S(1)}, f32[256]{0:T(256)}, u32[]{:S(2)}) copy-start(f32[256]{0:T(256)} %reshape.653) | copy-start | bytes 3076 | tf_op jit(solution)/shard_map/while
  309.2 7.6 %copy-start.4 = (f32[256,3,128]{2,0,1:T(8,128)S(1)}, f32[256,3,128]{2,0,1:T(8,128)}, u32[]{:S(2)}) copy-start(f32[256,3,128]{2,0,1:T(8,128)} %copy-done.3) | copy-start | bytes 1179652 | tf_op jit(solution)/shard_map/while
  309.2 7.6 %copy-start.12 = (f32[256,128]{1,0:T(8,128)S(1)}, f32[256,128]{1,0:T(8,128)}, u32[]{:S(2)}) copy-start(f32[256,128]{1,0:T(8,128)} %copy-done.11) | copy-start | bytes 393220 | tf_op jit(solution)/shard_map/while
  345.3 12.9 %copy-start.32 = (f32[256]{0:T(256)S(1)}, f32[256]{0:T(256)}, u32[]{:S(2)}) copy-start(f32[256]{0:T(256)} %reshape.653) | copy-start | bytes 3076 | tf_op jit(solution)/shard_map/while
  351.0 7.6 %copy-start.12 = (f32[256,128]{1,0:T(8,128)S(1)}, f32[256,128]{1,0:T(8,128)}, u32[]{:S(2)}) copy-start(f32[256,128]{1,0:T(8,128)} %copy-done.11) | copy-start | bytes 393220 | tf_op jit(solution)/shard_map/while
  387.2 12.9 %copy-start.32 = (f32[256]{0:T(256)S(1)}, f32[256]{0:T(256)}, u32[]{:S(2)}) copy-start(f32[256]{0:T(256)} %reshape.653) | copy-start | bytes 3076 | tf_op jit(solution)/shard_map/while
  392.9 7.6 %copy-start.12 = (f32[256,128]{1,0:T(8,128)S(1)}, f32[256,128]{1,0:T(8,128)}, u32[]{:S(2)}) copy-start(f32[256,128]{1,0:T(8,128)} %copy-done.11) | copy-start | bytes 393220 | tf_op jit(solution)/shard_map/while
  409.9 36.0 %copy-start.46 = (pred[2]{0:T(512)(128)(4,1)S(1)}, pred[2]{0:T(512)(128)(4,1)}, u32[]{:S(2)}) copy-start(pred[2]{0:T(512)(128)(4,1)} %constant.170.clone.1) | copy-start | bytes 10
  411.3 9.5 %collective-permute-start.12 = (f32[3,1,4,4,8]{4,3,2,1,0:T(4,128)S(1)}, f32[3,1,4,4,8]{4,3,2,1,0:T(4,128)S(1)}, u32[]{:S(2)}, u32[]{:S(2)}) collective-permute-start(f32[3,1,4,4,8]{4,3,2,1,0:T(4,128)S(1)} %get-tuple-element.365), channel_id=1, source_target_pairs={{0,128},{128,256},{256,384},{384,0},{1,129},{129,257},{257,385},{3... | collective-permute-start | bytes 4616 | tf_op jit(solution)/shard_map/ppermute | solution.py:18
  418.9 6.7 %collective-permute-start.13 = (f32[3,1,4,4,8]{4,3,2,1,0:T(4,128)S(1)}, f32[3,1,4,4,8]{4,3,2,1,0:T(4,128)S(1)}, u32[]{:S(2)}, u32[]{:S(2)}) collective-permute-start(f32[3,1,4,4,8]{4,3,2,1,0:T(4,128)S(1)} %get-tuple-element.366), channel_id=1, source_target_pairs={{128,0},{256,128},{384,256},{0,384},{129,1},{257,129},{385,257},{1... | collective-permute-start | bytes 4616 | tf_op jit(solution)/shard_map/ppermute | solution.py:19
  425.5 6.5 %collective-permute-start.14 = (f32[3,6,1,4,8]{4,3,2,1,0:T(4,128)S(1)}, f32[3,6,1,4,8]{4,3,2,1,0:T(4,128)S(1)}, u32[]{:S(2)}, u32[]{:S(2)}) collective-permute-start(f32[3,6,1,4,8]{4,3,2,1,0:T(4,128)S(1)} %get-tuple-element.363), channel_id=1, source_target_pairs={{0,32},{32,64},{64,96},{96,0},{1,33},{33,65},{65,97},{97,1},{2,34}... | collective-permute-start | bytes 6920 | tf_op jit(solution)/shard_map/ppermute | solution.py:18
  427.5 5.6 %collective-permute-start.15 = (f32[3,6,1,4,8]{4,3,2,1,0:T(4,128)S(1)}, f32[3,6,1,4,8]{4,3,2,1,0:T(4,128)S(1)}, u32[]{:S(2)}, u32[]{:S(2)}) collective-permute-start(f32[3,6,1,4,8]{4,3,2,1,0:T(4,128)S(1)} %get-tuple-element.364), channel_id=1, source_target_pairs={{32,0},{64,32},{96,64},{0,96},{33,1},{65,33},{97,65},{1,97},{34,2}... | collective-permute-start | bytes 6920 | tf_op jit(solution)/shard_map/ppermute | solution.py:19
  433.2 11.7 %collective-permute-start.16 = (f32[3,6,6,1,8]{4,3,2,1,0:T(1,128)S(1)}, f32[3,6,6,1,8]{4,3,2,1,0:T(1,128)S(1)}, u32[]{:S(2)}, u32[]{:S(2)}) collective-permute-start(f32[3,6,6,1,8]{4,3,2,1,0:T(1,128)S(1)} %get-tuple-element.361), channel_id=1, source_target_pairs={{0,1},{1,2},{2,3},{3,4},{4,5},{5,6},{6,7},{7,8},{8,9},{9,10},{10,1... | collective-permute-start | bytes 10376 | tf_op jit(solution)/shard_map/ppermute | solution.py:18
  435.1 9.8 %collective-permute-start.17 = (f32[3,6,6,1,8]{4,3,2,1,0:T(1,128)S(1)}, f32[3,6,6,1,8]{4,3,2,1,0:T(1,128)S(1)}, u32[]{:S(2)}, u32[]{:S(2)}) collective-permute-start(f32[3,6,6,1,8]{4,3,2,1,0:T(1,128)S(1)} %get-tuple-element.362), channel_id=1, source_target_pairs={{1,0},{2,1},{3,2},{4,3},{5,4},{6,5},{7,6},{8,7},{9,8},{10,9},{11,1... | collective-permute-start | bytes 10376 | tf_op jit(solution)/shard_map/ppermute | solution.py:19
  (323 other events, 1133.4 us)
where the time goes:
time: 454 us; the launch traced here: 447 us
  local copies, waits for them, and re-layouts  144 us (32%)
  other arithmetic  106 us (23%)
  matrix products  102 us (22%)
  starting transfers between devices  72.1 us (16%)
  waiting for transfers between devices  14.6 us (3%)
  loops' own time  6.45 us (1%)
    gather x16, local copies, waits for them, and re-layouts, block_step(): jnp.take(table_feat, flat_rows, axis=0)  59.2 us
    dot_general x80, matrix products, degree_matmul(): lax.dot_general(block, weights[degree], (((1,), (1,)), ((), ())), preferr...  46.2 us
    ppermute x9, starting transfers between devices, padded(): after = lax.ppermute(first, axis, down)  44.9 us
    dot_general x24, matrix products, product(): jnp.einsum(pattern, first_op, second_op, preferred_element_type=jnp.float32)  32.4 us
    ppermute x9, starting transfers between devices, padded(): before = lax.ppermute(last, axis, up)  27.1 us
    while x752, local copies, waits for them, and re-layouts  24.9 us
    dot_general x80, matrix products, degree_matmul(): result = jnp.dot(block, weights[degree], preferred_element_type=jnp.float32)  23.8 us
    scatter-add x8, other arithmetic, block_step(): grad_table = grad_table.at[:, flat_rows].add(pull_vec)  17.6 us
  transfers between devices with their start and end apart: 18, of which 6 were waited for; matrix products, arithmetic and copies ran while one was open for 3% of the time, Pallas kernels for 0%

commit v1 on v0

v1 whole, which is shorter than its diff:
```python
from functools import partial
import math

import jax
import jax.numpy as jnp
import numpy as np
from jax import lax
from jax.experimental import pallas as pl
from jax.experimental.pallas import tpu as pltpu
from jax.sharding import PartitionSpec as P

F32, BF16 = jnp.float32, jnp.bfloat16
ATOMS, SLOTS, HALF, C, FEAT, RBF, DEGREES = 64, 32, 16, 128, 3200, 512, 5
GHOST = 512
COEFFS = FEAT // C
DEGREE = [degree for degree in range(DEGREES) for _ in range(2 * degree + 1)]
PAIRS = [tuple(range(k, min(k + 2, COEFFS))) for k in range(0, COEFFS, 2)]
BLOCKS = sorted({(DEGREE[a], DEGREE[b]) for a, b in PAIRS[:-1]})
NORM = 1.0 / math.sqrt(SLOTS)
SPACING = 2.0 * math.sqrt(48.0) / (RBF - 1)
OWN_ROWS = 256
OWN_CHUNKS = ATOMS * HALF // OWN_ROWS
GHOST_ROWS = 128
GHOST_EDGES = ATOMS * HALF
VMEM_LIMIT = 50 * 1024 * 1024


def dot(a, b):
    return lax.dot_general(a, b, (((1,), (0,)), ((), ())), preferred_element_type=F32)


def dot_nt(a, b):
    return lax.dot_general(a, b, (((1,), (1,)), ((), ())), preferred_element_type=F32)


def iota(shape, dim):
    return lax.broadcasted_iota(jnp.int32, shape, dim)


def onehot_of(hit):
    return jnp.where(hit, 1.0, 0.0).astype(BF16)


def split3(value):
    high = value.astype(BF16)
    rest = value - high.astype(F32)
    middle = rest.astype(BF16)
    return high, middle, (rest - middle.astype(F32)).astype(BF16)


def gather_places(onehot, parts, flipped):
    total = None
    for part in parts[::-1]:
        value = dot_nt(part, onehot) if flipped else dot_nt(onehot, part)
        total = value if total is None else total + value
    return total


def fill_blocks(block_ref, weight_ref):
    block_ref[...] = jnp.zeros(block_ref.shape, BF16)
    for at, (first, second) in enumerate(BLOCKS):
        block_ref[at, :C, :C] = weight_ref[first]
        block_ref[at, C:, C:] = weight_ref[second]


def pair_weight(pair, block_ref, weight_ref):
    if len(pair) == 1:
        return weight_ref[DEGREE[pair[0]]]
    return block_ref[BLOCKS.index((DEGREE[pair[0]], DEGREE[pair[1]]))]


def wide(value, pair):
    return value if len(pair) == 1 else jnp.concatenate([value, value], axis=1)


def radial_of(rel, rbf_ref, radial_ref, rad_ref, drad_ref):
    distance = jnp.sqrt(jnp.sum(rel * rel, axis=1, keepdims=True))
    rows = rel.shape[0]
    centred = distance * (1.0 / SPACING) - iota((rows, RBF), 1).astype(F32)
    basis = jnp.exp(-0.5 * centred * centred)
    preact = dot(basis.astype(BF16), rbf_ref[...])
    slope = dot((basis * centred).astype(BF16), rbf_ref[...]) * (-1.0 / SPACING)
    logistic = jax.nn.sigmoid(preact)
    hidden = (preact * logistic).astype(BF16)
    dhidden = (slope * logistic * (1.0 + preact * (1.0 - logistic))).astype(BF16)
    rad_ref[...] = dot(hidden, radial_ref[...]).astype(BF16)
    drad_ref[...] = dot(dhidden, radial_ref[...]).astype(BF16)


def edge_forward(onehot, table_ref, rad_ref, drad_ref, block_ref, mix_ref, put_message, put_slope):
    rows = onehot.shape[0]
    gate = lean = None
    for pair in PAIRS:
        lanes = slice(pair[0] * C, (pair[-1] + 1) * C)
        near = dot(onehot, table_ref[:, lanes]).astype(BF16)
        cuts = [slice(DEGREE[k] * C, (DEGREE[k] + 1) * C) for k in pair]
        rad = jnp.concatenate([rad_ref[:, cut] for cut in cuts], axis=1)
        drad = jnp.concatenate([drad_ref[:, cut] for cut in cuts], axis=1)
        both = jnp.concatenate([near * rad, near * drad], axis=0)
        both = dot(both, pair_weight(pair, block_ref, mix_ref))
        mixed, dmixed = both[:rows], both[rows:]
        if gate is None:
            gate = jax.nn.sigmoid(mixed[:, :C])
            lean = (1.0 - gate) * dmixed[:, :C]
        put_message(lanes, (mixed * wide(gate, pair)).astype(BF16))
        put_slope(lanes, ((dmixed + mixed * wide(lean, pair)) * wide(gate, pair)).astype(BF16))


def select_lane(table, lane, value):
    return jnp.sum(jnp.where(iota(table.shape, 1) == lane, table, 0.0), axis=1, keepdims=True)


def neighbour_parts(neigh_ref):
    rows = neigh_ref[...]
    return (rows >> 3).astype(F32).astype(BF16), (rows & 7).astype(F32).astype(BF16)


def own_body(
    feat_ref, pos_ref, neigh_ref, counts_ref, rbf_ref, radial_ref, mix_ref,
    acc_ref, relt_ref, pair_ref, slope_hbm,
    block_ref, pos8_ref, cells_ref, within_ref, rad_ref, drad_ref, slope_ref, sem,
):
    fill_blocks(block_ref, mix_ref)
    pos8_ref[...] = jnp.zeros(pos8_ref.shape, F32)
    pos8_ref[0:3, :] = pos_ref[...]
    parts = split3(pos8_ref[...])
    cells, within = neighbour_parts(neigh_ref)
    cells_ref[...] = cells
    within_ref[...] = within
    atoms = OWN_ROWS // HALF
    edge = iota((OWN_ROWS, 1), 0)
    spread = onehot_of(edge // HALF == iota((OWN_ROWS, atoms), 1))
    gather = onehot_of(iota((atoms, OWN_ROWS), 1) // HALF == iota((atoms, OWN_ROWS), 0))

    def copy_out(chunk):
        return pltpu.make_async_copy(
            slope_ref.at[pl.ds(chunk * OWN_ROWS, OWN_ROWS), :],
            slope_hbm.at[pl.ds(chunk * OWN_ROWS, OWN_ROWS), :],
            sem.at[chunk],
        )

    @pl.loop(0, OWN_CHUNKS)
    def _(chunk):
        here = pl.ds(pl.multiple_of(chunk * atoms, atoms), atoms)
        rows = pl.ds(pl.multiple_of(chunk * OWN_ROWS, OWN_ROWS), OWN_ROWS)
        named = dot(spread, cells_ref[here, :]) * 8.0 + dot(spread, within_ref[here, :])
        named = select_lane(named, edge % HALF, 0.0)
        centre = chunk * atoms + edge // HALF
        lane = iota((OWN_ROWS, ATOMS), 1)
        live_count = jnp.sum(jnp.where(lane == centre, counts_ref[...].astype(F32), 0.0), axis=1, keepdims=True)
        hit = lane.astype(F32) == named
        edge_pair = jnp.where(hit, 1.0, jnp.where(lane == centre, -1.0, 0.0)).astype(BF16)
        pair_ref[rows, :] = edge_pair
        relt_ref[:, rows] = gather_places(edge_pair, parts, True)
        radial_of(gather_places(edge_pair, parts, False), rbf_ref, radial_ref, rad_ref, drad_ref)
        onehot = onehot_of(jnp.logical_and(hit, (edge % HALF).astype(F32) < live_count))

        def put_message(lanes, value):
            acc_ref[here, lanes] = dot(gather, value)

        def put_slope(lanes, value):
            slope_ref[rows, lanes] = value

        edge_forward(onehot, feat_ref, rad_ref, drad_ref, block_ref, mix_ref, put_message, put_slope)
        copy_out(chunk).start()

    for chunk in range(OWN_CHUNKS):
        copy_out(chunk).wait()


def own_edges(feat, pos, neigh, counts, rbf, radial, mix):
    vmem = pl.BlockSpec(memory_space=pltpu.VMEM)
    edges = ATOMS * HALF
    return pl.pallas_call(
        own_body,
        out_shape=(
            jax.ShapeDtypeStruct((ATOMS, FEAT), F32),
            jax.ShapeDtypeStruct((8, edges), F32),
            jax.ShapeDtypeStruct((edges, ATOMS), BF16),
            jax.ShapeDtypeStruct((edges, FEAT), BF16),
        ),
        in_specs=[vmem] * 7,
        out_specs=(vmem, vmem, vmem, pl.BlockSpec(memory_space=pl.ANY)),
        scratch_shapes=[
            pltpu.VMEM((len(BLOCKS), 2 * C, 2 * C), BF16),
            pltpu.VMEM((8, ATOMS), F32),
            pltpu.VMEM((ATOMS, SLOTS), BF16),
            pltpu.VMEM((ATOMS, SLOTS), BF16),
            pltpu.VMEM((OWN_ROWS, DEGREES * C), BF16),
            pltpu.VMEM((OWN_ROWS, DEGREES * C), BF16),
            pltpu.VMEM((edges, FEAT), BF16),
            pltpu.SemaphoreType.DMA((OWN_CHUNKS,)),
        ],
        compiler_params=pltpu.CompilerParams(vmem_limit_bytes=VMEM_LIMIT),
        cost_estimate=pl.CostEstimate(flops=8_000_000_000, bytes_accessed=10_000_000, transcendentals=600_000),
        name="own_edges",
    )(feat, pos, neigh, counts, rbf, radial, mix)


def ghost_body(
    feat_ref, pos_ref, gpos_ref, neigh_ref, counts_ref, rbf_ref, radial_ref, mix_ref, out_ref,
    energy_ref, norm_ref, acc_own_ref, relt_ref, pair_ref, slope_hbm, table_hbm,
    new_ref, energies_ref, grad_own_ref, grad_ghost_ref,
    block_ref, oblock_ref, pos8_ref, gpos8_ref, cells_ref, within_ref, rad_ref, drad_ref,
    slope_ref, gslope_ref, table_ref, acc_ref, grelt_ref, gslot_ref, gatom_ref, updated_ref, gsum_ref, sem,
):
    load_table = pltpu.make_async_copy(table_hbm, table_ref, sem.at[0])
    load_slope = pltpu.make_async_copy(slope_hbm, slope_ref, sem.at[1])
    load_table.start()
    load_slope.start()
    fill_blocks(block_ref, mix_ref)
    fill_blocks(oblock_ref, out_ref)
    for target, source in ((pos8_ref, pos_ref), (gpos8_ref, gpos_ref)):
        target[...] = jnp.zeros(target.shape, F32)
        target[0:3, :] = source[...]
    parts, gparts = split3(pos8_ref[...]), split3(gpos8_ref[...])
    cells, within = neighbour_parts(neigh_ref)
    cells_ref[...] = cells
    within_ref[...] = within
    live_row = jnp.maximum(counts_ref[...].astype(F32) - float(HALF), 0.0)
    square = (ATOMS, ATOMS)
    row_id, col_id = iota(square, 0), iota(square, 1)
    live_col = jnp.sum(jnp.where(row_id == col_id, live_row, 0.0), axis=1, keepdims=True)
    start_col = jnp.sum(jnp.where(col_id < row_id, live_row, 0.0), axis=1, keepdims=True)
    start_row = jnp.sum(jnp.where(row_id < col_id, live_col, 0.0), axis=0, keepdims=True)
    total = jnp.sum(live_row).astype(jnp.int32)
    chunks = (total + GHOST_ROWS - 1) // GHOST_ROWS
    acc_ref[...] = acc_own_ref[...]
    load_table.wait()

    def spread_of(chunk):
        place = (iota((ATOMS, GHOST_ROWS), 1) + chunk * GHOST_ROWS).astype(F32)
        return jnp.logical_and(place >= start_col, place < start_col + live_col)

    @pl.loop(0, chunks)
    def _(chunk):
        rows = pl.ds(pl.multiple_of(chunk * GHOST_ROWS, GHOST_ROWS), GHOST_ROWS)
        place = (iota((GHOST_ROWS, 1), 0) + chunk * GHOST_ROWS).astype(F32)
        inside = jnp.logical_and(place >= start_row, place < start_row + live_row)
        begin = jnp.sum(jnp.where(inside, start_row, 0.0), axis=1, keepdims=True)
        spread = onehot_of(inside)
        gather = onehot_of(spread_of(chunk))
        named = dot(spread, cells_ref[...]) * 8.0 + dot(spread, within_ref[...])
        named = select_lane(named, (place - begin).astype(jnp.int32) + HALF, 0.0)
        onehot = onehot_of(iota((GHOST_ROWS, GHOST), 1).astype(F32) == named - float(ATOMS))
        gslot_ref[rows, :] = onehot
        gatom_ref[rows, :] = spread
        grelt_ref[:, rows] = gather_places(onehot, gparts, True) - gather_places(spread, parts, True)
        rel = gather_places(onehot, gparts, False) - gather_places(spread, parts, False)
        radial_of(rel, rbf_ref, radial_ref, rad_ref, drad_ref)

        def put_message(lanes, value):
            acc_ref[:, lanes] += dot(gather, value)

        def put_slope(lanes, value):
            gslope_ref[rows, lanes] = value

        edge_forward(onehot, table_ref, rad_ref, drad_ref, block_ref, mix_ref, put_message, put_slope)

    energy = None
    for pair in PAIRS:
        lanes = slice(pair[0] * C, (pair[-1] + 1) * C)
        low = (acc_ref[:, lanes] * NORM).astype(BF16)
        weight = pair_weight(pair, oblock_ref, out_ref)
        updated = feat_ref[:, lanes].astype(F32) + dot(low, weight)
        new_ref[:, lanes] = updated.astype(BF16)
        grads = []
        for at, k in enumerate(pair):
            value = updated[:, at * C : (at + 1) * C]
            if k == 0:
                logistic = jax.nn.sigmoid(value)
                scale = energy_ref[...]
                term = scale * value * logistic
                grads.append(scale * logistic * (1.0 + value * (1.0 - logistic)))
            else:
                degree = DEGREE[k]
                scaled = norm_ref[degree - 1 : degree, :] * (1.0 / (2 * degree + 1)) * value
                term = scaled * value
                grads.append(2.0 * scaled)
            energy = term if energy is None else energy + term
        grad = jnp.concatenate(grads, axis=1).astype(BF16)
        gsum_ref[:, lanes] = (dot_nt(grad, weight) * NORM).astype(BF16)
    energy = jnp.sum(energy, axis=1, keepdims=True)
    energies_ref[...] = jnp.sum(jnp.where(row_id == col_id, energy, 0.0), axis=0, keepdims=True)

    def pull_of(relt, slope_grad):
        square = jnp.sum(relt * relt, axis=0, keepdims=True)
        pull = relt * (slope_grad * jnp.where(square > 0.0, lax.rsqrt(square), 0.0))
        high = pull.astype(BF16)
        return jnp.concatenate([high, (pull - high.astype(F32)).astype(BF16)], axis=0)

    load_slope.wait()
    atoms = OWN_ROWS // HALF
    own_gather = jnp.where(iota((atoms, OWN_ROWS), 1) // HALF == iota((atoms, OWN_ROWS), 0), 1.0, 0.0)

    def own_step(chunk, total):
        here = pl.ds(pl.multiple_of(chunk * atoms, atoms), atoms)
        rows = pl.ds(pl.multiple_of(chunk * OWN_ROWS, OWN_ROWS), OWN_ROWS)
        slopes = jnp.sum(dot_nt(gsum_ref[here, :], slope_ref[rows, :]) * own_gather, axis=0, keepdims=True)
        return total + dot(pull_of(relt_ref[:, rows], slopes), pair_ref[rows, :])

    def ghost_step(chunk, totals):
        own_total, ghost_total = totals
        rows = pl.ds(pl.multiple_of(chunk * GHOST_ROWS, GHOST_ROWS), GHOST_ROWS)
        slopes = dot_nt(gsum_ref[...], gslope_ref[rows, :])
        slopes = jnp.sum(jnp.where(spread_of(chunk), slopes, 0.0), axis=0, keepdims=True)
        pull = pull_of(grelt_ref[:, rows], slopes)
        return own_total - dot(pull, gatom_ref[rows, :]), ghost_total + dot(pull, gslot_ref[rows, :])

    own_total = lax.fori_loop(0, OWN_CHUNKS, own_step, jnp.zeros((16, ATOMS), F32))
    own_total, ghost_total = lax.fori_loop(0, chunks, ghost_step, (own_total, jnp.zeros((16, GHOST), F32)))
    grad_own_ref[...] = own_total[:8] + own_total[8:]
    grad_ghost_ref[...] = ghost_total[:8] + ghost_total[8:]


def ghost_edges(*operands):
    vmem = pl.BlockSpec(memory_space=pltpu.VMEM)
    hbm = pl.BlockSpec(memory_space=pl.ANY)
    own = ATOMS * HALF
    return pl.pallas_call(
        ghost_body,
        out_shape=(
            jax.ShapeDtypeStruct((ATOMS, FEAT), BF16),
            jax.ShapeDtypeStruct((1, ATOMS), F32),
            jax.ShapeDtypeStruct((8, ATOMS), F32),
            jax.ShapeDtypeStruct((8, GHOST), F32),
        ),
        in_specs=[vmem] * 14 + [hbm] * 2,
        out_specs=(vmem,) * 4,
        scratch_shapes=[
            pltpu.VMEM((len(BLOCKS), 2 * C, 2 * C), BF16),
            pltpu.VMEM((len(BLOCKS), 2 * C, 2 * C), BF16),
            pltpu.VMEM((8, ATOMS), F32),
            pltpu.VMEM((8, GHOST), F32),
            pltpu.VMEM((ATOMS, SLOTS), BF16),
            pltpu.VMEM((ATOMS, SLOTS), BF16),
            pltpu.VMEM((GHOST_ROWS, DEGREES * C), BF16),
            pltpu.VMEM((GHOST_ROWS, DEGREES * C), BF16),
            pltpu.VMEM((own, FEAT), BF16),
            pltpu.VMEM((GHOST_EDGES, FEAT), BF16),
            pltpu.VMEM((GHOST, FEAT), BF16),
            pltpu.VMEM((ATOMS, FEAT), F32),
            pltpu.VMEM((8, GHOST_EDGES), F32),
            pltpu.VMEM((GHOST_EDGES, GHOST), BF16),
            pltpu.VMEM((GHOST_EDGES, ATOMS), BF16),
            pltpu.VMEM((8, 128), F32),
            pltpu.VMEM((ATOMS, FEAT), BF16),
            pltpu.SemaphoreType.DMA((2,)),
        ],
        compiler_params=pltpu.CompilerParams(vmem_limit_bytes=VMEM_LIMIT),
        cost_estimate=pl.CostEstimate(flops=10_000_000_000, bytes_accessed=14_000_000, transcendentals=400_000),
        name="ghost_edges",
    )(*operands)


def padded(shard, sides, width):
    for axis, dim in sides:
        peers, length = (lax.axis_size(axis), shard.shape[dim])
        up = [(i, (i + 1) % peers) for i in range(peers)]
        down = [(j, i) for i, j in up]
        last = lax.slice_in_dim(shard, length - width, length, axis=dim)
        first = lax.slice_in_dim(shard, 0, width, axis=dim)
        before = lax.ppermute(last, axis, up)
        after = lax.ppermute(first, axis, down)
        shard = jnp.concatenate([before, shard, after], axis=dim)
    return shard


def image_shifts():
    side = np.array([-4.0, 0.0, 0.0, 4.0], np.float32)
    grid = np.meshgrid(side, side, side, indexing="ij")
    return jnp.asarray(np.stack(grid), F32)


def fold_axis(received, axis):
    middle = lax.slice_in_dim(received, 2, 4, axis=axis)
    lower = lax.slice_in_dim(received, 0, 1, axis=axis)
    upper = lax.slice_in_dim(received, 5, 6, axis=axis)
    return middle + jnp.concatenate([lower, upper], axis=axis)


def domain(feat, pos, ghost_feat, ghost_places, neigh, counts, rbf, radial, mix, out, energy, norm):
    acc, relt, pairs, slopes = own_edges(feat, pos, neigh, counts, rbf, radial, mix)
    return ghost_edges(
        feat, pos, ghost_places, neigh, counts, rbf, radial, mix, out, energy, norm,
        acc, relt, pairs, slopes, ghost_feat,
    )


def local(
    features, positions, neighbours, counts, cell_atoms,
    rbf_weight, radial_weight, mix_weight, out_weight, energy_weight, norm_weight,
):
    feat = features.reshape(ATOMS, FEAT)
    pos = positions.reshape(3, ATOMS)
    order = cell_atoms.reshape(ATOMS)
    onehot = order[:, None] == jnp.arange(ATOMS, dtype=jnp.int32)[None, :]
    cell_feat = jnp.dot(onehot.astype(BF16), feat, preferred_element_type=F32).astype(BF16)
    cell_places = jnp.sum(jnp.where(onehot[None], pos[:, None, :], 0.0), axis=2)
    ghost_feat = padded(cell_feat.reshape(2, 2, 2, 8, FEAT), (("gx", 0), ("gy", 1), ("gz", 2)), 1)
    ghost_places = padded(cell_places.reshape(3, 2, 2, 2, 8), (("gx", 1), ("gy", 2), ("gz", 3)), 1)
    ghost_places = (ghost_places + image_shifts()[..., None]).reshape(3, -1)
    updated, energies, grad_own, grad_ghost = domain(
        feat, pos, ghost_feat.reshape(GHOST, FEAT), ghost_places,
        neighbours.reshape(ATOMS, SLOTS), counts.reshape(1, ATOMS),
        rbf_weight, radial_weight, mix_weight, out_weight, energy_weight.reshape(1, C), norm_weight,
    )
    grad_blocks = grad_ghost[:3].reshape(3, 4, 4, 4, 8)
    returned = padded(grad_blocks, (("gx", 1), ("gy", 2), ("gz", 3)), 1)
    cell_grad = fold_axis(fold_axis(fold_axis(returned, 1), 2), 3).reshape(3, ATOMS)
    back_own = jnp.sum(jnp.where(onehot[None], cell_grad[:, :, None], 0.0), axis=1)
    forces = -(grad_own[:3] + back_own)
    return (
        updated.reshape(features.shape),
        energies.reshape(counts.shape),
        forces.reshape(positions.shape),
    )


def solution(mesh):
    spread = P("gx", "gy", "gz", None, None)
    rows = P("gx", "gy", "gz", None)
    return jax.shard_map(
        local,
        mesh=mesh,
        in_specs=(spread, spread, spread, rows, rows) + (P(),) * 6,
        out_specs=(spread, rows, spread),
        check_vma=False,
    )
```

time: 454 us -> 144 us (0.32); the launches traced: 447 us -> 144 us
  local copies, waits for them, and re-layouts: 144 us -> 3.5 us
  matrix products: 102 us -> 1.33 us
  other arithmetic: 106 us -> 5.34 us
  Pallas kernels: 0 us -> 42.7 us
  starting transfers between devices: 72.1 us -> 78.6 us
  loops' own time: 6.45 us -> 0 us
    dot_general x184 -> x1, matrix products: 102 us -> 1.33 us  [local(): jnp.dot(onehot.astype(BF16), feat, preferred_element_type=F32).astype(BF16)]
    gather x28 -> x0, local copies, waits for them, and re-layouts: 76.2 us -> none  [the longest x16 59.2 us: block_step(): jnp.take(table_feat, flat_rows, axis=0)]
    pallas_call x0 -> x2, Pallas kernels: none -> 42.7 us  [the longest x1 21.6 us: own_edges(): pl.pallas_call(own_body, out_shape=(jax.ShapeDtypeStruct((ATOMS, FEAT), F...]
    while x754 -> x0, local copies, waits for them, and re-layouts: 26.8 us -> none
    reduce_sum x73 -> x2, other arithmetic: 21.4 us -> 0.21 us  [the longest x1 0.11 us: local(): jnp.sum(jnp.where(onehot[None], cell_grad[:, :, None], 0.0), axis=1)]
    scatter-add x8 -> x0, other arithmetic: 17.6 us -> none  [block_step(): grad_table = grad_table.at[:, flat_rows].add(pull_vec)]
    dynamic_update_slice x16 -> x0, local copies, waits for them, and re-layouts: 15.1 us -> none  [domain_layer(): lax.scan(advance, jnp.zeros(table_places.shape, jnp.float32), scanned)]
    mul x48 -> x0, other arithmetic: 13.8 us -> none  [the longest x8 4.81 us: block_step(): 2.0 * norm_expanded[None, 1:, :] * updated[:, 1:, :]]
  transfers between devices with their start and end apart: 18 -> 18, of which waited for: 6 -> 6; matrix products, arithmetic and copies ran while one was open for 3% -> 2% of each run, Pallas kernels for 0% -> 15%
where the time goes in v1:
time: 144 us
  starting transfers between devices  78.6 us (55%)
  Pallas kernels  42.7 us (30%)
  waiting for transfers between devices  10.7 us (7%)
  other arithmetic  5.34 us (4%)
  local copies, waits for them, and re-layouts  3.5 us (2%)
    ppermute x9, starting transfers between devices, padded(): after = lax.ppermute(first, axis, down)  46.8 us
    ppermute x9, starting transfers between devices, padded(): before = lax.ppermute(last, axis, up)  31.9 us
    pallas_call x1, Pallas kernels, own_edges(): pl.pallas_call(own_body, out_shape=(jax.ShapeDtypeStruct((ATOMS, FEAT), F...  21.6 us
    pallas_call x1, Pallas kernels, ghost_edges(): pl.pallas_call(ghost_body, out_shape=(jax.ShapeDtypeStruct((ATOMS, FEAT),...  21.2 us
    ppermute x9, waiting for transfers between devices, padded(): after = lax.ppermute(first, axis, down)  9.08 us
    concatenate x5, other arithmetic, padded(): shard = jnp.concatenate([before, shard, after], axis=dim)  4.07 us
  transfers between devices with their start and end apart: 18, of which 6 were waited for; matrix products, arithmetic and copies ran while one was open for 2% of the time, Pallas kernels for 15%

profile of v1, /device:TPU:1, one launch (start us, length us, event | category | flops | bytes accessed | tf_op | source)
XLA Modules:
  0.0 143.5 jit_solution(8615150935682409766)
XLA Ops:
  0.6 0.7 copy.21
  1.3 0.7 iota_compare_fusion.2
  2.1 0.1 select_reduce_fusion.1
  2.2 0.1 reshape.74
  2.3 8.8 %collective-permute-start.1 = (f32[3,1,2,2,8]{4,3,2,1,0:T(2,128)S(1)}, f32[3,1,2,2,8]{4,3,2,1,0:T(2,128)S(1)}, u32[]{:S(2)}, u32[]{:S(2)}) collective-permute-start(f32[3,1,2,2,8]{4,3,2,1,0:T(2,128)S(1)} %get-tuple-element.45), channel_id=1, source_target_pairs={{128,0},{256,128},{384,256},{0,384},{129,1},{257,129},{385,257},{1... | collective-permute-start | bytes 1160 | tf_op jit(solution)/shard_map/ppermute | solution.py:364
  11.1 1.9 %collective-permute-start = (f32[3,1,2,2,8]{4,3,2,1,0:T(2,128)S(1)}, f32[3,1,2,2,8]{4,3,2,1,0:T(2,128)S(1)}, u32[]{:S(2)}, u32[]{:S(2)}) collective-permute-start(f32[3,1,2,2,8]{4,3,2,1,0:T(2,128)S(1)} %get-tuple-element.46), channel_id=1, source_target_pairs={{0,128},{128,256},{256,384},{384,0},{1,129},{129,257},{257,385},{3... | collective-permute-start | bytes 1160 | tf_op jit(solution)/shard_map/ppermute | solution.py:363
  13.0 1.3 convolution_convert_fusion
  14.4 2.4 %collective-permute-start.7 = (bf16[1,2,2,8,3200]{4,3,2,1,0:T(8,128)(2,1)S(1)}, bf16[1,2,2,8,3200]{4,3,2,1,0:T(8,128)(2,1)S(1)}, u32[]{:S(2)}, u32[]{:S(2)}) collective-permute-start(bf16[1,2,2,8,3200]{4,3,2,1,0:T(8,128)(2,1)S(1)} %bitcast.33), channel_id=1, source_target_pairs={{128,0},{256,128},{384,256},{0,384},{129,1},{257,129},{385,257},{1... | collective-permute-start | bytes 614408 | tf_op jit(solution)/shard_map/ppermute | solution.py:364
  16.8 4.7 %collective-permute-start.6 = (bf16[1,2,2,8,3200]{4,3,2,1,0:T(8,128)(2,1)S(1)}, bf16[1,2,2,8,3200]{4,3,2,1,0:T(8,128)(2,1)S(1)}, u32[]{:S(2)}, u32[]{:S(2)}) collective-permute-start(bf16[1,2,2,8,3200]{4,3,2,1,0:T(8,128)(2,1)S(1)} %bitcast.32), channel_id=1, source_target_pairs={{0,128},{128,256},{256,384},{384,0},{1,129},{129,257},{257,385},{3... | collective-permute-start | bytes 614408 | tf_op jit(solution)/shard_map/ppermute | solution.py:363
  21.5 1.4 %collective-permute-done.7 = bf16[1,2,2,8,3200]{4,3,2,1,0:T(8,128)(2,1)S(1)} collective-permute-done((bf16[1,2,2,8,3200]{4,3,2,1,0:T(8,128)(2,1)S(1)}, bf16[1,2,2,8,3200]{4,3,2,1,0:T(8,128)(2,1)S(1)}, u32[]{:S(2)}, u32[]{:S(2)}) %collective-permute-start.7) | collective-permute-done | bytes 204832 | tf_op jit(solution)/shard_map/ppermute | solution.py:364
  23.0 1.6 %collective-permute-done.6 = bf16[1,2,2,8,3200]{4,3,2,1,0:T(8,128)(2,1)S(1)} collective-permute-done((bf16[1,2,2,8,3200]{4,3,2,1,0:T(8,128)(2,1)S(1)}, bf16[1,2,2,8,3200]{4,3,2,1,0:T(8,128)(2,1)S(1)}, u32[]{:S(2)}, u32[]{:S(2)}) %collective-permute-start.6) | collective-permute-done | bytes 204832 | tf_op jit(solution)/shard_map/ppermute | solution.py:363
  24.6 0.1 pad_maximum_fusion.2
  24.7 0.1 fusion.14
  24.8 1.9 %collective-permute-start.8 = (bf16[4,1,2,8,3200]{4,3,2,1,0:T(8,128)(2,1)S(1)}, bf16[4,1,2,8,3200]{4,3,2,1,0:T(8,128)(2,1)S(1)}, u32[]{:S(2)}, u32[]{:S(2)}) collective-permute-start(bf16[4,1,2,8,3200]{4,3,2,1,0:T(8,128)(2,1)S(1)} %get-tuple-element.27), channel_id=1, source_target_pairs={{0,32},{32,64},{64,96},{96,0},{1,33},{33,65},{65,97},{97,1},{2,34}... | collective-permute-start | bytes 1228808 | tf_op jit(solution)/shard_map/ppermute | solution.py:363
  26.7 4.6 %collective-permute-start.9 = (bf16[4,1,2,8,3200]{4,3,2,1,0:T(8,128)(2,1)S(1)}, bf16[4,1,2,8,3200]{4,3,2,1,0:T(8,128)(2,1)S(1)}, u32[]{:S(2)}, u32[]{:S(2)}) collective-permute-start(bf16[4,1,2,8,3200]{4,3,2,1,0:T(8,128)(2,1)S(1)} %get-tuple-element.28), channel_id=1, source_target_pairs={{32,0},{64,32},{96,64},{0,96},{33,1},{65,33},{97,65},{1,97},{34,2}... | collective-permute-start | bytes 1228808 | tf_op jit(solution)/shard_map/ppermute | solution.py:364
  31.3 1.9 %collective-permute-start.2 = (f32[3,4,1,2,8]{4,3,2,1,0:T(2,128)S(1)}, f32[3,4,1,2,8]{4,3,2,1,0:T(2,128)S(1)}, u32[]{:S(2)}, u32[]{:S(2)}) collective-permute-start(f32[3,4,1,2,8]{4,3,2,1,0:T(2,128)S(1)} %get-tuple-element.43), channel_id=1, source_target_pairs={{0,32},{32,64},{64,96},{96,0},{1,33},{33,65},{65,97},{97,1},{2,34}... | collective-permute-start | bytes 2312 | tf_op jit(solution)/shard_map/ppermute | solution.py:363
  33.2 4.6 %collective-permute-start.3 = (f32[3,4,1,2,8]{4,3,2,1,0:T(2,128)S(1)}, f32[3,4,1,2,8]{4,3,2,1,0:T(2,128)S(1)}, u32[]{:S(2)}, u32[]{:S(2)}) collective-permute-start(f32[3,4,1,2,8]{4,3,2,1,0:T(2,128)S(1)} %get-tuple-element.44), channel_id=1, source_target_pairs={{32,0},{64,32},{96,64},{0,96},{33,1},{65,33},{97,65},{1,97},{34,2}... | collective-permute-start | bytes 2312 | tf_op jit(solution)/shard_map/ppermute | solution.py:364
  37.8 0.1 copy.17
  37.9 0.7 collective-permute-done.3
  38.7 1.9 %collective-permute-start.4 = (f32[3,4,4,1,8]{4,3,2,1,0:T(1,128)S(1)}, f32[3,4,4,1,8]{4,3,2,1,0:T(1,128)S(1)}, u32[]{:S(2)}, u32[]{:S(2)}) collective-permute-start(f32[3,4,4,1,8]{4,3,2,1,0:T(1,128)S(1)} %get-tuple-element.41), channel_id=1, source_target_pairs={{0,1},{1,2},{2,3},{3,4},{4,5},{5,6},{6,7},{7,8},{8,9},{9,10},{10,1... | collective-permute-start | bytes 4616 | tf_op jit(solution)/shard_map/ppermute | solution.py:363
  40.6 0.0 copy-start
  40.7 9.0 %collective-permute-start.5 = (f32[3,4,4,1,8]{4,3,2,1,0:T(1,128)S(1)}, f32[3,4,4,1,8]{4,3,2,1,0:T(1,128)S(1)}, u32[]{:S(2)}, u32[]{:S(2)}) collective-permute-start(f32[3,4,4,1,8]{4,3,2,1,0:T(1,128)S(1)} %get-tuple-element.42), channel_id=1, source_target_pairs={{1,0},{2,1},{3,2},{4,3},{5,4},{6,5},{7,6},{8,7},{9,8},{10,9},{11,1... | collective-permute-start | bytes 4616 | tf_op jit(solution)/shard_map/ppermute | solution.py:364
  49.7 0.3 pad_maximum_fusion.1
  50.0 1.4 fusion.13
  51.4 1.9 %collective-permute-start.10 = (bf16[4,4,1,8,3200]{4,3,2,1,0:T(8,128)(2,1)}, bf16[4,4,1,8,3200]{4,3,2,1,0:T(8,128)(2,1)}, u32[]{:S(2)}, u32[]{:S(2)}) collective-permute-start(bf16[4,4,1,8,3200]{4,3,2,1,0:T(8,128)(2,1)} %get-tuple-element.25), channel_id=1, source_target_pairs={{0,1},{1,2},{2,3},{3,4},{4,5},{5,6},{6,7},{7,8},{8,9},{9,10},{10,1... | collective-permute-start | bytes 2457608 | tf_op jit(solution)/shard_map/ppermute | solution.py:363
  53.3 5.5 %collective-permute-start.11 = (bf16[4,4,1,8,3200]{4,3,2,1,0:T(8,128)(2,1)}, bf16[4,4,1,8,3200]{4,3,2,1,0:T(8,128)(2,1)}, u32[]{:S(2)}, u32[]{:S(2)}) collective-permute-start(bf16[4,4,1,8,3200]{4,3,2,1,0:T(8,128)(2,1)} %get-tuple-element.26), channel_id=1, source_target_pairs={{1,0},{2,1},{3,2},{4,3},{5,4},{6,5},{7,6},{8,7},{9,8},{10,9},{11,1... | collective-permute-start | bytes 2457608 | tf_op jit(solution)/shard_map/ppermute | solution.py:364
  58.8 0.0 copy-start.9
  58.9 21.6 %own_edges.1 = (f32[64,3200]{1,0:T(8,128)S(1)}, f32[8,1024]{1,0:T(8,128)S(1)}, bf16[1024,64]{1,0:T(8,128)(2,1)S(1)}, bf16[1024,3200]{1,0:T(8,128)(2,1)}) custom-call(bf16[64,3200]{1,0:T(8,128)(2,1)S(1)} %bitcast.18, f32[3,64]{1,0:T(4,128)S(1)} %bitcast.23, s32[64,32]{1,0:T(8,128)S(1)} %bitcast.20, s32[1,64]{1,0:T(1,128)S(1)} %bitcast.25, ...), custom_call_target="tpu_custom_call" | custom-call | flops 8000000000 | bytes 10000000 | tf_op jit(solution)/shard_map/own_edges/pallas_call | solution.py:174
  80.5 0.1 maximum_add_fusion
  80.6 0.1 add.26.gpos_ref
  80.8 3.5 %pad_maximum_fusion = bf16[4,4,4,8,3200]{4,3,2,1,0:T(8,128)(2,1)} fusion(bf16[4,4,1,8,3200]{4,3,2,1,0:T(8,128)(2,1)} %collective-permute-done.11, bf16[4,1,2,8,3200]{4,3,2,1,0:T(8,128)(2,1)} %copy-done.8, bf16[1,2,2,8,3200]{4,3,2,1,0:T(8,128)(2,1)S(1)} %collective-permute-done.7, bf16[2,2,2,8,3200]{4,3,2,1,0:T(8,128)(2,1)S(1)} %bitcast.30, ...), kind=kLoop, calls=%fused_computation.1 | loop fusion | flops 9830400 | bytes 6553600 | tf_op jit(solution)/shard_map/concatenate | solution.py:365
  84.3 21.2 %ghost_edges.1 = (bf16[64,3200]{1,0:T(8,128)(2,1)}, f32[1,64]{1,0:T(1,128)}, f32[8,64]{1,0:T(8,128)S(1)}, f32[8,512]{1,0:T(8,128)S(1)}) custom-call(bf16[64,3200]{1,0:T(8,128)(2,1)S(1)} %bitcast.19, f32[3,64]{1,0:T(4,128)S(1)} %bitcast.24, f32[3,512]{1,0:T(4,128)S(1)} %add.26.gpos_ref, s32[64,32]{1,0:T(8,128)S(1)} %bitcast.21, s32[1,64]{1,0:T(1,128)S(1)} %bitcast.26, ...), custom_call_target="tpu_custom_call" | custom-call | flops 10000000000 | bytes 14000000 | tf_op jit(solution)/shard_map/ghost_edges/pallas_call | solution.py:320
  105.5 0.2 reshape.82
  105.6 13.8 %collective-permute-start.12 = (f32[3,1,4,4,8]{4,3,2,1,0:T(4,128)S(1)}, f32[3,1,4,4,8]{4,3,2,1,0:T(4,128)S(1)}, u32[]{:S(2)}, u32[]{:S(2)}) collective-permute-start(f32[3,1,4,4,8]{4,3,2,1,0:T(4,128)S(1)} %get-tuple-element.38), channel_id=1, source_target_pairs={{0,128},{128,256},{256,384},{384,0},{1,129},{129,257},{257,385},{3... | collective-permute-start | bytes 4616 | tf_op jit(solution)/shard_map/ppermute | solution.py:363
  119.4 1.9 %collective-permute-start.13 = (f32[3,1,4,4,8]{4,3,2,1,0:T(4,128)S(1)}, f32[3,1,4,4,8]{4,3,2,1,0:T(4,128)S(1)}, u32[]{:S(2)}, u32[]{:S(2)}) collective-permute-start(f32[3,1,4,4,8]{4,3,2,1,0:T(4,128)S(1)} %get-tuple-element.37), channel_id=1, source_target_pairs={{128,0},{256,128},{384,256},{0,384},{129,1},{257,129},{385,257},{1... | collective-permute-start | bytes 4616 | tf_op jit(solution)/shard_map/ppermute | solution.py:364
  121.4 4.7 %collective-permute-done.13 = f32[3,1,4,4,8]{4,3,2,1,0:T(4,128)S(1)} collective-permute-done((f32[3,1,4,4,8]{4,3,2,1,0:T(4,128)S(1)}, f32[3,1,4,4,8]{4,3,2,1,0:T(4,128)S(1)}, u32[]{:S(2)}, u32[]{:S(2)}) %collective-permute-start.13) | collective-permute-done | bytes 1568 | tf_op jit(solution)/shard_map/ppermute | solution.py:364
  126.1 1.9 %collective-permute-start.14 = (f32[3,6,1,4,8]{4,3,2,1,0:T(4,128)S(1)}, f32[3,6,1,4,8]{4,3,2,1,0:T(4,128)S(1)}, u32[]{:S(2)}, u32[]{:S(2)}) collective-permute-start(f32[3,6,1,4,8]{4,3,2,1,0:T(4,128)S(1)} %get-tuple-element.35), channel_id=1, source_target_pairs={{0,32},{32,64},{64,96},{96,0},{1,33},{33,65},{65,97},{97,1},{2,34}... | collective-permute-start | bytes 6920 | tf_op jit(solution)/shard_map/ppermute | solution.py:363
  128.0 4.6 %collective-permute-start.15 = (f32[3,6,1,4,8]{4,3,2,1,0:T(4,128)S(1)}, f32[3,6,1,4,8]{4,3,2,1,0:T(4,128)S(1)}, u32[]{:S(2)}, u32[]{:S(2)}) collective-permute-start(f32[3,6,1,4,8]{4,3,2,1,0:T(4,128)S(1)} %get-tuple-element.36), channel_id=1, source_target_pairs={{32,0},{64,32},{96,64},{0,96},{33,1},{65,33},{97,65},{1,97},{34,2}... | collective-permute-start | bytes 6920 | tf_op jit(solution)/shard_map/ppermute | solution.py:364
  132.6 1.0 collective-permute-done.15
  133.7 0.1 pad_maximum_fusion.6
  133.8 1.9 %collective-permute-start.16 = (f32[3,6,6,1,8]{4,3,2,1,0:T(1,128)S(1)}, f32[3,6,6,1,8]{4,3,2,1,0:T(1,128)S(1)}, u32[]{:S(2)}, u32[]{:S(2)}) collective-permute-start(f32[3,6,6,1,8]{4,3,2,1,0:T(1,128)S(1)} %get-tuple-element.31), channel_id=1, source_target_pairs={{0,1},{1,2},{2,3},{3,4},{4,5},{5,6},{6,7},{7,8},{8,9},{9,10},{10,1... | collective-permute-start | bytes 10376 | tf_op jit(solution)/shard_map/ppermute | solution.py:363
  135.7 5.5 %collective-permute-start.17 = (f32[3,6,6,1,8]{4,3,2,1,0:T(1,128)S(1)}, f32[3,6,6,1,8]{4,3,2,1,0:T(1,128)S(1)}, u32[]{:S(2)}, u32[]{:S(2)}) collective-permute-start(f32[3,6,6,1,8]{4,3,2,1,0:T(1,128)S(1)} %get-tuple-element.32), channel_id=1, source_target_pairs={{1,0},{2,1},{3,2},{4,3},{5,4},{6,5},{7,6},{8,7},{9,8},{10,9},{11,1... | collective-permute-start | bytes 10376 | tf_op jit(solution)/shard_map/ppermute | solution.py:364
  141.2 1.2 collective-permute-done.17
  142.4 0.2 pad_maximum_fusion.3
  142.6 0.1 fusion.1
  142.7 0.1 broadcast_in_dim.45
  142.8 0.1 select_reduce_fusion
  142.9 0.6 copy.18
  (51 shorter events, 0.3 us)
Async XLA Ops:
  0.6 37.2 %copy-start.10 = (s32[1,1,1,64,32]{3,4,2,1,0:T(8,128)S(1)}, s32[1,1,1,64,32]{3,4,2,1,0:T(8,128)}, u32[]{:S(2)}) copy-start(s32[1,1,1,64,32]{3,4,2,1,0:T(8,128)} %param.14) | copy-start | bytes 24580
  2.3 19.2 %collective-permute-start.1 = (f32[3,1,2,2,8]{4,3,2,1,0:T(2,128)S(1)}, f32[3,1,2,2,8]{4,3,2,1,0:T(2,128)S(1)}, u32[]{:S(2)}, u32[]{:S(2)}) collective-permute-start(f32[3,1,2,2,8]{4,3,2,1,0:T(2,128)S(1)} %get-tuple-element.45), channel_id=1, source_target_pairs={{128,0},{256,128},{384,256},{0,384},{129,1},{257,129},{385,257},{1... | collective-permute-start | bytes 1160 | tf_op jit(solution)/shard_map/ppermute | solution.py:364
  11.1 10.4 %collective-permute-start = (f32[3,1,2,2,8]{4,3,2,1,0:T(2,128)S(1)}, f32[3,1,2,2,8]{4,3,2,1,0:T(2,128)S(1)}, u32[]{:S(2)}, u32[]{:S(2)}) collective-permute-start(f32[3,1,2,2,8]{4,3,2,1,0:T(2,128)S(1)} %get-tuple-element.46), channel_id=1, source_target_pairs={{0,128},{128,256},{256,384},{384,0},{1,129},{129,257},{257,385},{3... | collective-permute-start | bytes 1160 | tf_op jit(solution)/shard_map/ppermute | solution.py:363
  14.4 8.6 %collective-permute-start.7 = (bf16[1,2,2,8,3200]{4,3,2,1,0:T(8,128)(2,1)S(1)}, bf16[1,2,2,8,3200]{4,3,2,1,0:T(8,128)(2,1)S(1)}, u32[]{:S(2)}, u32[]{:S(2)}) collective-permute-start(bf16[1,2,2,8,3200]{4,3,2,1,0:T(8,128)(2,1)S(1)} %bitcast.33), channel_id=1, source_target_pairs={{128,0},{256,128},{384,256},{0,384},{129,1},{257,129},{385,257},{1... | collective-permute-start | bytes 614408 | tf_op jit(solution)/shard_map/ppermute | solution.py:364
  16.8 7.8 %collective-permute-start.6 = (bf16[1,2,2,8,3200]{4,3,2,1,0:T(8,128)(2,1)S(1)}, bf16[1,2,2,8,3200]{4,3,2,1,0:T(8,128)(2,1)S(1)}, u32[]{:S(2)}, u32[]{:S(2)}) collective-permute-start(bf16[1,2,2,8,3200]{4,3,2,1,0:T(8,128)(2,1)S(1)} %bitcast.32), channel_id=1, source_target_pairs={{0,128},{128,256},{256,384},{384,0},{1,129},{129,257},{257,385},{3... | collective-permute-start | bytes 614408 | tf_op jit(solution)/shard_map/ppermute | solution.py:363
  24.8 24.9 %collective-permute-start.8 = (bf16[4,1,2,8,3200]{4,3,2,1,0:T(8,128)(2,1)S(1)}, bf16[4,1,2,8,3200]{4,3,2,1,0:T(8,128)(2,1)S(1)}, u32[]{:S(2)}, u32[]{:S(2)}) collective-permute-start(bf16[4,1,2,8,3200]{4,3,2,1,0:T(8,128)(2,1)S(1)} %get-tuple-element.27), channel_id=1, source_target_pairs={{0,32},{32,64},{64,96},{96,0},{1,33},{33,65},{65,97},{97,1},{2,34}... | collective-permute-start | bytes 1228808 | tf_op jit(solution)/shard_map/ppermute | solution.py:363
  26.7 23.0 %collective-permute-start.9 = (bf16[4,1,2,8,3200]{4,3,2,1,0:T(8,128)(2,1)S(1)}, bf16[4,1,2,8,3200]{4,3,2,1,0:T(8,128)(2,1)S(1)}, u32[]{:S(2)}, u32[]{:S(2)}) collective-permute-start(bf16[4,1,2,8,3200]{4,3,2,1,0:T(8,128)(2,1)S(1)} %get-tuple-element.28), channel_id=1, source_target_pairs={{32,0},{64,32},{96,64},{0,96},{33,1},{65,33},{97,65},{1,97},{34,2}... | collective-permute-start | bytes 1228808 | tf_op jit(solution)/shard_map/ppermute | solution.py:364
  31.3 6.6 %collective-permute-start.2 = (f32[3,4,1,2,8]{4,3,2,1,0:T(2,128)S(1)}, f32[3,4,1,2,8]{4,3,2,1,0:T(2,128)S(1)}, u32[]{:S(2)}, u32[]{:S(2)}) collective-permute-start(f32[3,4,1,2,8]{4,3,2,1,0:T(2,128)S(1)} %get-tuple-element.43), channel_id=1, source_target_pairs={{0,32},{32,64},{64,96},{96,0},{1,33},{33,65},{65,97},{97,1},{2,34}... | collective-permute-start | bytes 2312 | tf_op jit(solution)/shard_map/ppermute | solution.py:363
  33.2 5.4 %collective-permute-start.3 = (f32[3,4,1,2,8]{4,3,2,1,0:T(2,128)S(1)}, f32[3,4,1,2,8]{4,3,2,1,0:T(2,128)S(1)}, u32[]{:S(2)}, u32[]{:S(2)}) collective-permute-start(f32[3,4,1,2,8]{4,3,2,1,0:T(2,128)S(1)} %get-tuple-element.44), channel_id=1, source_target_pairs={{32,0},{64,32},{96,64},{0,96},{33,1},{65,33},{97,65},{1,97},{34,2}... | collective-permute-start | bytes 2312 | tf_op jit(solution)/shard_map/ppermute | solution.py:364
  38.7 41.7 %collective-permute-start.4 = (f32[3,4,4,1,8]{4,3,2,1,0:T(1,128)S(1)}, f32[3,4,4,1,8]{4,3,2,1,0:T(1,128)S(1)}, u32[]{:S(2)}, u32[]{:S(2)}) collective-permute-start(f32[3,4,4,1,8]{4,3,2,1,0:T(1,128)S(1)} %get-tuple-element.41), channel_id=1, source_target_pairs={{0,1},{1,2},{2,3},{3,4},{4,5},{5,6},{6,7},{7,8},{8,9},{9,10},{10,1... | collective-permute-start | bytes 4616 | tf_op jit(solution)/shard_map/ppermute | solution.py:363
  40.6 18.2 %copy-start = (bf16[1,1,1,64,3200]{4,3,2,1,0:T(8,128)(2,1)S(1)}, bf16[1,1,1,64,3200]{4,3,2,1,0:T(8,128)(2,1)}, u32[]{:S(2)}) copy-start(bf16[1,1,1,64,3200]{4,3,2,1,0:T(8,128)(2,1)} %param.12) | copy-start | bytes 1228804
  40.6 18.2 %copy-start.1 = (bf16[128,640]{1,0:T(8,128)(2,1)S(1)}, bf16[128,640]{1,0:T(8,128)(2,1)}, u32[]{:S(2)}) copy-start(bf16[128,640]{1,0:T(8,128)(2,1)} %radial_ref.3) | copy-start | bytes 491524
  40.7 18.2 %copy-start.2 = (bf16[5,128,128]{2,1,0:T(8,128)(2,1)S(1)}, bf16[5,128,128]{2,1,0:T(8,128)(2,1)}, u32[]{:S(2)}) copy-start(bf16[5,128,128]{2,1,0:T(8,128)(2,1)} %mix_ref.3) | copy-start | bytes 491524
  40.7 18.2 %copy-start.4 = (bf16[512,128]{1,0:T(8,128)(2,1)S(1)}, bf16[512,128]{1,0:T(8,128)(2,1)}, u32[]{:S(2)}) copy-start(bf16[512,128]{1,0:T(8,128)(2,1)} %rbf_ref.3) | copy-start | bytes 393220
  40.7 18.1 %copy-start.6 = (s32[1,1,1,64]{3,2,1,0:T(1,128)S(1)}, s32[1,1,1,64]{3,2,1,0:T(1,128)}, u32[]{:S(2)}) copy-start(s32[1,1,1,64]{3,2,1,0:T(1,128)} %param.15) | copy-start | bytes 772
  40.7 39.8 %collective-permute-start.5 = (f32[3,4,4,1,8]{4,3,2,1,0:T(1,128)S(1)}, f32[3,4,4,1,8]{4,3,2,1,0:T(1,128)S(1)}, u32[]{:S(2)}, u32[]{:S(2)}) collective-permute-start(f32[3,4,4,1,8]{4,3,2,1,0:T(1,128)S(1)} %get-tuple-element.42), channel_id=1, source_target_pairs={{1,0},{2,1},{3,2},{4,3},{5,4},{6,5},{7,6},{8,7},{9,8},{10,9},{11,1... | collective-permute-start | bytes 4616 | tf_op jit(solution)/shard_map/ppermute | solution.py:364
  49.7 1.7 %copy-start.8 = (bf16[4,1,2,8,3200]{4,3,2,1,0:T(8,128)(2,1)}, bf16[4,1,2,8,3200]{4,3,2,1,0:T(8,128)(2,1)S(1)}, u32[]{:S(2)}) copy-start(bf16[4,1,2,8,3200]{4,3,2,1,0:T(8,128)(2,1)S(1)} %collective-permute-done.9) | copy-start | bytes 1228804
  51.4 29.4 %collective-permute-start.10 = (bf16[4,4,1,8,3200]{4,3,2,1,0:T(8,128)(2,1)}, bf16[4,4,1,8,3200]{4,3,2,1,0:T(8,128)(2,1)}, u32[]{:S(2)}, u32[]{:S(2)}) collective-permute-start(bf16[4,4,1,8,3200]{4,3,2,1,0:T(8,128)(2,1)} %get-tuple-element.25), channel_id=1, source_target_pairs={{0,1},{1,2},{2,3},{3,4},{4,5},{5,6},{6,7},{7,8},{8,9},{9,10},{10,1... | collective-permute-start | bytes 2457608 | tf_op jit(solution)/shard_map/ppermute | solution.py:363
  53.3 27.5 %collective-permute-start.11 = (bf16[4,4,1,8,3200]{4,3,2,1,0:T(8,128)(2,1)}, bf16[4,4,1,8,3200]{4,3,2,1,0:T(8,128)(2,1)}, u32[]{:S(2)}, u32[]{:S(2)}) collective-permute-start(bf16[4,4,1,8,3200]{4,3,2,1,0:T(8,128)(2,1)} %get-tuple-element.26), channel_id=1, source_target_pairs={{1,0},{2,1},{3,2},{4,3},{5,4},{6,5},{7,6},{8,7},{9,8},{10,9},{11,1... | collective-permute-start | bytes 2457608 | tf_op jit(solution)/shard_map/ppermute | solution.py:364
  58.8 21.6 %copy-start.9 = (f32[3,4,4,4]{3,2,1,0:T(4,128)S(1)}, f32[3,4,4,4]{3,2,1,0:T(4,128)}, u32[]{:S(2)}) copy-start(f32[3,4,4,4]{3,2,1,0:T(4,128)} %constant.4.clone) | copy-start | bytes 2308
  80.7 3.5 %copy-start.3 = (bf16[5,128,128]{2,1,0:T(8,128)(2,1)S(1)}, bf16[5,128,128]{2,1,0:T(8,128)(2,1)}, u32[]{:S(2)}) copy-start(bf16[5,128,128]{2,1,0:T(8,128)(2,1)} %out_ref.1) | copy-start | bytes 491524
  80.8 3.5 %copy-start.5 = (f32[4,128]{1,0:T(4,128)S(1)}, f32[4,128]{1,0:T(4,128)}, u32[]{:S(2)}) copy-start(f32[4,128]{1,0:T(4,128)} %norm_ref.1) | copy-start | bytes 6148
  80.8 3.5 %copy-start.7 = (f32[128]{0:T(128)S(1)}, f32[128]{0:T(128)}, u32[]{:S(2)}) copy-start(f32[128]{0:T(128)} %param.21) | copy-start | bytes 1540
  105.6 15.7 %collective-permute-start.12 = (f32[3,1,4,4,8]{4,3,2,1,0:T(4,128)S(1)}, f32[3,1,4,4,8]{4,3,2,1,0:T(4,128)S(1)}, u32[]{:S(2)}, u32[]{:S(2)}) collective-permute-start(f32[3,1,4,4,8]{4,3,2,1,0:T(4,128)S(1)} %get-tuple-element.38), channel_id=1, source_target_pairs={{0,128},{128,256},{256,384},{384,0},{1,129},{129,257},{257,385},{3... | collective-permute-start | bytes 4616 | tf_op jit(solution)/shard_map/ppermute | solution.py:363
  119.4 6.7 %collective-permute-start.13 = (f32[3,1,4,4,8]{4,3,2,1,0:T(4,128)S(1)}, f32[3,1,4,4,8]{4,3,2,1,0:T(4,128)S(1)}, u32[]{:S(2)}, u32[]{:S(2)}) collective-permute-start(f32[3,1,4,4,8]{4,3,2,1,0:T(4,128)S(1)} %get-tuple-element.37), channel_id=1, source_target_pairs={{128,0},{256,128},{384,256},{0,384},{129,1},{257,129},{385,257},{1... | collective-permute-start | bytes 4616 | tf_op jit(solution)/shard_map/ppermute | solution.py:364
  126.1 6.5 %collective-permute-start.14 = (f32[3,6,1,4,8]{4,3,2,1,0:T(4,128)S(1)}, f32[3,6,1,4,8]{4,3,2,1,0:T(4,128)S(1)}, u32[]{:S(2)}, u32[]{:S(2)}) collective-permute-start(f32[3,6,1,4,8]{4,3,2,1,0:T(4,128)S(1)} %get-tuple-element.35), channel_id=1, source_target_pairs={{0,32},{32,64},{64,96},{96,0},{1,33},{33,65},{65,97},{97,1},{2,34}... | collective-permute-start | bytes 6920 | tf_op jit(solution)/shard_map/ppermute | solution.py:363
  128.0 5.6 %collective-permute-start.15 = (f32[3,6,1,4,8]{4,3,2,1,0:T(4,128)S(1)}, f32[3,6,1,4,8]{4,3,2,1,0:T(4,128)S(1)}, u32[]{:S(2)}, u32[]{:S(2)}) collective-permute-start(f32[3,6,1,4,8]{4,3,2,1,0:T(4,128)S(1)} %get-tuple-element.36), channel_id=1, source_target_pairs={{32,0},{64,32},{96,64},{0,96},{33,1},{65,33},{97,65},{1,97},{34,2}... | collective-permute-start | bytes 6920 | tf_op jit(solution)/shard_map/ppermute | solution.py:364
  133.8 7.4 %collective-permute-start.16 = (f32[3,6,6,1,8]{4,3,2,1,0:T(1,128)S(1)}, f32[3,6,6,1,8]{4,3,2,1,0:T(1,128)S(1)}, u32[]{:S(2)}, u32[]{:S(2)}) collective-permute-start(f32[3,6,6,1,8]{4,3,2,1,0:T(1,128)S(1)} %get-tuple-element.31), channel_id=1, source_target_pairs={{0,1},{1,2},{2,3},{3,4},{4,5},{5,6},{6,7},{7,8},{8,9},{9,10},{10,1... | collective-permute-start | bytes 10376 | tf_op jit(solution)/shard_map/ppermute | solution.py:363
  135.7 6.7 %collective-permute-start.17 = (f32[3,6,6,1,8]{4,3,2,1,0:T(1,128)S(1)}, f32[3,6,6,1,8]{4,3,2,1,0:T(1,128)S(1)}, u32[]{:S(2)}, u32[]{:S(2)}) collective-permute-start(f32[3,6,6,1,8]{4,3,2,1,0:T(1,128)S(1)} %get-tuple-element.32), channel_id=1, source_target_pairs={{1,0},{2,1},{3,2},{4,3},{5,4},{6,5},{7,6},{8,7},{9,8},{10,9},{11,1... | collective-permute-start | bytes 10376 | tf_op jit(solution)/shard_map/ppermute | solution.py:364

commit v2 on v1

--- a/solution.py
+++ b/solution.py
@@ -1,9 +1,7 @@
-from functools import partial
 import math
 
 import jax
 import jax.numpy as jnp
-import numpy as np
 from jax import lax
 from jax.experimental import pallas as pl
 from jax.experimental.pallas import tpu as pltpu
@@ -12,6 +10,10 @@
 F32, BF16 = jnp.float32, jnp.bfloat16
 ATOMS, SLOTS, HALF, C, FEAT, RBF, DEGREES = 64, 32, 16, 128, 3200, 512, 5
 GHOST = 512
+WIDE = FEAT + C
+DIRECTIONS = 27
+TILES = 14
+MESH_ID = pl.DeviceIdType.MESH
 COEFFS = FEAT // C
 DEGREE = [degree for degree in range(DEGREES) for _ in range(2 * degree + 1)]
 PAIRS = [tuple(range(k, min(k + 2, COEFFS))) for k in range(0, COEFFS, 2)]
@@ -87,12 +89,15 @@
     drad_ref[...] = dot(dhidden, radial_ref[...]).astype(BF16)
 
 
-def edge_forward(onehot, table_ref, rad_ref, drad_ref, block_ref, mix_ref, put_message, put_slope):
+def edge_forward(onehot, table_ref, rad_ref, drad_ref, block_ref, mix_ref, put_message, put_slope, last=None):
     rows = onehot.shape[0]
     gate = lean = None
     for pair in PAIRS:
         lanes = slice(pair[0] * C, (pair[-1] + 1) * C)
-        near = dot(onehot, table_ref[:, lanes]).astype(BF16)
+        if len(pair) == 1 and last is not None:
+            near = last
+        else:
+            near = dot(onehot, table_ref[:, lanes]).astype(BF16)
         cuts = [slice(DEGREE[k] * C, (DEGREE[k] + 1) * C) for k in pair]
         rad = jnp.concatenate([rad_ref[:, cut] for cut in cuts], axis=1)
         drad = jnp.concatenate([drad_ref[:, cut] for cut in cuts], axis=1)
@@ -115,15 +120,91 @@
     return (rows >> 3).astype(F32).astype(BF16), (rows & 7).astype(F32).astype(BF16)
 
 
+def column_of(row):
+    square = (ATOMS, ATOMS)
+    return jnp.sum(jnp.where(iota(square, 0) == iota(square, 1), row, 0.0), axis=1, keepdims=True)
+
+
+def halo_copies(table_ref, send_sem, recv_sem):
+    gx, gy, gz = (lax.axis_index(axis) for axis in ("gx", "gy", "gz"))
+    nx, ny, nz = (lax.axis_size(axis) for axis in ("gx", "gy", "gz"))
+    odd = lax.rem(gx, 2)
+    sibling = (gx + 1 - 2 * odd, gy, gz)
+    far = (lax.rem(gx + nx - 1 + 2 * odd, nx), gy, gz)
+    down_y, up_y = ((gx, lax.rem(gy + ny + step, ny), gz) for step in (-1, 1))
+    down_z, up_z = ((gx, gy, lax.rem(gz + nz + step, nz)) for step in (-1, 1))
+    far_cell, shared, far_own = 3 * odd, 2 - odd, 1 + odd
+    far_target, sibling_target = 3 - 3 * odd, 3 * odd
+    one = lambda at: pl.ds(at, 1)
+    inner, whole = pl.ds(1, 2), pl.ds(0, 4)
+    plan = ([], [], [], [])
+
+    def add(stage, device, x, y, z, to_x=None, to_y=None, to_z=None):
+        at = sum(len(items) for items in plan)
+        source = table_ref.at[x, y, z]
+        target = table_ref.at[
+            x if to_x is None else one(to_x), y if to_y is None else one(to_y), z if to_z is None else one(to_z)
+        ]
+        plan[stage].append(
+            pltpu.make_async_remote_copy(
+                src_ref=source, dst_ref=target, send_sem=send_sem.at[at], recv_sem=recv_sem.at[at],
+                device_id=device, device_id_type=MESH_ID,
+            )
+        )
+
+    ends = ((down_z, 1, 3), (up_z, 2, 0))
+    add(0, far, one(far_own), inner, inner, to_x=far_target)
+    add(0, down_y, inner, one(1), inner, to_y=3)
+    add(0, up_y, inner, one(2), inner, to_y=0)
+    for device, at, to in ends:
+        add(0, device, inner, inner, one(at), to_z=to)
+    add(0, sibling, one(shared), inner, inner, to_x=sibling_target)
+    add(1, down_y, one(far_cell), one(1), inner, to_y=3)
+    add(1, up_y, one(far_cell), one(2), inner, to_y=0)
+    for edge in (0, 3):
+        for device, at, to in ends:
+            add(1, device, inner, one(edge), one(at), to_z=to)
+    for device, at, to in ends:
+        add(1, device, one(far_cell), inner, one(at), to_z=to)
+    for edge in (0, 3):
+        add(1, sibling, one(shared), one(edge), inner, to_x=sibling_target)
+    for edge in (0, 3):
+        for device, at, to in ends:
+            add(2, device, one(far_cell), one(edge), one(at), to_z=to)
+    for edge in (0, 3):
+        add(3, sibling, one(shared), whole, one(edge), to_x=sibling_target)
+    return plan, (sibling, far, down_y, up_y, down_z, up_z)
+
+
+HALO_COPIES = 22
+
+
 def own_body(
-    feat_ref, pos_ref, neigh_ref, counts_ref, rbf_ref, radial_ref, mix_ref,
-    acc_ref, relt_ref, pair_ref, slope_hbm,
-    block_ref, pos8_ref, cells_ref, within_ref, rad_ref, drad_ref, slope_ref, sem,
+    feat_ref, pos_ref, neigh_ref, counts_ref, order_ref, rbf_ref, radial_ref, mix_ref,
+    acc_ref, relt_ref, pair_ref, table_ref, slope_hbm,
+    block_ref, pos8_ref, cells_ref, within_ref, rad_ref, drad_ref, slope_ref, sem, send_sem, recv_sem,
 ):
-    fill_blocks(block_ref, mix_ref)
+    plan, devices = halo_copies(table_ref, send_sem, recv_sem)
+    barrier = pltpu.get_barrier_semaphore()
+    for device in devices:
+        pl.semaphore_signal(barrier, inc=1, device_id=device, device_id_type=MESH_ID)
     pos8_ref[...] = jnp.zeros(pos8_ref.shape, F32)
     pos8_ref[0:3, :] = pos_ref[...]
     parts = split3(pos8_ref[...])
+    listed = column_of(order_ref[...].astype(F32)) == iota((ATOMS, ATOMS), 1).astype(F32)
+    listed = onehot_of(listed)
+    box = (2, 2, 2, 8)
+    for start in range(0, FEAT, 2 * C):
+        lanes = slice(start, min(start + 2 * C, FEAT))
+        value = dot(listed, feat_ref[:, lanes])
+        table_ref[1:3, 1:3, 1:3, :, lanes] = value.reshape(box + (value.shape[1],)).astype(BF16)
+    stacked = [part.astype(F32) for part in parts] + [jnp.zeros((C - 24, ATOMS), F32)]
+    value = dot_nt(listed, jnp.concatenate(stacked, axis=0).astype(BF16))
+    table_ref[1:3, 1:3, 1:3, :, FEAT:] = value.reshape(box + (C,)).astype(BF16)
+    pl.semaphore_wait(barrier, len(devices))
+    for copy in plan[0]:
+        copy.start()
+    fill_blocks(block_ref, mix_ref)
     cells, within = neighbour_parts(neigh_ref)
     cells_ref[...] = cells
     within_ref[...] = within
@@ -164,11 +245,37 @@
         edge_forward(onehot, feat_ref, rad_ref, drad_ref, block_ref, mix_ref, put_message, put_slope)
         copy_out(chunk).start()
 
+        @pl.when(chunk == 0)
+        def _():
+            for at in (0, 1, 2):
+                plan[0][at].wait_recv()
+            for copy in plan[1]:
+                copy.start()
+
+        @pl.when(chunk == 1)
+        def _():
+            for at in (0, 1):
+                plan[1][at].wait_recv()
+            for copy in plan[2]:
+                copy.start()
+
+        @pl.when(chunk == 2)
+        def _():
+            for copy in (plan[0][3], plan[0][4]) + tuple(plan[1][2:6]):
+                copy.wait_recv()
+            for copy in plan[3]:
+                copy.start()
+
+    for copy in [plan[0][5]] + plan[1][6:] + plan[2] + plan[3]:
+        copy.wait_recv()
+    for items in plan:
+        for copy in items:
+            copy.wait_send()
     for chunk in range(OWN_CHUNKS):
         copy_out(chunk).wait()
 
 
-def own_edges(feat, pos, neigh, counts, rbf, radial, mix):
+def own_edges(feat, pos, neigh, counts, order, rbf, radial, mix):
     vmem = pl.BlockSpec(memory_space=pltpu.VMEM)
     edges = ATOMS * HALF
     return pl.pallas_call(
@@ -177,10 +284,11 @@
             jax.ShapeDtypeStruct((ATOMS, FEAT), F32),
             jax.ShapeDtypeStruct((8, edges), F32),
             jax.ShapeDtypeStruct((edges, ATOMS), BF16),
+            jax.ShapeDtypeStruct((4, 4, 4, 8, WIDE), BF16),
             jax.ShapeDtypeStruct((edges, FEAT), BF16),
         ),
-        in_specs=[vmem] * 7,
-        out_specs=(vmem, vmem, vmem, pl.BlockSpec(memory_space=pl.ANY)),
+        in_specs=[vmem] * 8,
+        out_specs=(vmem, vmem, vmem, vmem, pl.BlockSpec(memory_space=pl.ANY)),
         scratch_shapes=[
             pltpu.VMEM((len(BLOCKS), 2 * C, 2 * C), BF16),
             pltpu.VMEM((8, ATOMS), F32),
@@ -190,30 +298,30 @@
             pltpu.VMEM((OWN_ROWS, DEGREES * C), BF16),
             pltpu.VMEM((edges, FEAT), BF16),
             pltpu.SemaphoreType.DMA((OWN_CHUNKS,)),
+            pltpu.SemaphoreType.DMA((HALO_COPIES,)),
+            pltpu.SemaphoreType.DMA((HALO_COPIES,)),
         ],
-        compiler_params=pltpu.CompilerParams(vmem_limit_bytes=VMEM_LIMIT),
+        compiler_params=pltpu.CompilerParams(vmem_limit_bytes=VMEM_LIMIT, collective_id=0, has_side_effects=True),
         cost_estimate=pl.CostEstimate(flops=8_000_000_000, bytes_accessed=10_000_000, transcendentals=600_000),
         name="own_edges",
-    )(feat, pos, neigh, counts, rbf, radial, mix)
+    )(feat, pos, neigh, counts, order, rbf, radial, mix)
 
 
 def ghost_body(
-    feat_ref, pos_ref, gpos_ref, neigh_ref, counts_ref, rbf_ref, radial_ref, mix_ref, out_ref,
-    energy_ref, norm_ref, acc_own_ref, relt_ref, pair_ref, slope_hbm, table_hbm,
-    new_ref, energies_ref, grad_own_ref, grad_ghost_ref,
-    block_ref, oblock_ref, pos8_ref, gpos8_ref, cells_ref, within_ref, rad_ref, drad_ref,
-    slope_ref, gslope_ref, table_ref, acc_ref, grelt_ref, gslot_ref, gatom_ref, updated_ref, gsum_ref, sem,
+    feat_ref, pos_ref, neigh_ref, counts_ref, rbf_ref, radial_ref, mix_ref, out_ref,
+    energy_ref, norm_ref, acc_own_ref, relt_ref, pair_ref, table_ref, slope_hbm,
+    new_ref, energies_ref, grad_own_ref, tiles_ref,
+    block_ref, oblock_ref, pos8_ref, cells_ref, within_ref, rad_ref, drad_ref,
+    slope_ref, gslope_ref, acc_ref, grelt_ref, gslot_ref, gatom_ref, gsum_ref, sem,
 ):
-    load_table = pltpu.make_async_copy(table_hbm, table_ref, sem.at[0])
-    load_slope = pltpu.make_async_copy(slope_hbm, slope_ref, sem.at[1])
-    load_table.start()
+    load_slope = pltpu.make_async_copy(slope_hbm, slope_ref, sem)
     load_slope.start()
     fill_blocks(block_ref, mix_ref)
     fill_blocks(oblock_ref, out_ref)
-    for target, source in ((pos8_ref, pos_ref), (gpos8_ref, gpos_ref)):
-        target[...] = jnp.zeros(target.shape, F32)
-        target[0:3, :] = source[...]
-    parts, gparts = split3(pos8_ref[...]), split3(gpos8_ref[...])
+    pos8_ref[...] = jnp.zeros(pos8_ref.shape, F32)
+    pos8_ref[0:3, :] = pos_ref[...]
+    stacked = [part.astype(F32) for part in split3(pos8_ref[...])] + [jnp.zeros((C - 24, ATOMS), F32)]
+    stacked = jnp.concatenate(stacked, axis=0).astype(BF16)
     cells, within = neighbour_parts(neigh_ref)
     cells_ref[...] = cells
     within_ref[...] = within
@@ -226,7 +334,9 @@
     total = jnp.sum(live_row).astype(jnp.int32)
     chunks = (total + GHOST_ROWS - 1) // GHOST_ROWS
     acc_ref[...] = acc_own_ref[...]
-    load_table.wait()
+
+    def whole(gathered):
+        return gathered + (pltpu.roll(gathered, C - 8, 1) + pltpu.roll(gathered, C - 16, 1))
 
     def spread_of(chunk):
         place = (iota((ATOMS, GHOST_ROWS), 1) + chunk * GHOST_ROWS).astype(F32)
@@ -243,10 +353,26 @@
         named = dot(spread, cells_ref[...]) * 8.0 + dot(spread, within_ref[...])
         named = select_lane(named, (place - begin).astype(jnp.int32) + HALF, 0.0)
         onehot = onehot_of(iota((GHOST_ROWS, GHOST), 1).astype(F32) == named - float(ATOMS))
-        gslot_ref[rows, :] = onehot
+        row = named.astype(jnp.int32) - ATOMS
+        inside = row >= 0
+        row = jnp.maximum(row, 0)
+        spots = [(row >> shift) & 3 for shift in (7, 5, 3)]
+        moves = [jnp.where(spot == 0, -1, jnp.where(spot == 3, 1, 0)) for spot in spots]
+        toward = moves[0] * 9 + moves[1] * 3 + moves[2] + 13
+        slot = row & 7
+        for at, spot in enumerate(spots):
+            slot = slot + (((spot + 1) & 1) << (5 - at))
+        place = jnp.where(inside, toward * ATOMS + slot, -1)
+        gslot_ref[rows, :] = onehot_of(iota((GHOST_ROWS, TILES * C), 1) == place)
         gatom_ref[rows, :] = spread
-        grelt_ref[:, rows] = gather_places(onehot, gparts, True) - gather_places(spread, parts, True)
-        rel = gather_places(onehot, gparts, False) - gather_places(spread, parts, False)
+        lane = iota((GHOST_ROWS, C), 1)
+        last = dot(onehot, table_ref[:, FEAT - C :])
+        image = jnp.zeros((GHOST_ROWS, C), F32)
+        for at, move in enumerate(moves):
+            image = jnp.where(lane == at, move.astype(F32) * 4.0, image)
+        rel = (whole(last[:, C:]) + image) - whole(dot_nt(spread, stacked))
+        rel = jnp.where(jnp.logical_and(lane < 3, inside), rel, 0.0)
+        grelt_ref[:, rows] = rel.T[:8]
         radial_of(rel, rbf_ref, radial_ref, rad_ref, drad_ref)
 
         def put_message(lanes, value):
@@ -255,7 +381,8 @@
         def put_slope(lanes, value):
             gslope_ref[rows, lanes] = value
 
-        edge_forward(onehot, table_ref, rad_ref, drad_ref, block_ref, mix_ref, put_message, put_slope)
+        last = last[:, :C].astype(BF16)
+        edge_forward(onehot, table_ref, rad_ref, drad_ref, block_ref, mix_ref, put_message, put_slope, last)
 
     energy = None
     for pair in PAIRS:
@@ -308,9 +435,11 @@
         return own_total - dot(pull, gatom_ref[rows, :]), ghost_total + dot(pull, gslot_ref[rows, :])
 
     own_total = lax.fori_loop(0, OWN_CHUNKS, own_step, jnp.zeros((16, ATOMS), F32))
-    own_total, ghost_total = lax.fori_loop(0, chunks, ghost_step, (own_total, jnp.zeros((16, GHOST), F32)))
+    own_total, ghost_total = lax.fori_loop(0, chunks, ghost_step, (own_total, jnp.zeros((16, TILES * C), F32)))
     grad_own_ref[...] = own_total[:8] + own_total[8:]
-    grad_ghost_ref[...] = ghost_total[:8] + ghost_total[8:]
+    for tile in range(TILES):
+        lanes = slice(tile * C, (tile + 1) * C)
+        tiles_ref[tile] = ghost_total[:8, lanes] + ghost_total[8:, lanes]
 
 
 def ghost_edges(*operands):
@@ -323,29 +452,26 @@
             jax.ShapeDtypeStruct((ATOMS, FEAT), BF16),
             jax.ShapeDtypeStruct((1, ATOMS), F32),
             jax.ShapeDtypeStruct((8, ATOMS), F32),
-            jax.ShapeDtypeStruct((8, GHOST), F32),
+            jax.ShapeDtypeStruct((TILES, 8, C), F32),
         ),
-        in_specs=[vmem] * 14 + [hbm] * 2,
+        in_specs=[vmem] * 14 + [hbm],
         out_specs=(vmem,) * 4,
         scratch_shapes=[
             pltpu.VMEM((len(BLOCKS), 2 * C, 2 * C), BF16),
             pltpu.VMEM((len(BLOCKS), 2 * C, 2 * C), BF16),
             pltpu.VMEM((8, ATOMS), F32),
-            pltpu.VMEM((8, GHOST), F32),
             pltpu.VMEM((ATOMS, SLOTS), BF16),
             pltpu.VMEM((ATOMS, SLOTS), BF16),
             pltpu.VMEM((GHOST_ROWS, DEGREES * C), BF16),
             pltpu.VMEM((GHOST_ROWS, DEGREES * C), BF16),
             pltpu.VMEM((own, FEAT), BF16),
             pltpu.VMEM((GHOST_EDGES, FEAT), BF16),
-            pltpu.VMEM((GHOST, FEAT), BF16),
             pltpu.VMEM((ATOMS, FEAT), F32),
             pltpu.VMEM((8, GHOST_EDGES), F32),
-            pltpu.VMEM((GHOST_EDGES, GHOST), BF16),
+            pltpu.VMEM((GHOST_EDGES, TILES * C), BF16),
             pltpu.VMEM((GHOST_EDGES, ATOMS), BF16),
-            pltpu.VMEM((8, 128), F32),
             pltpu.VMEM((ATOMS, FEAT), BF16),
-            pltpu.SemaphoreType.DMA((2,)),
+            pltpu.SemaphoreType.DMA,
         ],
         compiler_params=pltpu.CompilerParams(vmem_limit_bytes=VMEM_LIMIT),
         cost_estimate=pl.CostEstimate(flops=10_000_000_000, bytes_accessed=14_000_000, transcendentals=400_000),
@@ -353,38 +479,54 @@
     )(*operands)
 
 
-def padded(shard, sides, width):
-    for axis, dim in sides:
-        peers, length = (lax.axis_size(axis), shard.shape[dim])
-        up = [(i, (i + 1) % peers) for i in range(peers)]
-        down = [(j, i) for i, j in up]
-        last = lax.slice_in_dim(shard, length - width, length, axis=dim)
-        first = lax.slice_in_dim(shard, 0, width, axis=dim)
-        before = lax.ppermute(last, axis, up)
-        after = lax.ppermute(first, axis, down)
-        shard = jnp.concatenate([before, shard, after], axis=dim)
-    return shard
-
-
-def image_shifts():
-    side = np.array([-4.0, 0.0, 0.0, 4.0], np.float32)
-    grid = np.meshgrid(side, side, side, indexing="ij")
-    return jnp.asarray(np.stack(grid), F32)
-
-
-def fold_axis(received, axis):
-    middle = lax.slice_in_dim(received, 2, 4, axis=axis)
-    lower = lax.slice_in_dim(received, 0, 1, axis=axis)
-    upper = lax.slice_in_dim(received, 5, 6, axis=axis)
-    return middle + jnp.concatenate([lower, upper], axis=axis)
-
-
-def domain(feat, pos, ghost_feat, ghost_places, neigh, counts, rbf, radial, mix, out, energy, norm):
-    acc, relt, pairs, slopes = own_edges(feat, pos, neigh, counts, rbf, radial, mix)
-    return ghost_edges(
-        feat, pos, ghost_places, neigh, counts, rbf, radial, mix, out, energy, norm,
-        acc, relt, pairs, slopes, ghost_feat,
-    )
+def return_body(tiles_ref, grad_own_ref, order_ref, forces_ref, landed_ref, send_sem, recv_sem):
+    here = [lax.axis_index(axis) for axis in ("gx", "gy", "gz")]
+    sizes = [lax.axis_size(axis) for axis in ("gx", "gy", "gz")]
+    barrier = pltpu.get_barrier_semaphore()
+    others = [at for at in range(DIRECTIONS) if at != DIRECTIONS // 2]
+    copies = []
+    for at in others:
+        moves = (at // 9 - 1, at // 3 % 3 - 1, at % 3 - 1)
+        device = tuple(lax.rem(h + n + m, n) for h, n, m in zip(here, sizes, moves))
+        pl.semaphore_signal(barrier, inc=1, device_id=device, device_id_type=MESH_ID)
+        copies.append(
+            pltpu.make_async_remote_copy(
+                src_ref=tiles_ref.at[at // 2], dst_ref=landed_ref.at[at],
+                send_sem=send_sem.at[at], recv_sem=recv_sem.at[at],
+                device_id=device, device_id_type=MESH_ID,
+            )
+        )
+    pl.semaphore_wait(barrier, len(others))
+    for copy in copies:
+        copy.start()
+    listed = column_of(order_ref[...].astype(F32)) == iota((ATOMS, ATOMS), 1).astype(F32)
+    listed = onehot_of(listed)
+    for copy in copies:
+        copy.wait_recv()
+    even = sum(landed_ref[at] for at in others if at % 2 == 0)
+    odd = sum(landed_ref[at] for at in others if at % 2 == 1)
+    total = (even + pltpu.roll(odd, ATOMS, 1))[:, :ATOMS]
+    back = sum(dot(part, listed) for part in split3(total)[::-1])
+    forces_ref[...] = -(grad_own_ref[...] + back)[:3]
+    for copy in copies:
+        copy.wait_send()
+
+
+def return_forces(tiles, grad_own, order):
+    vmem = pl.BlockSpec(memory_space=pltpu.VMEM)
+    return pl.pallas_call(
+        return_body,
+        out_shape=jax.ShapeDtypeStruct((3, ATOMS), F32),
+        in_specs=[vmem] * 3,
+        out_specs=vmem,
+        scratch_shapes=[
+            pltpu.VMEM((DIRECTIONS, 8, C), F32),
+            pltpu.SemaphoreType.DMA((DIRECTIONS,)),
+            pltpu.SemaphoreType.DMA((DIRECTIONS,)),
+        ],
+        compiler_params=pltpu.CompilerParams(collective_id=1, has_side_effects=True),
+        name="return_forces",
+    )(tiles, grad_own, order)
 
 
 def local(
@@ -393,23 +535,15 @@
 ):
     feat = features.reshape(ATOMS, FEAT)
     pos = positions.reshape(3, ATOMS)
-    order = cell_atoms.reshape(ATOMS)
-    onehot = order[:, None] == jnp.arange(ATOMS, dtype=jnp.int32)[None, :]
-    cell_feat = jnp.dot(onehot.astype(BF16), feat, preferred_element_type=F32).astype(BF16)
-    cell_places = jnp.sum(jnp.where(onehot[None], pos[:, None, :], 0.0), axis=2)
-    ghost_feat = padded(cell_feat.reshape(2, 2, 2, 8, FEAT), (("gx", 0), ("gy", 1), ("gz", 2)), 1)
-    ghost_places = padded(cell_places.reshape(3, 2, 2, 2, 8), (("gx", 1), ("gy", 2), ("gz", 3)), 1)
-    ghost_places = (ghost_places + image_shifts()[..., None]).reshape(3, -1)
-    updated, energies, grad_own, grad_ghost = domain(
-        feat, pos, ghost_feat.reshape(GHOST, FEAT), ghost_places,
-        neighbours.reshape(ATOMS, SLOTS), counts.reshape(1, ATOMS),
-        rbf_weight, radial_weight, mix_weight, out_weight, energy_weight.reshape(1, C), norm_weight,
+    neigh = neighbours.reshape(ATOMS, SLOTS)
+    live = counts.reshape(1, ATOMS)
+    order = cell_atoms.reshape(1, ATOMS)
+    acc, relt, pairs, table, slopes = own_edges(feat, pos, neigh, live, order, rbf_weight, radial_weight, mix_weight)
+    updated, energies, grad_own, tiles = ghost_edges(
+        feat, pos, neigh, live, rbf_weight, radial_weight, mix_weight, out_weight,
+        energy_weight.reshape(1, C), norm_weight, acc, relt, pairs, table.reshape(GHOST, WIDE), slopes,
     )
-    grad_blocks = grad_ghost[:3].reshape(3, 4, 4, 4, 8)
-    returned = padded(grad_blocks, (("gx", 1), ("gy", 2), ("gz", 3)), 1)
-    cell_grad = fold_axis(fold_axis(fold_axis(returned, 1), 2), 3).reshape(3, ATOMS)
-    back_own = jnp.sum(jnp.where(onehot[None], cell_grad[:, :, None], 0.0), axis=1)
-    forces = -(grad_own[:3] + back_own)
+    forces = return_forces(tiles, grad_own, order)
     return (
         updated.reshape(features.shape),
         energies.reshape(counts.shape),

time: 144 us -> 90.6 us (0.63)
  starting transfers between devices: 78.6 us -> 0 us
  Pallas kernels: 42.7 us -> 80.4 us
  waiting for transfers between devices: 10.7 us -> 0 us
  local copies, waits for them, and re-layouts: 3.5 us -> 8.98 us
  other arithmetic: 5.34 us -> 0 us
    ppermute x18 -> x0, starting transfers between devices: 78.6 us -> none  [the longest x9 46.8 us: padded(): after = lax.ppermute(first, axis, down)]
    pallas_call x1, Pallas kernels: 21.6 us -> 43.6 us  [own_edges(): pl.pallas_call(own_body, out_shape=(jax.ShapeDtypeStruct((ATOMS, FEAT), F...]
    pallas_call x0 -> x1, Pallas kernels: none -> 16.1 us  [return_forces(): pl.pallas_call(return_body, out_shape=jax.ShapeDtypeStruct((3, ATOMS), F3...]
    ppermute x18 -> x0, waiting for transfers between devices: 10.7 us -> none  [the longest x9 9.08 us: padded(): after = lax.ppermute(first, axis, down)]
    unnamed x29, local copies, waits for them, and re-layouts: 1.44 us -> 8.98 us
    concatenate x5 -> x0, other arithmetic: 4.07 us -> none  [padded(): shard = jnp.concatenate([before, shard, after], axis=dim)]
    slice x11 -> x0, local copies, waits for them, and re-layouts: 1.56 us -> none  [the longest x6 1.53 us: padded(): last = lax.slice_in_dim(shard, length - width, length, axis=dim)]
  transfers between devices with their start and end apart: 18 -> 0, of which waited for: 6 -> 0; matrix products, arithmetic and copies ran while one was open for 2% -> 0% of each run, Pallas kernels for 15% -> 0%
where the time goes in v2:
time: 90.6 us; the launch traced here: 90.1 us
  Pallas kernels  80.4 us (89%)
  local copies, waits for them, and re-layouts  8.98 us (10%)
    pallas_call x1, Pallas kernels, own_edges(): pl.pallas_call(own_body, out_shape=(jax.ShapeDtypeStruct((ATOMS, FEAT), F...  43.6 us
    pallas_call x1, Pallas kernels, ghost_edges(): pl.pallas_call(ghost_body, out_shape=(jax.ShapeDtypeStruct((ATOMS, FEAT),...  20.7 us
    pallas_call x1, Pallas kernels, return_forces(): pl.pallas_call(return_body, out_shape=jax.ShapeDtypeStruct((3, ATOMS), F3...  16.1 us
    unnamed x29, local copies, waits for them, and re-layouts  8.98 us

profile of v2, /device:TPU:1, one launch (start us, length us, event | category | flops | bytes accessed | tf_op | source)
XLA Modules:
  0.0 90.1 jit_solution(16059051651732981688)
XLA Ops:
  0.6 0.7 copy.18
  1.3 0.8 copy.14
  2.1 0.0 copy-start.2
  2.1 0.7 copy-done.2
  2.8 0.0 copy-start.3
  2.8 1.0 %copy-done.3 = bf16[1,1,1,64,3200]{4,3,2,1,0:T(8,128)(2,1)S(1)} copy-done((bf16[1,1,1,64,3200]{4,3,2,1,0:T(8,128)(2,1)S(1)}, bf16[1,1,1,64,3200]{4,3,2,1,0:T(8,128)(2,1)}, u32[]{:S(2)}) %copy-start.3) | copy-done | bytes 409624
  3.8 0.0 copy-start.4
  3.8 0.9 %copy-done.4 = bf16[128,640]{1,0:T(8,128)(2,1)S(1)} copy-done((bf16[128,640]{1,0:T(8,128)(2,1)S(1)}, bf16[128,640]{1,0:T(8,128)(2,1)}, u32[]{:S(2)}) %copy-start.4) | copy-done | bytes 163864
  4.7 0.0 copy-start.6
  4.7 0.9 %copy-done.6 = bf16[5,128,128]{2,1,0:T(8,128)(2,1)S(1)} copy-done((bf16[5,128,128]{2,1,0:T(8,128)(2,1)S(1)}, bf16[5,128,128]{2,1,0:T(8,128)(2,1)}, u32[]{:S(2)}) %copy-start.6) | copy-done | bytes 163864
  5.6 0.0 copy-start.9
  5.6 0.9 %copy-done.9 = bf16[512,128]{1,0:T(8,128)(2,1)S(1)} copy-done((bf16[512,128]{1,0:T(8,128)(2,1)S(1)}, bf16[512,128]{1,0:T(8,128)(2,1)}, u32[]{:S(2)}) %copy-start.9) | copy-done | bytes 131096
  6.5 0.0 copy-start.11
  6.5 0.7 copy-done.11
  7.2 0.0 copy-start.5
  7.2 0.0 copy-start.7
  7.2 0.0 copy-start.8
  7.2 0.0 copy-start.10
  7.2 0.0 copy-start.12
  7.2 43.6 %own_edges.1 = (f32[64,3200]{1,0:T(8,128)S(1)}, f32[8,1024]{1,0:T(8,128)S(1)}, bf16[1024,64]{1,0:T(8,128)(2,1)S(1)}, bf16[4,4,4,8,3328]{4,3,2,1,0:T(8,128)(2,1)}, bf16[1024,3200]{1,0:T(8,128)(2,1)}) custom-call(bf16[64,3200]{1,0:T(8,128)(2,1)S(1)} %bitcast.18, f32[3,64]{1,0:T(4,128)S(1)} %bitcast.14, s32[64,32]{1,0:T(8,128)S(1)} %bitcast.12, ...), custom_call_target="tpu_custom_call" | custom-call | flops 8000000000 | bytes 10000000 | tf_op jit(solution)/shard_map/own_edges/pallas_call | solution.py:281
  50.8 0.0 copy-done.5
  50.8 0.0 copy-done.7
  50.8 0.0 copy-done.8
  50.8 0.0 copy-done.10
  50.8 0.0 copy-done.12
  50.9 20.7 %ghost_edges.1 = (bf16[64,3200]{1,0:T(8,128)(2,1)}, f32[1,64]{1,0:T(1,128)}, f32[8,64]{1,0:T(8,128)S(1)}, f32[14,8,128]{2,1,0:T(8,128)S(1)}) custom-call(bf16[64,3200]{1,0:T(8,128)(2,1)S(1)} %bitcast.19, f32[3,64]{1,0:T(4,128)S(1)} %bitcast.15, s32[64,32]{1,0:T(8,128)S(1)} %bitcast.13, s32[1,64]{1,0:T(1,128)S(1)} %bitcast.21, ...), custom_call_target="tpu_custom_call" | custom-call | flops 10000000000 | bytes 14000000 | tf_op jit(solution)/shard_map/ghost_edges/pallas_call | solution.py:449
  71.5 0.0 copy-start
  71.5 0.6 copy-done
  72.2 0.0 copy-start.1
  72.2 0.6 copy-done.1
  72.7 16.1 %return_forces.1 = f32[3,64]{1,0:T(4,128)} custom-call(f32[14,8,128]{2,1,0:T(8,128)} %copy-done, f32[8,64]{1,0:T(8,128)} %copy-done.1, s32[1,64]{1,0:T(1,128)} %bitcast.16), custom_call_target="tpu_custom_call" | custom-call | tf_op jit(solution)/shard_map/return_forces/pallas_call | solution.py:517
  88.9 1.2 %copy.15 = f32[1,1,1,3,64]{4,2,3,1,0:T(1,128)} copy(f32[1,1,1,3,64]{4,3,2,1,0:T(4,128)} %bitcast.23) | data formatting | bytes 1536
Async XLA Ops:
  2.1 0.7 copy-start.2
  2.8 1.0 %copy-start.3 = (bf16[1,1,1,64,3200]{4,3,2,1,0:T(8,128)(2,1)S(1)}, bf16[1,1,1,64,3200]{4,3,2,1,0:T(8,128)(2,1)}, u32[]{:S(2)}) copy-start(bf16[1,1,1,64,3200]{4,3,2,1,0:T(8,128)(2,1)} %param.11) | copy-start | bytes 1228804
  3.8 0.9 %copy-start.4 = (bf16[128,640]{1,0:T(8,128)(2,1)S(1)}, bf16[128,640]{1,0:T(8,128)(2,1)}, u32[]{:S(2)}) copy-start(bf16[128,640]{1,0:T(8,128)(2,1)} %radial_ref.3) | copy-start | bytes 491524
  4.7 0.9 %copy-start.6 = (bf16[5,128,128]{2,1,0:T(8,128)(2,1)S(1)}, bf16[5,128,128]{2,1,0:T(8,128)(2,1)}, u32[]{:S(2)}) copy-start(bf16[5,128,128]{2,1,0:T(8,128)(2,1)} %mix_ref.3) | copy-start | bytes 491524
  5.6 0.9 %copy-start.9 = (bf16[512,128]{1,0:T(8,128)(2,1)S(1)}, bf16[512,128]{1,0:T(8,128)(2,1)}, u32[]{:S(2)}) copy-start(bf16[512,128]{1,0:T(8,128)(2,1)} %rbf_ref.3) | copy-start | bytes 393220
  6.5 0.7 copy-start.11
  7.2 43.6 %copy-start.5 = (bf16[128,640]{1,0:T(8,128)(2,1)S(1)}, bf16[128,640]{1,0:T(8,128)(2,1)}, u32[]{:S(2)}) copy-start(bf16[128,640]{1,0:T(8,128)(2,1)} %radial_ref.3) | copy-start | bytes 491524
  7.2 43.6 %copy-start.7 = (bf16[5,128,128]{2,1,0:T(8,128)(2,1)S(1)}, bf16[5,128,128]{2,1,0:T(8,128)(2,1)}, u32[]{:S(2)}) copy-start(bf16[5,128,128]{2,1,0:T(8,128)(2,1)} %mix_ref.3) | copy-start | bytes 491524
  7.2 43.7 %copy-start.8 = (bf16[5,128,128]{2,1,0:T(8,128)(2,1)S(1)}, bf16[5,128,128]{2,1,0:T(8,128)(2,1)}, u32[]{:S(2)}) copy-start(bf16[5,128,128]{2,1,0:T(8,128)(2,1)} %out_ref.1) | copy-start | bytes 491524
  7.2 43.7 %copy-start.10 = (f32[4,128]{1,0:T(4,128)S(1)}, f32[4,128]{1,0:T(4,128)}, u32[]{:S(2)}) copy-start(f32[4,128]{1,0:T(4,128)} %norm_ref.1) | copy-start | bytes 6148
  7.2 43.7 %copy-start.12 = (f32[128]{0:T(128)S(1)}, f32[128]{0:T(128)}, u32[]{:S(2)}) copy-start(f32[128]{0:T(128)} %param.20) | copy-start | bytes 1540
  71.5 0.6 copy-start
  72.2 0.6 copy-start.1

commit v3 on v2

--- a/solution.py
+++ b/solution.py
@@ -89,25 +89,30 @@
     drad_ref[...] = dot(dhidden, radial_ref[...]).astype(BF16)
 
 
-def edge_forward(onehot, table_ref, rad_ref, drad_ref, block_ref, mix_ref, put_message, put_slope, last=None):
+def edge_forward(onehot, table_ref, rad_ref, drad_ref, block_ref, mix_ref, lhs_ref, message_ref, put_slope, last=None, middle=None):
     rows = onehot.shape[0]
-    gate = lean = None
     for pair in PAIRS:
         lanes = slice(pair[0] * C, (pair[-1] + 1) * C)
         if len(pair) == 1 and last is not None:
             near = last
         else:
             near = dot(onehot, table_ref[:, lanes]).astype(BF16)
-        cuts = [slice(DEGREE[k] * C, (DEGREE[k] + 1) * C) for k in pair]
-        rad = jnp.concatenate([rad_ref[:, cut] for cut in cuts], axis=1)
-        drad = jnp.concatenate([drad_ref[:, cut] for cut in cuts], axis=1)
-        both = jnp.concatenate([near * rad, near * drad], axis=0)
-        both = dot(both, pair_weight(pair, block_ref, mix_ref))
+        for at, k in enumerate(pair):
+            cut = slice(DEGREE[k] * C, (DEGREE[k] + 1) * C)
+            half = near[:, at * C : (at + 1) * C]
+            lhs_ref[:rows, k * C : (k + 1) * C] = half * rad_ref[:, cut]
+            lhs_ref[rows:, k * C : (k + 1) * C] = half * drad_ref[:, cut]
+    if middle is not None:
+        middle()
+    gate = lean = None
+    for pair in PAIRS:
+        lanes = slice(pair[0] * C, (pair[-1] + 1) * C)
+        both = dot(lhs_ref[:, lanes], pair_weight(pair, block_ref, mix_ref))
         mixed, dmixed = both[:rows], both[rows:]
         if gate is None:
             gate = jax.nn.sigmoid(mixed[:, :C])
             lean = (1.0 - gate) * dmixed[:, :C]
-        put_message(lanes, (mixed * wide(gate, pair)).astype(BF16))
+        message_ref[:, lanes] = (mixed * wide(gate, pair)).astype(BF16)
         put_slope(lanes, ((dmixed + mixed * wide(lean, pair)) * wide(gate, pair)).astype(BF16))
 
 
@@ -137,59 +142,99 @@
     far_target, sibling_target = 3 - 3 * odd, 3 * odd
     one = lambda at: pl.ds(at, 1)
     inner, whole = pl.ds(1, 2), pl.ds(0, 4)
-    plan = ([], [], [], [])
-
-    def add(stage, device, x, y, z, to_x=None, to_y=None, to_z=None):
-        at = sum(len(items) for items in plan)
+    plan = {}
+
+    def add(name, device, x, y, z, to_x=None, to_y=None, to_z=None):
+        at = len(plan)
         source = table_ref.at[x, y, z]
         target = table_ref.at[
             x if to_x is None else one(to_x), y if to_y is None else one(to_y), z if to_z is None else one(to_z)
         ]
-        plan[stage].append(
-            pltpu.make_async_remote_copy(
-                src_ref=source, dst_ref=target, send_sem=send_sem.at[at], recv_sem=recv_sem.at[at],
-                device_id=device, device_id_type=MESH_ID,
-            )
+        plan[name] = pltpu.make_async_remote_copy(
+            src_ref=source, dst_ref=target, send_sem=send_sem.at[at], recv_sem=recv_sem.at[at],
+            device_id=device, device_id_type=MESH_ID,
         )
 
-    ends = ((down_z, 1, 3), (up_z, 2, 0))
-    add(0, far, one(far_own), inner, inner, to_x=far_target)
-    add(0, down_y, inner, one(1), inner, to_y=3)
-    add(0, up_y, inner, one(2), inner, to_y=0)
-    for device, at, to in ends:
-        add(0, device, inner, inner, one(at), to_z=to)
-    add(0, sibling, one(shared), inner, inner, to_x=sibling_target)
-    add(1, down_y, one(far_cell), one(1), inner, to_y=3)
-    add(1, up_y, one(far_cell), one(2), inner, to_y=0)
+    add("far", far, one(far_own), inner, inner, to_x=far_target)
+    for x, kind in ((inner, "own"), (one(far_cell), "far")):
+        add(kind + "_yd_a", down_y, x, one(1), one(1), to_y=3)
+        add(kind + "_yu_a", up_y, x, one(2), one(2), to_y=0)
+        add(kind + "_zd_a", down_z, x, one(2), one(1), to_z=3)
+        add(kind + "_zu_a", up_z, x, one(1), one(2), to_z=0)
+        add(kind + "_yd_b", down_y, x, one(1), one(2), to_y=3)
+        add(kind + "_yu_b", up_y, x, one(2), one(1), to_y=0)
+        add(kind + "_zd_b", down_z, x, one(1), one(1), to_z=3)
+        add(kind + "_zu_b", up_z, x, one(2), one(2), to_z=0)
+        add(kind + "_zd_e", down_z, x, one(3), one(1), to_z=3)
+        add(kind + "_zu_e", up_z, x, one(0), one(2), to_z=0)
+        add(kind + "_yd_e", down_y, x, one(1), one(0), to_y=3)
+        add(kind + "_yu_e", up_y, x, one(2), one(3), to_y=0)
+    add("sib", sibling, one(shared), inner, inner, to_x=sibling_target)
     for edge in (0, 3):
-        for device, at, to in ends:
-            add(1, device, inner, one(edge), one(at), to_z=to)
-    for device, at, to in ends:
-        add(1, device, one(far_cell), inner, one(at), to_z=to)
-    for edge in (0, 3):
-        add(1, sibling, one(shared), one(edge), inner, to_x=sibling_target)
-    for edge in (0, 3):
-        for device, at, to in ends:
-            add(2, device, one(far_cell), one(edge), one(at), to_z=to)
-    for edge in (0, 3):
-        add(3, sibling, one(shared), whole, one(edge), to_x=sibling_target)
+        add("sib_y%d" % edge, sibling, one(shared), one(edge), inner, to_x=sibling_target)
+        add("sib_z%d" % edge, sibling, one(shared), inner, one(edge), to_x=sibling_target)
+        add("sib_e%d0" % edge, sibling, one(shared), one(edge), one(0), to_x=sibling_target)
+        add("sib_e%d3" % edge, sibling, one(shared), one(edge), one(3), to_x=sibling_target)
     return plan, (sibling, far, down_y, up_y, down_z, up_z)
 
 
-HALO_COPIES = 22
+def halo_steps(plan):
+    sides = ("_yd", "_yu", "_zd", "_zu")
+    names = lambda kind, piece: [kind + side + piece for side in sides]
+    steps = (
+        ([], ["far"] + names("own", "_a") + names("own", "_b") + ["sib"]),
+        (names("own", "_a"), names("own", "_e")),
+        (["far"], names("far", "_a") + names("far", "_b")),
+        (names("own", "_b"), ["sib_y0", "sib_y3", "sib_z0", "sib_z3"]),
+        (names("far", "_a"), names("far", "_e")),
+        (names("own", "_e"), ["sib_e00", "sib_e03", "sib_e30", "sib_e33"]),
+        (names("far", "_b") + names("far", "_e") + [name for name in plan if name.startswith("sib")], []),
+    )
+
+    def run(step):
+        for name in steps[step][0]:
+            plan[name].wait_recv()
+        for name in steps[step][1]:
+            plan[name].start()
+
+    return run
+
+
+HALO_COPIES = 34
+
+
+def load_all(sources, targets, sem):
+    copies = [pltpu.make_async_copy(a, b, sem.at[at]) for at, (a, b) in enumerate(zip(sources, targets))]
+    for copy in copies:
+        copy.start()
+    return copies
+
+
+def like(operands):
+    return [pltpu.VMEM(operand.shape, operand.dtype) for operand in operands] + [
+        pltpu.SemaphoreType.DMA((len(operands),))
+    ]
 
 
 def own_body(
-    feat_ref, pos_ref, neigh_ref, counts_ref, order_ref, rbf_ref, radial_ref, mix_ref,
-    acc_ref, relt_ref, pair_ref, table_ref, slope_hbm,
-    block_ref, pos8_ref, cells_ref, within_ref, rad_ref, drad_ref, slope_ref, sem, send_sem, recv_sem,
+    feat_hbm, pos_hbm, neigh_hbm, counts_hbm, order_hbm, rbf_hbm, radial_hbm, mix_hbm, out_hbm,
+    acc_ref, relt_ref, pair_ref, table_ref, block_ref, oblock_ref, slope_hbm,
+    feat_ref, pos_ref, neigh_ref, counts_ref, order_ref, rbf_ref, radial_ref, mix_ref, out_ref, load_sem,
+    pos8_ref, cells_ref, within_ref, rad_ref, drad_ref, lhs_ref, message_ref, slope_ref, sem, send_sem, recv_sem,
 ):
+    loads = load_all(
+        (feat_hbm, pos_hbm, neigh_hbm, counts_hbm, order_hbm, rbf_hbm, radial_hbm, mix_hbm, out_hbm),
+        (feat_ref, pos_ref, neigh_ref, counts_ref, order_ref, rbf_ref, radial_ref, mix_ref, out_ref),
+        load_sem,
+    )
     plan, devices = halo_copies(table_ref, send_sem, recv_sem)
     barrier = pltpu.get_barrier_semaphore()
     for device in devices:
         pl.semaphore_signal(barrier, inc=1, device_id=device, device_id_type=MESH_ID)
     pos8_ref[...] = jnp.zeros(pos8_ref.shape, F32)
-    pos8_ref[0:3, :] = pos_ref[...]
+    for at in (0, 1, 4):
+        loads[at].wait()
+    pos8_ref[0:3, :] = pos_ref[:, 0, :]
     parts = split3(pos8_ref[...])
     listed = column_of(order_ref[...].astype(F32)) == iota((ATOMS, ATOMS), 1).astype(F32)
     listed = onehot_of(listed)
@@ -201,16 +246,20 @@
     stacked = [part.astype(F32) for part in parts] + [jnp.zeros((C - 24, ATOMS), F32)]
     value = dot_nt(listed, jnp.concatenate(stacked, axis=0).astype(BF16))
     table_ref[1:3, 1:3, 1:3, :, FEAT:] = value.reshape(box + (C,)).astype(BF16)
+    for at in (7, 8):
+        loads[at].wait()
+    fill_blocks(block_ref, mix_ref)
+    fill_blocks(oblock_ref, out_ref)
+    advance = halo_steps(plan)
     pl.semaphore_wait(barrier, len(devices))
-    for copy in plan[0]:
-        copy.start()
-    fill_blocks(block_ref, mix_ref)
+    advance(0)
+    for at in (2, 3, 5, 6):
+        loads[at].wait()
     cells, within = neighbour_parts(neigh_ref)
     cells_ref[...] = cells
     within_ref[...] = within
     atoms = OWN_ROWS // HALF
     edge = iota((OWN_ROWS, 1), 0)
-    spread = onehot_of(edge // HALF == iota((OWN_ROWS, atoms), 1))
     gather = onehot_of(iota((atoms, OWN_ROWS), 1) // HALF == iota((atoms, OWN_ROWS), 0))
 
     def copy_out(chunk):
@@ -224,10 +273,11 @@
     def _(chunk):
         here = pl.ds(pl.multiple_of(chunk * atoms, atoms), atoms)
         rows = pl.ds(pl.multiple_of(chunk * OWN_ROWS, OWN_ROWS), OWN_ROWS)
-        named = dot(spread, cells_ref[here, :]) * 8.0 + dot(spread, within_ref[here, :])
-        named = select_lane(named, edge % HALF, 0.0)
         centre = chunk * atoms + edge // HALF
         lane = iota((OWN_ROWS, ATOMS), 1)
+        spread = onehot_of(lane == centre)
+        named = dot_nt(spread, cells_ref[...]) * 8.0 + dot_nt(spread, within_ref[...])
+        named = select_lane(named, edge % HALF, 0.0)
         live_count = jnp.sum(jnp.where(lane == centre, counts_ref[...].astype(F32), 0.0), axis=1, keepdims=True)
         hit = lane.astype(F32) == named
         edge_pair = jnp.where(hit, 1.0, jnp.where(lane == centre, -1.0, 0.0)).astype(BF16)
@@ -236,46 +286,35 @@
         radial_of(gather_places(edge_pair, parts, False), rbf_ref, radial_ref, rad_ref, drad_ref)
         onehot = onehot_of(jnp.logical_and(hit, (edge % HALF).astype(F32) < live_count))
 
-        def put_message(lanes, value):
-            acc_ref[here, lanes] = dot(gather, value)
-
         def put_slope(lanes, value):
             slope_ref[rows, lanes] = value
 
-        edge_forward(onehot, feat_ref, rad_ref, drad_ref, block_ref, mix_ref, put_message, put_slope)
+        def middle():
+            for at, step in ((1, 1), (3, 5)):
+                @pl.when(chunk == at)
+                def _():
+                    advance(step)
+
+        edge_forward(onehot, feat_ref, rad_ref, drad_ref, block_ref, mix_ref, lhs_ref, message_ref, put_slope, middle=middle)
+        for pair in PAIRS:
+            lanes = slice(pair[0] * C, (pair[-1] + 1) * C)
+            acc_ref[here, lanes] = dot(gather, message_ref[:, lanes])
         copy_out(chunk).start()
 
-        @pl.when(chunk == 0)
-        def _():
-            for at in (0, 1, 2):
-                plan[0][at].wait_recv()
-            for copy in plan[1]:
-                copy.start()
-
-        @pl.when(chunk == 1)
-        def _():
-            for at in (0, 1):
-                plan[1][at].wait_recv()
-            for copy in plan[2]:
-                copy.start()
-
-        @pl.when(chunk == 2)
-        def _():
-            for copy in (plan[0][3], plan[0][4]) + tuple(plan[1][2:6]):
-                copy.wait_recv()
-            for copy in plan[3]:
-                copy.start()
-
-    for copy in [plan[0][5]] + plan[1][6:] + plan[2] + plan[3]:
-        copy.wait_recv()
-    for items in plan:
-        for copy in items:
-            copy.wait_send()
+        for at, steps in ((1, (2, 3)), (2, (4,))):
+            @pl.when(chunk == at)
+            def _():
+                for step in steps:
+                    advance(step)
+
+    advance(6)
+    for copy in plan.values():
+        copy.wait_send()
     for chunk in range(OWN_CHUNKS):
         copy_out(chunk).wait()
 
 
-def own_edges(feat, pos, neigh, counts, order, rbf, radial, mix):
+def own_edges(*operands):
     vmem = pl.BlockSpec(memory_space=pltpu.VMEM)
     edges = ATOMS * HALF
     return pl.pallas_call(
@@ -285,17 +324,21 @@
             jax.ShapeDtypeStruct((8, edges), F32),
             jax.ShapeDtypeStruct((edges, ATOMS), BF16),
             jax.ShapeDtypeStruct((4, 4, 4, 8, WIDE), BF16),
+            jax.ShapeDtypeStruct((len(BLOCKS), 2 * C, 2 * C), BF16),
+            jax.ShapeDtypeStruct((len(BLOCKS), 2 * C, 2 * C), BF16),
             jax.ShapeDtypeStruct((edges, FEAT), BF16),
         ),
-        in_specs=[vmem] * 8,
-        out_specs=(vmem, vmem, vmem, vmem, pl.BlockSpec(memory_space=pl.ANY)),
-        scratch_shapes=[
-            pltpu.VMEM((len(BLOCKS), 2 * C, 2 * C), BF16),
+        in_specs=[pl.BlockSpec(memory_space=pltpu.HBM)] * len(operands),
+        out_specs=(vmem,) * 6 + (pl.BlockSpec(memory_space=pl.ANY),),
+        scratch_shapes=like(operands)
+        + [
             pltpu.VMEM((8, ATOMS), F32),
-            pltpu.VMEM((ATOMS, SLOTS), BF16),
-            pltpu.VMEM((ATOMS, SLOTS), BF16),
+            pltpu.VMEM((SLOTS, ATOMS), BF16),
+            pltpu.VMEM((SLOTS, ATOMS), BF16),
             pltpu.VMEM((OWN_ROWS, DEGREES * C), BF16),
             pltpu.VMEM((OWN_ROWS, DEGREES * C), BF16),
+            pltpu.VMEM((2 * OWN_ROWS, FEAT), BF16),
+            pltpu.VMEM((OWN_ROWS, FEAT), BF16),
             pltpu.VMEM((edges, FEAT), BF16),
             pltpu.SemaphoreType.DMA((OWN_CHUNKS,)),
             pltpu.SemaphoreType.DMA((HALO_COPIES,)),
@@ -304,22 +347,29 @@
         compiler_params=pltpu.CompilerParams(vmem_limit_bytes=VMEM_LIMIT, collective_id=0, has_side_effects=True),
         cost_estimate=pl.CostEstimate(flops=8_000_000_000, bytes_accessed=10_000_000, transcendentals=600_000),
         name="own_edges",
-    )(feat, pos, neigh, counts, order, rbf, radial, mix)
+    )(*operands)
 
 
 def ghost_body(
+    feat_hbm, pos_hbm, neigh_hbm, counts_hbm, rbf_hbm, radial_hbm, mix_hbm, out_hbm,
+    energy_hbm, norm_hbm, acc_own_ref, relt_ref, pair_ref, table_ref, block_ref, oblock_ref, slope_hbm,
+    new_ref, energies_ref, grad_own_ref, tiles_ref,
     feat_ref, pos_ref, neigh_ref, counts_ref, rbf_ref, radial_ref, mix_ref, out_ref,
-    energy_ref, norm_ref, acc_own_ref, relt_ref, pair_ref, table_ref, slope_hbm,
-    new_ref, energies_ref, grad_own_ref, tiles_ref,
-    block_ref, oblock_ref, pos8_ref, cells_ref, within_ref, rad_ref, drad_ref,
-    slope_ref, gslope_ref, acc_ref, grelt_ref, gslot_ref, gatom_ref, gsum_ref, sem,
+    energy_ref, norm_ref, load_sem,
+    pos8_ref, cells_ref, within_ref, rad_ref, drad_ref, lhs_ref, message_ref,
+    slope_ref, gslope_ref, acc_ref, grelt_ref, gslot_ref, gatom_ref, updated_ref, grad_ref, gsum_ref, sem,
 ):
+    loads = load_all(
+        (pos_hbm, neigh_hbm, counts_hbm, rbf_hbm, radial_hbm, mix_hbm, out_hbm, feat_hbm, energy_hbm, norm_hbm),
+        (pos_ref, neigh_ref, counts_ref, rbf_ref, radial_ref, mix_ref, out_ref, feat_ref, energy_ref, norm_ref),
+        load_sem,
+    )
     load_slope = pltpu.make_async_copy(slope_hbm, slope_ref, sem)
     load_slope.start()
-    fill_blocks(block_ref, mix_ref)
-    fill_blocks(oblock_ref, out_ref)
+    for at in (0, 1, 2):
+        loads[at].wait()
     pos8_ref[...] = jnp.zeros(pos8_ref.shape, F32)
-    pos8_ref[0:3, :] = pos_ref[...]
+    pos8_ref[0:3, :] = pos_ref[:, 0, :]
     stacked = [part.astype(F32) for part in split3(pos8_ref[...])] + [jnp.zeros((C - 24, ATOMS), F32)]
     stacked = jnp.concatenate(stacked, axis=0).astype(BF16)
     cells, within = neighbour_parts(neigh_ref)
@@ -334,6 +384,8 @@
     total = jnp.sum(live_row).astype(jnp.int32)
     chunks = (total + GHOST_ROWS - 1) // GHOST_ROWS
     acc_ref[...] = acc_own_ref[...]
+    for copy in loads[3:]:
+        copy.wait()
 
     def whole(gathered):
         return gathered + (pltpu.roll(gathered, C - 8, 1) + pltpu.roll(gathered, C - 16, 1))
@@ -350,7 +402,7 @@
         begin = jnp.sum(jnp.where(inside, start_row, 0.0), axis=1, keepdims=True)
         spread = onehot_of(inside)
         gather = onehot_of(spread_of(chunk))
-        named = dot(spread, cells_ref[...]) * 8.0 + dot(spread, within_ref[...])
+        named = dot_nt(spread, cells_ref[...]) * 8.0 + dot_nt(spread, within_ref[...])
         named = select_lane(named, (place - begin).astype(jnp.int32) + HALF, 0.0)
         onehot = onehot_of(iota((GHOST_ROWS, GHOST), 1).astype(F32) == named - float(ATOMS))
         row = named.astype(jnp.int32) - ATOMS
@@ -375,38 +427,40 @@
         grelt_ref[:, rows] = rel.T[:8]
         radial_of(rel, rbf_ref, radial_ref, rad_ref, drad_ref)
 
-        def put_message(lanes, value):
-            acc_ref[:, lanes] += dot(gather, value)
-
         def put_slope(lanes, value):
             gslope_ref[rows, lanes] = value
 
         last = last[:, :C].astype(BF16)
-        edge_forward(onehot, table_ref, rad_ref, drad_ref, block_ref, mix_ref, put_message, put_slope, last)
-
-    energy = None
+        edge_forward(onehot, table_ref, rad_ref, drad_ref, block_ref, mix_ref, lhs_ref, message_ref, put_slope, last)
+        for pair in PAIRS:
+            lanes = slice(pair[0] * C, (pair[-1] + 1) * C)
+            acc_ref[:, lanes] += dot(gather, message_ref[:, lanes])
+
     for pair in PAIRS:
         lanes = slice(pair[0] * C, (pair[-1] + 1) * C)
         low = (acc_ref[:, lanes] * NORM).astype(BF16)
+        updated_ref[:, lanes] = dot(low, pair_weight(pair, oblock_ref, out_ref))
+    energy = None
+    for k in range(COEFFS):
+        lanes = slice(k * C, (k + 1) * C)
+        value = feat_ref[:, lanes].astype(F32) + updated_ref[:, lanes]
+        new_ref[:, lanes] = value.astype(BF16)
+        if k == 0:
+            logistic = jax.nn.sigmoid(value)
+            scale = energy_ref[...]
+            term = scale * value * logistic
+            grad = scale * logistic * (1.0 + value * (1.0 - logistic))
+        else:
+            degree = DEGREE[k]
+            scaled = norm_ref[degree - 1 : degree, :] * (1.0 / (2 * degree + 1)) * value
+            term = scaled * value
+            grad = 2.0 * scaled
+        energy = term if energy is None else energy + term
+        grad_ref[:, lanes] = grad.astype(BF16)
+    for pair in PAIRS:
+        lanes = slice(pair[0] * C, (pair[-1] + 1) * C)
         weight = pair_weight(pair, oblock_ref, out_ref)
-        updated = feat_ref[:, lanes].astype(F32) + dot(low, weight)
-        new_ref[:, lanes] = updated.astype(BF16)
-        grads = []
-        for at, k in enumerate(pair):
-            value = updated[:, at * C : (at + 1) * C]
-            if k == 0:
-                logistic = jax.nn.sigmoid(value)
-                scale = energy_ref[...]
-                term = scale * value * logistic
-                grads.append(scale * logistic * (1.0 + value * (1.0 - logistic)))
-            else:
-                degree = DEGREE[k]
-                scaled = norm_ref[degree - 1 : degree, :] * (1.0 / (2 * degree + 1)) * value
-                term = scaled * value
-                grads.append(2.0 * scaled)
-            energy = term if energy is None else energy + term
-        grad = jnp.concatenate(grads, axis=1).astype(BF16)
-        gsum_ref[:, lanes] = (dot_nt(grad, weight) * NORM).astype(BF16)
+        gsum_ref[:, lanes] = (dot_nt(grad_ref[:, lanes], weight) * NORM).astype(BF16)
     energy = jnp.sum(energy, axis=1, keepdims=True)
     energies_ref[...] = jnp.sum(jnp.where(row_id == col_id, energy, 0.0), axis=0, keepdims=True)
 
@@ -417,19 +471,18 @@
         return jnp.concatenate([high, (pull - high.astype(F32)).astype(BF16)], axis=0)
 
     load_slope.wait()
-    atoms = OWN_ROWS // HALF
-    own_gather = jnp.where(iota((atoms, OWN_ROWS), 1) // HALF == iota((atoms, OWN_ROWS), 0), 1.0, 0.0)
 
     def own_step(chunk, total):
-        here = pl.ds(pl.multiple_of(chunk * atoms, atoms), atoms)
         rows = pl.ds(pl.multiple_of(chunk * OWN_ROWS, OWN_ROWS), OWN_ROWS)
-        slopes = jnp.sum(dot_nt(gsum_ref[here, :], slope_ref[rows, :]) * own_gather, axis=0, keepdims=True)
+        slopes = dot_nt(slope_ref[rows, :], gsum_ref[...]).T
+        own = (iota((ATOMS, OWN_ROWS), 1) + chunk * OWN_ROWS) // HALF == iota((ATOMS, OWN_ROWS), 0)
+        slopes = jnp.sum(jnp.where(own, slopes, 0.0), axis=0, keepdims=True)
         return total + dot(pull_of(relt_ref[:, rows], slopes), pair_ref[rows, :])
 
     def ghost_step(chunk, totals):
         own_total, ghost_total = totals
         rows = pl.ds(pl.multiple_of(chunk * GHOST_ROWS, GHOST_ROWS), GHOST_ROWS)
-        slopes = dot_nt(gsum_ref[...], gslope_ref[rows, :])
+        slopes = dot_nt(gslope_ref[rows, :], gsum_ref[...]).T
         slopes = jnp.sum(jnp.where(spread_of(chunk), slopes, 0.0), axis=0, keepdims=True)
         pull = pull_of(grelt_ref[:, rows], slopes)
         return own_total - dot(pull, gatom_ref[rows, :]), ghost_total + dot(pull, gslot_ref[rows, :])
@@ -454,22 +507,25 @@
             jax.ShapeDtypeStruct((8, ATOMS), F32),
             jax.ShapeDtypeStruct((TILES, 8, C), F32),
         ),
-        in_specs=[vmem] * 14 + [hbm],
+        in_specs=[pl.BlockSpec(memory_space=pltpu.HBM)] * 10 + [vmem] * 6 + [hbm],
         out_specs=(vmem,) * 4,
-        scratch_shapes=[
-            pltpu.VMEM((len(BLOCKS), 2 * C, 2 * C), BF16),
-            pltpu.VMEM((len(BLOCKS), 2 * C, 2 * C), BF16),
+        scratch_shapes=like(operands[:10])
+        + [
             pltpu.VMEM((8, ATOMS), F32),
-            pltpu.VMEM((ATOMS, SLOTS), BF16),
-            pltpu.VMEM((ATOMS, SLOTS), BF16),
+            pltpu.VMEM((SLOTS, ATOMS), BF16),
+            pltpu.VMEM((SLOTS, ATOMS), BF16),
             pltpu.VMEM((GHOST_ROWS, DEGREES * C), BF16),
             pltpu.VMEM((GHOST_ROWS, DEGREES * C), BF16),
+            pltpu.VMEM((2 * GHOST_ROWS, FEAT), BF16),
+            pltpu.VMEM((GHOST_ROWS, FEAT), BF16),
             pltpu.VMEM((own, FEAT), BF16),
             pltpu.VMEM((GHOST_EDGES, FEAT), BF16),
             pltpu.VMEM((ATOMS, FEAT), F32),
             pltpu.VMEM((8, GHOST_EDGES), F32),
             pltpu.VMEM((GHOST_EDGES, TILES * C), BF16),
             pltpu.VMEM((GHOST_EDGES, ATOMS), BF16),
+            pltpu.VMEM((ATOMS, FEAT), F32),
+            pltpu.VMEM((ATOMS, FEAT), BF16),
             pltpu.VMEM((ATOMS, FEAT), BF16),
             pltpu.SemaphoreType.DMA,
         ],
@@ -479,7 +535,8 @@
     )(*operands)
 
 
-def return_body(tiles_ref, grad_own_ref, order_ref, forces_ref, landed_ref, send_sem, recv_sem):
+def return_body(tiles_ref, grad_own_ref, order_hbm, forces_ref, order_ref, load_sem, landed_ref, send_sem, recv_sem):
+    loads = load_all((order_hbm,), (order_ref,), load_sem)
     here = [lax.axis_index(axis) for axis in ("gx", "gy", "gz")]
     sizes = [lax.axis_size(axis) for axis in ("gx", "gy", "gz")]
     barrier = pltpu.get_barrier_semaphore()
@@ -499,6 +556,7 @@
     pl.semaphore_wait(barrier, len(others))
     for copy in copies:
         copy.start()
+    loads[0].wait()
     listed = column_of(order_ref[...].astype(F32)) == iota((ATOMS, ATOMS), 1).astype(F32)
     listed = onehot_of(listed)
     for copy in copies:
@@ -507,7 +565,7 @@
     odd = sum(landed_ref[at] for at in others if at % 2 == 1)
     total = (even + pltpu.roll(odd, ATOMS, 1))[:, :ATOMS]
     back = sum(dot(part, listed) for part in split3(total)[::-1])
-    forces_ref[...] = -(grad_own_ref[...] + back)[:3]
+    forces_ref[:, 0, :] = -(grad_own_ref[...] + back)[:3]
     for copy in copies:
         copy.wait_send()
 
@@ -516,15 +574,16 @@
     vmem = pl.BlockSpec(memory_space=pltpu.VMEM)
     return pl.pallas_call(
         return_body,
-        out_shape=jax.ShapeDtypeStruct((3, ATOMS), F32),
-        in_specs=[vmem] * 3,
+        out_shape=jax.ShapeDtypeStruct((3, 1, ATOMS), F32),
+        in_specs=[vmem] * 2 + [pl.BlockSpec(memory_space=pltpu.HBM)],
         out_specs=vmem,
-        scratch_shapes=[
+        scratch_shapes=like((order,))
+        + [
             pltpu.VMEM((DIRECTIONS, 8, C), F32),
             pltpu.SemaphoreType.DMA((DIRECTIONS,)),
             pltpu.SemaphoreType.DMA((DIRECTIONS,)),
         ],
-        compiler_params=pltpu.CompilerParams(collective_id=1, has_side_effects=True),
+        compiler_params=pltpu.CompilerParams(collective_id=1, has_side_effects=True, vmem_limit_bytes=4 * 1024 * 1024),
         name="return_forces",
     )(tiles, grad_own, order)
 
@@ -534,14 +593,21 @@
     rbf_weight, radial_weight, mix_weight, out_weight, energy_weight, norm_weight,
 ):
     feat = features.reshape(ATOMS, FEAT)
-    pos = positions.reshape(3, ATOMS)
-    neigh = neighbours.reshape(ATOMS, SLOTS)
+    pos = positions.reshape(3, 1, ATOMS)
+    neigh = jnp.transpose(neighbours.reshape(ATOMS, SLOTS))
     live = counts.reshape(1, ATOMS)
     order = cell_atoms.reshape(1, ATOMS)
-    acc, relt, pairs, table, slopes = own_edges(feat, pos, neigh, live, order, rbf_weight, radial_weight, mix_weight)
+    energy, norm = energy_weight.reshape(1, C), norm_weight
+    feat, pos, neigh, live, order, rbf_weight, radial_weight, mix_weight, out_weight, energy, norm = (
+        pltpu.with_memory_space_constraint(operand, pltpu.HBM)
+        for operand in (feat, pos, neigh, live, order, rbf_weight, radial_weight, mix_weight, out_weight, energy, norm)
+    )
+    acc, relt, pairs, table, blocks, oblocks, slopes = own_edges(
+        feat, pos, neigh, live, order, rbf_weight, radial_weight, mix_weight, out_weight
+    )
     updated, energies, grad_own, tiles = ghost_edges(
         feat, pos, neigh, live, rbf_weight, radial_weight, mix_weight, out_weight,
-        energy_weight.reshape(1, C), norm_weight, acc, relt, pairs, table.reshape(GHOST, WIDE), slopes,
+        energy, norm, acc, relt, pairs, table.reshape(GHOST, WIDE), blocks, oblocks, slopes,
     )
     forces = return_forces(tiles, grad_own, order)
     return (

time: 90.6 us -> 69.5 us (0.77)
  Pallas kernels: 80.4 us -> 68.1 us
  local copies, waits for them, and re-layouts: 8.98 us -> 0.56 us
    unnamed x29 -> x1, local copies, waits for them, and re-layouts: 8.98 us -> 0.56 us
    pallas_call x1, Pallas kernels: 43.6 us -> 38.2 us  [own_edges(): pl.pallas_call(own_body, out_shape=(jax.ShapeDtypeStruct((ATOMS, FEAT), F...]
    pallas_call x1, Pallas kernels: 20.7 us -> 16.5 us  [ghost_edges(): pl.pallas_call(ghost_body, out_shape=(jax.ShapeDtypeStruct((ATOMS, FEAT),...]
    pallas_call x1, Pallas kernels: 16.1 us -> 13.4 us  [return_forces(): pl.pallas_call(return_body, out_shape=jax.ShapeDtypeStruct((3, 1, ATOMS),...]
where the time goes in v3:
time: 69.5 us; the launch traced here: 69.3 us
  Pallas kernels  68.1 us (98%)
    pallas_call x1, Pallas kernels, own_edges(): pl.pallas_call(own_body, out_shape=(jax.ShapeDtypeStruct((ATOMS, FEAT), F...  38.2 us
    pallas_call x1, Pallas kernels, ghost_edges(): pl.pallas_call(ghost_body, out_shape=(jax.ShapeDtypeStruct((ATOMS, FEAT),...  16.5 us
    pallas_call x1, Pallas kernels, return_forces(): pl.pallas_call(return_body, out_shape=jax.ShapeDtypeStruct((3, 1, ATOMS),...  13.4 us

profile of v3, /device:TPU:1, one launch (start us, length us, event | category | flops | bytes accessed | tf_op | source)
XLA Modules:
  0.0 69.3 jit_solution(6868194135266284358)
XLA Ops:
  0.6 38.2 %own_edges.1 = (f32[64,3200]{1,0:T(8,128)S(1)}, f32[8,1024]{1,0:T(8,128)S(1)}, bf16[1024,64]{1,0:T(8,128)(2,1)S(1)}, bf16[4,4,4,8,3328]{4,3,2,1,0:T(8,128)(2,1)}...) custom-call(bf16[64,3200]{1,0:T(8,128)(2,1)} %bitcast.17, ...), custom_call_target="tpu_custom_call" | custom-call | flops 8000000000 | bytes 10000000 | tf_op jit(solution)/shard_map/own_edges/pallas_call | solution.py:320
  38.9 16.5 %ghost_edges.1 = (bf16[64,3200]{1,0:T(8,128)(2,1)}, f32[1,64]{1,0:T(1,128)}, f32[8,64]{1,0:T(8,128)S(1)}, f32[14,8,128]{2,1,0:T(8,128)S(1)}) custom-call(bf16[64,3200]{1,0:T(8,128)(2,1)} %bitcast.18, f32[3,1,64]{2,1,0:T(1,128)} %bitcast.22, s32[32,64]{1,0:T(8,128)} %bitcast.20, s32[1,64]{1,0:T(1,128)} %bitcast.24, bf16[512,128]{1,0:T(8,128)(2,1)} %rbf_hbm.3, ...), custom_call_target="tpu_custom_call" | custom-call | flops 10000000000 | bytes 14000000 | tf_op jit(solution)/shard_map/ghost_edges/pallas_call | solution.py:502
  55.3 13.4 %return_forces.1 = f32[3,1,64]{2,1,0:T(1,128)S(1)} custom-call(f32[14,8,128]{2,1,0:T(8,128)S(1)} %get-tuple-element.23.tiles_ref, f32[8,64]{1,0:T(8,128)S(1)} %get-tuple-element.24.grad_own_ref, s32[1,64]{1,0:T(1,128)} %bitcast.16), custom_call_target="tpu_custom_call" | custom-call | tf_op jit(solution)/shard_map/return_forces/pallas_call | solution.py:575
  68.8 0.6 copy.16

commit v4 on v3

--- a/solution.py
+++ b/solution.py
@@ -23,6 +23,8 @@
 OWN_ROWS = 256
 OWN_CHUNKS = ATOMS * HALF // OWN_ROWS
 GHOST_ROWS = 128
+HEAD = 512
+TAIL = 256
 GHOST_EDGES = ATOMS * HALF
 VMEM_LIMIT = 50 * 1024 * 1024
 
@@ -75,7 +77,7 @@
     return value if len(pair) == 1 else jnp.concatenate([value, value], axis=1)
 
 
-def radial_of(rel, rbf_ref, radial_ref, rad_ref, drad_ref):
+def radial_of(rel, rbf_ref, radial_ref, rad_ref, drad_ref, at):
     distance = jnp.sqrt(jnp.sum(rel * rel, axis=1, keepdims=True))
     rows = rel.shape[0]
     centred = distance * (1.0 / SPACING) - iota((rows, RBF), 1).astype(F32)
@@ -85,11 +87,11 @@
     logistic = jax.nn.sigmoid(preact)
     hidden = (preact * logistic).astype(BF16)
     dhidden = (slope * logistic * (1.0 + preact * (1.0 - logistic))).astype(BF16)
-    rad_ref[...] = dot(hidden, radial_ref[...]).astype(BF16)
-    drad_ref[...] = dot(dhidden, radial_ref[...]).astype(BF16)
-
-
-def edge_forward(onehot, table_ref, rad_ref, drad_ref, block_ref, mix_ref, lhs_ref, message_ref, put_slope, last=None, middle=None):
+    rad_ref[at, :] = dot(hidden, radial_ref[...]).astype(BF16)
+    drad_ref[at, :] = dot(dhidden, radial_ref[...]).astype(BF16)
+
+
+def edge_forward(onehot, table_ref, rad_ref, drad_ref, at_rows, block_ref, mix_ref, lhs_ref, message_ref, put_slope, last=None, middle=None):
     rows = onehot.shape[0]
     for pair in PAIRS:
         lanes = slice(pair[0] * C, (pair[-1] + 1) * C)
@@ -100,8 +102,8 @@
         for at, k in enumerate(pair):
             cut = slice(DEGREE[k] * C, (DEGREE[k] + 1) * C)
             half = near[:, at * C : (at + 1) * C]
-            lhs_ref[:rows, k * C : (k + 1) * C] = half * rad_ref[:, cut]
-            lhs_ref[rows:, k * C : (k + 1) * C] = half * drad_ref[:, cut]
+            lhs_ref[:rows, k * C : (k + 1) * C] = half * rad_ref[at_rows, cut]
+            lhs_ref[rows:, k * C : (k + 1) * C] = half * drad_ref[at_rows, cut]
     if middle is not None:
         middle()
     gate = lean = None
@@ -220,7 +222,7 @@
     feat_hbm, pos_hbm, neigh_hbm, counts_hbm, order_hbm, rbf_hbm, radial_hbm, mix_hbm, out_hbm,
     acc_ref, relt_ref, pair_ref, table_ref, block_ref, oblock_ref, slope_hbm,
     feat_ref, pos_ref, neigh_ref, counts_ref, order_ref, rbf_ref, radial_ref, mix_ref, out_ref, load_sem,
-    pos8_ref, cells_ref, within_ref, rad_ref, drad_ref, lhs_ref, message_ref, slope_ref, sem, send_sem, recv_sem,
+    pos8_ref, cells_ref, within_ref, rad_ref, drad_ref, hot_ref, lhs_ref, message_ref, slope_ref, sem, send_sem, recv_sem,
 ):
     loads = load_all(
         (feat_hbm, pos_hbm, neigh_hbm, counts_hbm, order_hbm, rbf_hbm, radial_hbm, mix_hbm, out_hbm),
@@ -259,7 +261,6 @@
     cells_ref[...] = cells
     within_ref[...] = within
     atoms = OWN_ROWS // HALF
-    edge = iota((OWN_ROWS, 1), 0)
     gather = onehot_of(iota((atoms, OWN_ROWS), 1) // HALF == iota((atoms, OWN_ROWS), 0))
 
     def copy_out(chunk):
@@ -269,12 +270,11 @@
             sem.at[chunk],
         )
 
-    @pl.loop(0, OWN_CHUNKS)
-    def _(chunk):
-        here = pl.ds(pl.multiple_of(chunk * atoms, atoms), atoms)
-        rows = pl.ds(pl.multiple_of(chunk * OWN_ROWS, OWN_ROWS), OWN_ROWS)
-        centre = chunk * atoms + edge // HALF
-        lane = iota((OWN_ROWS, ATOMS), 1)
+    def geometry(start, count):
+        rows = slice(start, start + count)
+        edge = iota((count, 1), 0)
+        centre = (start + edge) // HALF
+        lane = iota((count, ATOMS), 1)
         spread = onehot_of(lane == centre)
         named = dot_nt(spread, cells_ref[...]) * 8.0 + dot_nt(spread, within_ref[...])
         named = select_lane(named, edge % HALF, 0.0)
@@ -283,25 +283,35 @@
         edge_pair = jnp.where(hit, 1.0, jnp.where(lane == centre, -1.0, 0.0)).astype(BF16)
         pair_ref[rows, :] = edge_pair
         relt_ref[:, rows] = gather_places(edge_pair, parts, True)
-        radial_of(gather_places(edge_pair, parts, False), rbf_ref, radial_ref, rad_ref, drad_ref)
-        onehot = onehot_of(jnp.logical_and(hit, (edge % HALF).astype(F32) < live_count))
+        hot_ref[rows, :] = onehot_of(jnp.logical_and(hit, (edge % HALF).astype(F32) < live_count))
+        radial_of(gather_places(edge_pair, parts, False), rbf_ref, radial_ref, rad_ref, drad_ref, rows)
+
+    for start in range(0, ATOMS * HALF, HEAD):
+        geometry(start, HEAD)
+    advance(1)
+
+    @pl.loop(0, OWN_CHUNKS)
+    def _(chunk):
+        here = pl.ds(pl.multiple_of(chunk * atoms, atoms), atoms)
+        rows = pl.ds(pl.multiple_of(chunk * OWN_ROWS, OWN_ROWS), OWN_ROWS)
+        onehot = hot_ref[rows, :]
 
         def put_slope(lanes, value):
             slope_ref[rows, lanes] = value
 
         def middle():
-            for at, step in ((1, 1), (3, 5)):
+            for at, step in ((1, 3), (2, 4)):
                 @pl.when(chunk == at)
                 def _():
                     advance(step)
 
-        edge_forward(onehot, feat_ref, rad_ref, drad_ref, block_ref, mix_ref, lhs_ref, message_ref, put_slope, middle=middle)
+        edge_forward(onehot, feat_ref, rad_ref, drad_ref, rows, block_ref, mix_ref, lhs_ref, message_ref, put_slope, middle=middle)
         for pair in PAIRS:
             lanes = slice(pair[0] * C, (pair[-1] + 1) * C)
             acc_ref[here, lanes] = dot(gather, message_ref[:, lanes])
         copy_out(chunk).start()
 
-        for at, steps in ((1, (2, 3)), (2, (4,))):
+        for at, steps in ((0, (2,)), (3, (5,))):
             @pl.when(chunk == at)
             def _():
                 for step in steps:
@@ -335,8 +345,9 @@
             pltpu.VMEM((8, ATOMS), F32),
             pltpu.VMEM((SLOTS, ATOMS), BF16),
             pltpu.VMEM((SLOTS, ATOMS), BF16),
-            pltpu.VMEM((OWN_ROWS, DEGREES * C), BF16),
-            pltpu.VMEM((OWN_ROWS, DEGREES * C), BF16),
+            pltpu.VMEM((edges, DEGREES * C), BF16),
+            pltpu.VMEM((edges, DEGREES * C), BF16),
+            pltpu.VMEM((edges, ATOMS), BF16),
             pltpu.VMEM((2 * OWN_ROWS, FEAT), BF16),
             pltpu.VMEM((OWN_ROWS, FEAT), BF16),
             pltpu.VMEM((edges, FEAT), BF16),
@@ -357,7 +368,7 @@
     feat_ref, pos_ref, neigh_ref, counts_ref, rbf_ref, radial_ref, mix_ref, out_ref,
     energy_ref, norm_ref, load_sem,
     pos8_ref, cells_ref, within_ref, rad_ref, drad_ref, lhs_ref, message_ref,
-    slope_ref, gslope_ref, acc_ref, grelt_ref, gslot_ref, gatom_ref, updated_ref, grad_ref, gsum_ref, sem,
+    slope_ref, gslope_ref, acc_ref, grelt_ref, gslot_ref, gatom_ref, hot_ref, last_ref, updated_ref, grad_ref, gsum_ref, sem,
 ):
     loads = load_all(
         (pos_hbm, neigh_hbm, counts_hbm, rbf_hbm, radial_hbm, mix_hbm, out_hbm, feat_hbm, energy_hbm, norm_hbm),
@@ -390,21 +401,19 @@
     def whole(gathered):
         return gathered + (pltpu.roll(gathered, C - 8, 1) + pltpu.roll(gathered, C - 16, 1))
 
-    def spread_of(chunk):
-        place = (iota((ATOMS, GHOST_ROWS), 1) + chunk * GHOST_ROWS).astype(F32)
+    def spread_of(start, count):
+        place = (iota((ATOMS, count), 1) + start).astype(F32)
         return jnp.logical_and(place >= start_col, place < start_col + live_col)
 
-    @pl.loop(0, chunks)
-    def _(chunk):
-        rows = pl.ds(pl.multiple_of(chunk * GHOST_ROWS, GHOST_ROWS), GHOST_ROWS)
-        place = (iota((GHOST_ROWS, 1), 0) + chunk * GHOST_ROWS).astype(F32)
+    def geometry(start, count):
+        rows = pl.ds(start, count)
+        place = (iota((count, 1), 0) + start).astype(F32)
         inside = jnp.logical_and(place >= start_row, place < start_row + live_row)
         begin = jnp.sum(jnp.where(inside, start_row, 0.0), axis=1, keepdims=True)
         spread = onehot_of(inside)
-        gather = onehot_of(spread_of(chunk))
         named = dot_nt(spread, cells_ref[...]) * 8.0 + dot_nt(spread, within_ref[...])
         named = select_lane(named, (place - begin).astype(jnp.int32) + HALF, 0.0)
-        onehot = onehot_of(iota((GHOST_ROWS, GHOST), 1).astype(F32) == named - float(ATOMS))
+        onehot = onehot_of(iota((count, GHOST), 1).astype(F32) == named - float(ATOMS))
         row = named.astype(jnp.int32) - ATOMS
         inside = row >= 0
         row = jnp.maximum(row, 0)
@@ -415,23 +424,38 @@
         for at, spot in enumerate(spots):
             slot = slot + (((spot + 1) & 1) << (5 - at))
         place = jnp.where(inside, toward * ATOMS + slot, -1)
-        gslot_ref[rows, :] = onehot_of(iota((GHOST_ROWS, TILES * C), 1) == place)
+        hot_ref[rows, :] = onehot
+        gslot_ref[rows, :] = onehot_of(iota((count, TILES * C), 1) == place)
         gatom_ref[rows, :] = spread
-        lane = iota((GHOST_ROWS, C), 1)
+        lane = iota((count, C), 1)
         last = dot(onehot, table_ref[:, FEAT - C :])
-        image = jnp.zeros((GHOST_ROWS, C), F32)
+        image = jnp.zeros((count, C), F32)
         for at, move in enumerate(moves):
             image = jnp.where(lane == at, move.astype(F32) * 4.0, image)
         rel = (whole(last[:, C:]) + image) - whole(dot_nt(spread, stacked))
         rel = jnp.where(jnp.logical_and(lane < 3, inside), rel, 0.0)
         grelt_ref[:, rows] = rel.T[:8]
-        radial_of(rel, rbf_ref, radial_ref, rad_ref, drad_ref)
+        last_ref[rows, :] = last[:, :C].astype(BF16)
+        radial_of(rel, rbf_ref, radial_ref, rad_ref, drad_ref, rows)
+
+    tails = jnp.maximum(total - HEAD + TAIL - 1, 0) // TAIL
+    tail_at = lambda at: pl.multiple_of(HEAD + at * TAIL, TAIL)
+    geometry(0, HEAD)
+
+    @pl.loop(0, tails)
+    def _(at):
+        geometry(tail_at(at), TAIL)
+
+    @pl.loop(0, chunks)
+    def _(chunk):
+        rows = pl.ds(pl.multiple_of(chunk * GHOST_ROWS, GHOST_ROWS), GHOST_ROWS)
 
         def put_slope(lanes, value):
             gslope_ref[rows, lanes] = value
 
-        last = last[:, :C].astype(BF16)
-        edge_forward(onehot, table_ref, rad_ref, drad_ref, block_ref, mix_ref, lhs_ref, message_ref, put_slope, last)
+        onehot, last = hot_ref[rows, :], last_ref[rows, :]
+        gather = onehot_of(spread_of(chunk * GHOST_ROWS, GHOST_ROWS))
+        edge_forward(onehot, table_ref, rad_ref, drad_ref, rows, block_ref, mix_ref, lhs_ref, message_ref, put_slope, last)
         for pair in PAIRS:
             lanes = slice(pair[0] * C, (pair[-1] + 1) * C)
             acc_ref[:, lanes] += dot(gather, message_ref[:, lanes])
@@ -460,7 +484,7 @@
     for pair in PAIRS:
         lanes = slice(pair[0] * C, (pair[-1] + 1) * C)
         weight = pair_weight(pair, oblock_ref, out_ref)
-        gsum_ref[:, lanes] = (dot_nt(grad_ref[:, lanes], weight) * NORM).astype(BF16)
+        gsum_ref[lanes, :] = (dot_nt(weight, grad_ref[:, lanes]) * NORM).astype(BF16)
     energy = jnp.sum(energy, axis=1, keepdims=True)
     energies_ref[...] = jnp.sum(jnp.where(row_id == col_id, energy, 0.0), axis=0, keepdims=True)
 
@@ -472,23 +496,24 @@
 
     load_slope.wait()
 
-    def own_step(chunk, total):
-        rows = pl.ds(pl.multiple_of(chunk * OWN_ROWS, OWN_ROWS), OWN_ROWS)
-        slopes = dot_nt(slope_ref[rows, :], gsum_ref[...]).T
-        own = (iota((ATOMS, OWN_ROWS), 1) + chunk * OWN_ROWS) // HALF == iota((ATOMS, OWN_ROWS), 0)
+    own_total = jnp.zeros((16, ATOMS), F32)
+    for start in range(0, ATOMS * HALF, OWN_ROWS):
+        rows = slice(start, start + OWN_ROWS)
+        slopes = dot(slope_ref[rows, :], gsum_ref[...]).T
+        own = (iota((ATOMS, OWN_ROWS), 1) + start) // HALF == iota((ATOMS, OWN_ROWS), 0)
         slopes = jnp.sum(jnp.where(own, slopes, 0.0), axis=0, keepdims=True)
-        return total + dot(pull_of(relt_ref[:, rows], slopes), pair_ref[rows, :])
-
-    def ghost_step(chunk, totals):
+        own_total = own_total + dot(pull_of(relt_ref[:, rows], slopes), pair_ref[rows, :])
+
+    def ghost_step(start, count, totals):
         own_total, ghost_total = totals
-        rows = pl.ds(pl.multiple_of(chunk * GHOST_ROWS, GHOST_ROWS), GHOST_ROWS)
-        slopes = dot_nt(gslope_ref[rows, :], gsum_ref[...]).T
-        slopes = jnp.sum(jnp.where(spread_of(chunk), slopes, 0.0), axis=0, keepdims=True)
+        rows = pl.ds(start, count)
+        slopes = dot(gslope_ref[rows, :], gsum_ref[...]).T
+        slopes = jnp.sum(jnp.where(spread_of(start, count), slopes, 0.0), axis=0, keepdims=True)
         pull = pull_of(grelt_ref[:, rows], slopes)
         return own_total - dot(pull, gatom_ref[rows, :]), ghost_total + dot(pull, gslot_ref[rows, :])
 
-    own_total = lax.fori_loop(0, OWN_CHUNKS, own_step, jnp.zeros((16, ATOMS), F32))
-    own_total, ghost_total = lax.fori_loop(0, chunks, ghost_step, (own_total, jnp.zeros((16, TILES * C), F32)))
+    totals = ghost_step(0, HEAD, (own_total, jnp.zeros((16, TILES * C), F32)))
+    own_total, ghost_total = lax.fori_loop(0, tails, lambda at, total: ghost_step(tail_at(at), TAIL, total), totals)
     grad_own_ref[...] = own_total[:8] + own_total[8:]
     for tile in range(TILES):
         lanes = slice(tile * C, (tile + 1) * C)
@@ -514,8 +539,8 @@
             pltpu.VMEM((8, ATOMS), F32),
             pltpu.VMEM((SLOTS, ATOMS), BF16),
             pltpu.VMEM((SLOTS, ATOMS), BF16),
-            pltpu.VMEM((GHOST_ROWS, DEGREES * C), BF16),
-            pltpu.VMEM((GHOST_ROWS, DEGREES * C), BF16),
+            pltpu.VMEM((GHOST_EDGES, DEGREES * C), BF16),
+            pltpu.VMEM((GHOST_EDGES, DEGREES * C), BF16),
             pltpu.VMEM((2 * GHOST_ROWS, FEAT), BF16),
             pltpu.VMEM((GHOST_ROWS, FEAT), BF16),
             pltpu.VMEM((own, FEAT), BF16),
@@ -524,9 +549,11 @@
             pltpu.VMEM((8, GHOST_EDGES), F32),
             pltpu.VMEM((GHOST_EDGES, TILES * C), BF16),
             pltpu.VMEM((GHOST_EDGES, ATOMS), BF16),
+            pltpu.VMEM((GHOST_EDGES, GHOST), BF16),
+            pltpu.VMEM((GHOST_EDGES, C), BF16),
             pltpu.VMEM((ATOMS, FEAT), F32),
             pltpu.VMEM((ATOMS, FEAT), BF16),
-            pltpu.VMEM((ATOMS, FEAT), BF16),
+            pltpu.VMEM((FEAT, ATOMS), BF16),
             pltpu.SemaphoreType.DMA,
         ],
         compiler_params=pltpu.CompilerParams(vmem_limit_bytes=VMEM_LIMIT),

time: 69.5 us -> 67.4 us (0.970)
  Pallas kernels: 68.1 us -> 66 us
    pallas_call x1, Pallas kernels: 13.4 us -> 10.6 us  [return_forces(): pl.pallas_call(return_body, out_shape=jax.ShapeDtypeStruct((3, 1, ATOMS),...]
    pallas_call x1, Pallas kernels: 38.2 us -> 40 us  [own_edges(): pl.pallas_call(own_body, out_shape=(jax.ShapeDtypeStruct((ATOMS, FEAT), F...]
    pallas_call x1, Pallas kernels: 16.5 us -> 15.4 us  [ghost_edges(): pl.pallas_call(ghost_body, out_shape=(jax.ShapeDtypeStruct((ATOMS, FEAT),...]
where the time goes in v4:
time: 67.4 us; the launch traced here: 67.2 us
  Pallas kernels  66 us (98%)
    pallas_call x1, Pallas kernels, own_edges(): pl.pallas_call(own_body, out_shape=(jax.ShapeDtypeStruct((ATOMS, FEAT), F...  40 us
    pallas_call x1, Pallas kernels, ghost_edges(): pl.pallas_call(ghost_body, out_shape=(jax.ShapeDtypeStruct((ATOMS, FEAT),...  15.4 us
    pallas_call x1, Pallas kernels, return_forces(): pl.pallas_call(return_body, out_shape=jax.ShapeDtypeStruct((3, 1, ATOMS),...  10.6 us

profile of v4, /device:TPU:1, one launch (start us, length us, event | category | flops | bytes accessed | tf_op | source)
XLA Modules:
  0.0 67.2 jit_solution(5205897338714450951)
XLA Ops:
  0.6 40.0 %own_edges.1 = (f32[64,3200]{1,0:T(8,128)S(1)}, f32[8,1024]{1,0:T(8,128)S(1)}, bf16[1024,64]{1,0:T(8,128)(2,1)S(1)}, bf16[4,4,4,8,3328]{4,3,2,1,0:T(8,128)(2,1)}...) custom-call(bf16[64,3200]{1,0:T(8,128)(2,1)} %bitcast.17, ...), custom_call_target="tpu_custom_call" | custom-call | flops 8000000000 | bytes 10000000 | tf_op jit(solution)/shard_map/own_edges/pallas_call | solution.py:330
  40.6 15.4 %ghost_edges.1 = (bf16[64,3200]{1,0:T(8,128)(2,1)}, f32[1,64]{1,0:T(1,128)}, f32[8,64]{1,0:T(8,128)S(1)}, f32[14,8,128]{2,1,0:T(8,128)S(1)}) custom-call(bf16[64,3200]{1,0:T(8,128)(2,1)} %bitcast.18, f32[3,1,64]{2,1,0:T(1,128)} %bitcast.22, s32[32,64]{1,0:T(8,128)} %bitcast.20, s32[1,64]{1,0:T(1,128)} %bitcast.24, bf16[512,128]{1,0:T(8,128)(2,1)} %rbf_hbm.3, ...), custom_call_target="tpu_custom_call" | custom-call | flops 10000000000 | bytes 14000000 | tf_op jit(solution)/shard_map/ghost_edges/pallas_call | solution.py:527
  56.0 10.6 %return_forces.1 = f32[3,1,64]{2,1,0:T(1,128)S(1)} custom-call(f32[14,8,128]{2,1,0:T(8,128)S(1)} %get-tuple-element.23.tiles_ref, f32[8,64]{1,0:T(8,128)S(1)} %get-tuple-element.24.grad_own_ref, s32[1,64]{1,0:T(1,128)} %bitcast.16), custom_call_target="tpu_custom_call" | custom-call | tf_op jit(solution)/shard_map/return_forces/pallas_call | solution.py:602
  66.6 0.6 copy.16

commit v5 on v4

--- a/solution.py
+++ b/solution.py
@@ -22,11 +22,11 @@
 SPACING = 2.0 * math.sqrt(48.0) / (RBF - 1)
 OWN_ROWS = 256
 OWN_CHUNKS = ATOMS * HALF // OWN_ROWS
-GHOST_ROWS = 128
+GHOST_ROWS = 256
 HEAD = 512
 TAIL = 256
 GHOST_EDGES = ATOMS * HALF
-VMEM_LIMIT = 50 * 1024 * 1024
+VMEM_LIMIT = 40 * 1024 * 1024
 
 
 def dot(a, b):
@@ -220,8 +220,9 @@
 
 def own_body(
     feat_hbm, pos_hbm, neigh_hbm, counts_hbm, order_hbm, rbf_hbm, radial_hbm, mix_hbm, out_hbm,
+    feat_ref, pos_ref, neigh_ref, counts_ref, order_ref, rbf_ref, radial_ref, mix_ref, out_ref,
     acc_ref, relt_ref, pair_ref, table_ref, block_ref, oblock_ref, slope_hbm,
-    feat_ref, pos_ref, neigh_ref, counts_ref, order_ref, rbf_ref, radial_ref, mix_ref, out_ref, load_sem,
+    load_sem,
     pos8_ref, cells_ref, within_ref, rad_ref, drad_ref, hot_ref, lhs_ref, message_ref, slope_ref, sem, send_sem, recv_sem,
 ):
     loads = load_all(
@@ -329,7 +330,8 @@
     edges = ATOMS * HALF
     return pl.pallas_call(
         own_body,
-        out_shape=(
+        out_shape=tuple(jax.ShapeDtypeStruct(operand.shape, operand.dtype) for operand in operands)
+        + (
             jax.ShapeDtypeStruct((ATOMS, FEAT), F32),
             jax.ShapeDtypeStruct((8, edges), F32),
             jax.ShapeDtypeStruct((edges, ATOMS), BF16),
@@ -339,9 +341,9 @@
             jax.ShapeDtypeStruct((edges, FEAT), BF16),
         ),
         in_specs=[pl.BlockSpec(memory_space=pltpu.HBM)] * len(operands),
-        out_specs=(vmem,) * 6 + (pl.BlockSpec(memory_space=pl.ANY),),
-        scratch_shapes=like(operands)
-        + [
+        out_specs=(vmem,) * (6 + len(operands)) + (pl.BlockSpec(memory_space=pl.ANY),),
+        scratch_shapes=[
+            pltpu.SemaphoreType.DMA((len(operands),)),
             pltpu.VMEM((8, ATOMS), F32),
             pltpu.VMEM((SLOTS, ATOMS), BF16),
             pltpu.VMEM((SLOTS, ATOMS), BF16),
@@ -362,23 +364,20 @@
 
 
 def ghost_body(
-    feat_hbm, pos_hbm, neigh_hbm, counts_hbm, rbf_hbm, radial_hbm, mix_hbm, out_hbm,
-    energy_hbm, norm_hbm, acc_own_ref, relt_ref, pair_ref, table_ref, block_ref, oblock_ref, slope_hbm,
+    energy_hbm, norm_hbm, feat_ref, pos_ref, neigh_ref, counts_ref, rbf_ref, radial_ref, mix_ref, out_ref,
+    acc_own_ref, relt_ref, pair_ref, table_ref, block_ref, oblock_ref, slope_hbm,
     new_ref, energies_ref, grad_own_ref, tiles_ref,
-    feat_ref, pos_ref, neigh_ref, counts_ref, rbf_ref, radial_ref, mix_ref, out_ref,
     energy_ref, norm_ref, load_sem,
     pos8_ref, cells_ref, within_ref, rad_ref, drad_ref, lhs_ref, message_ref,
     slope_ref, gslope_ref, acc_ref, grelt_ref, gslot_ref, gatom_ref, hot_ref, last_ref, updated_ref, grad_ref, gsum_ref, sem,
 ):
     loads = load_all(
-        (pos_hbm, neigh_hbm, counts_hbm, rbf_hbm, radial_hbm, mix_hbm, out_hbm, feat_hbm, energy_hbm, norm_hbm),
-        (pos_ref, neigh_ref, counts_ref, rbf_ref, radial_ref, mix_ref, out_ref, feat_ref, energy_ref, norm_ref),
+        (energy_hbm, norm_hbm),
+        (energy_ref, norm_ref),
         load_sem,
     )
     load_slope = pltpu.make_async_copy(slope_hbm, slope_ref, sem)
     load_slope.start()
-    for at in (0, 1, 2):
-        loads[at].wait()
     pos8_ref[...] = jnp.zeros(pos8_ref.shape, F32)
     pos8_ref[0:3, :] = pos_ref[:, 0, :]
     stacked = [part.astype(F32) for part in split3(pos8_ref[...])] + [jnp.zeros((C - 24, ATOMS), F32)]
@@ -395,8 +394,6 @@
     total = jnp.sum(live_row).astype(jnp.int32)
     chunks = (total + GHOST_ROWS - 1) // GHOST_ROWS
     acc_ref[...] = acc_own_ref[...]
-    for copy in loads[3:]:
-        copy.wait()
 
     def whole(gathered):
         return gathered + (pltpu.roll(gathered, C - 8, 1) + pltpu.roll(gathered, C - 16, 1))
@@ -460,6 +457,8 @@
             lanes = slice(pair[0] * C, (pair[-1] + 1) * C)
             acc_ref[:, lanes] += dot(gather, message_ref[:, lanes])
 
+    for copy in loads:
+        copy.wait()
     for pair in PAIRS:
         lanes = slice(pair[0] * C, (pair[-1] + 1) * C)
         low = (acc_ref[:, lanes] * NORM).astype(BF16)
@@ -532,9 +531,9 @@
             jax.ShapeDtypeStruct((8, ATOMS), F32),
             jax.ShapeDtypeStruct((TILES, 8, C), F32),
         ),
-        in_specs=[pl.BlockSpec(memory_space=pltpu.HBM)] * 10 + [vmem] * 6 + [hbm],
+        in_specs=[pl.BlockSpec(memory_space=pltpu.HBM)] * 2 + [vmem] * 14 + [hbm],
         out_specs=(vmem,) * 4,
-        scratch_shapes=like(operands[:10])
+        scratch_shapes=like(operands[:2])
         + [
             pltpu.VMEM((8, ATOMS), F32),
             pltpu.VMEM((SLOTS, ATOMS), BF16),
@@ -629,12 +628,12 @@
         pltpu.with_memory_space_constraint(operand, pltpu.HBM)
         for operand in (feat, pos, neigh, live, order, rbf_weight, radial_weight, mix_weight, out_weight, energy, norm)
     )
-    acc, relt, pairs, table, blocks, oblocks, slopes = own_edges(
+    held = own_edges(
         feat, pos, neigh, live, order, rbf_weight, radial_weight, mix_weight, out_weight
     )
+    acc, relt, pairs, table, blocks, oblocks, slopes = held[9:]
     updated, energies, grad_own, tiles = ghost_edges(
-        feat, pos, neigh, live, rbf_weight, radial_weight, mix_weight, out_weight,
-        energy, norm, acc, relt, pairs, table.reshape(GHOST, WIDE), blocks, oblocks, slopes,
+        energy, norm, *held[:4], *held[5:9], acc, relt, pairs, table.reshape(GHOST, WIDE), blocks, oblocks, slopes
     )
     forces = return_forces(tiles, grad_own, order)
     return (

time: 67.4 us -> 64.2 us (0.953)
  Pallas kernels: 66 us -> 62.8 us
    pallas_call x1, Pallas kernels: 15.4 us -> 13.4 us  [ghost_edges(): pl.pallas_call(ghost_body, out_shape=(jax.ShapeDtypeStruct((ATOMS, FEAT),...]
    pallas_call x1, Pallas kernels: 40 us -> 39.2 us  [own_edges(): pl.pallas_call(own_body, out_shape=tuple((jax.ShapeDtypeStruct(operand.sh...]
where the time goes in v5:
time: 64.2 us; the launch traced here: 64.1 us
  Pallas kernels  62.8 us (98%)
  between operations  0.66 us (1%)
    pallas_call x1, Pallas kernels, own_edges(): pl.pallas_call(own_body, out_shape=tuple((jax.ShapeDtypeStruct(operand.sh...  39.2 us
    pallas_call x1, Pallas kernels, ghost_edges(): pl.pallas_call(ghost_body, out_shape=(jax.ShapeDtypeStruct((ATOMS, FEAT),...  13.4 us
    pallas_call x1, Pallas kernels, return_forces(): pl.pallas_call(return_body, out_shape=jax.ShapeDtypeStruct((3, 1, ATOMS),...  10.2 us

profile of v5, /device:TPU:1, one launch (start us, length us, event | category | flops | bytes accessed | tf_op | source)
XLA Modules:
  0.0 64.1 jit_solution(463344676346740557)
XLA Ops:
  0.6 39.2 %own_edges.1 = (bf16[64,3200]{1,0:T(8,128)(2,1)S(1)}, f32[3,1,64]{2,1,0:T(1,128)S(1)}, s32[32,64]{1,0:T(8,128)S(1)}, s32[1,64]{1,0:T(1,128)S(1)}, s32[1,64]{1,0:...) custom-call(bf16[64,3200]{1,0:T(8,128)(2,1)} %bitcast.18, ...), custom_call_target="tpu_custom_call" | custom-call | flops 8000000000 | bytes 10000000 | tf_op jit(solution)/shard_map/own_edges/pallas_call | solution.py:331
  39.9 13.4 %ghost_edges.1 = (bf16[64,3200]{1,0:T(8,128)(2,1)}, f32[1,64]{1,0:T(1,128)}, f32[8,64]{1,0:T(8,128)S(1)}, f32[14,8,128]{2,1,0:T(8,128)S(1)}) custom-call(f32[1,128]{1,0:T(1,128)} %bitcast.22, f32[4,128]{1,0:T(4,128)} %norm_hbm.1, bf16[64,3200]{1,0:T(8,128)(2,1)S(1)} %get-tuple-element.22.feat_ref, f32[3,1,64]{2,1,0:T(1,128)S(1)} %get-tuple-element.23.pos_ref, ...), custom_call_target="tpu_custom_call" | custom-call | flops 10000000000 | bytes 14000000 | tf_op jit(solution)/shard_map/ghost_edges/pallas_call | solution.py:526
  53.3 10.2 %return_forces.1 = f32[3,1,64]{2,1,0:T(1,128)S(1)} custom-call(f32[14,8,128]{2,1,0:T(8,128)S(1)} %get-tuple-element.39.tiles_ref, f32[8,64]{1,0:T(8,128)S(1)} %get-tuple-element.40.grad_own_ref, s32[1,64]{1,0:T(1,128)} %bitcast.17), custom_call_target="tpu_custom_call" | custom-call | tf_op jit(solution)/shard_map/return_forces/pallas_call | solution.py:601
  63.5 0.6 copy.16
